TPU v7x, 768 devices: a whole 4x8x12 slice. The times are simulated.
768 devices in a mesh: dp: 48 (over y_hi, z, core), tensor: 16 (over y_lo, x).
Axes of the slice: x: 4, y: 8 (y_hi: 2, y_lo: 4; y = y_hi * 4 + y_lo), z: 12, core: 2. Of those that a mesh axis runs over, the one named last changes fastest.
Arguments:
- patches: bfloat16 [12288, 3072], P('dp', 'tensor'), may hold values from -6 to 6
- keep_order: int32 [48, 256], P('dp'), may hold values from 0 to 255, each once within a row
- keep_count: int32 [48], P('dp'), may hold values from 1 to 192, 6144 in all
- ln_gain: float32 [3072], replicated, may hold values from 0.1 to 1.9
- w_in: bfloat16 [3072, 12288], P('dp', 'tensor'), may hold values from -0.109375 to 0.109375
- cotangent: bfloat16 [12288, 12288], P('dp', 'tensor'), may hold values from -6 to 6
Outputs:
- hidden: bfloat16 [12288, 12288], P('dp', 'tensor')
- grad_patches: bfloat16 [12288, 3072], P('dp', 'tensor')
- w_grad: float32 [3072, 12288], P('dp', 'tensor')
Inputs may be any that keep to these rules, and one draw needn't show every extreme that they name: Each row holds every patch number once; image i keeps the patches keep_order[i, 0] to keep_order[i, keep_count[i] - 1]. `keep_count`: the counts of all images add up to 6144; some image keeps exactly 192.
All inputs are finite; a program needn't handle non-finite values. No bound on the sum of `keep_count` on one device may be relied on, other than what follows from the above.
Results may differ from a plain program's by a relative error of at most 0.024.
Values may be sent and summed in bfloat16 or wider, within the bound.
No kernel may reach another device: no remote copies, remote signals or barrier semaphores. Data moves between devices by JAX's collectives and lax.ppermute only.
A program may use at most 64 MiB of HBM per device.

v0:
```python
import jax
import jax.numpy as jnp
from jax import lax
from jax.sharding import PartitionSpec as P

KMOST = 192


def gelu_pair(pre_act):
    normal_cdf = 0.5 * (1.0 + lax.erf(pre_act * 0.7071067811865476))
    density = jnp.exp(-0.5 * pre_act * pre_act) * 0.3989422804014327
    return (pre_act * normal_cdf, normal_cdf + pre_act * density)


def pull_rows(select, source):
    return jnp.dot(select, source, preferred_element_type=jnp.float32).astype(jnp.bfloat16)


def push_rows(select, source):
    return lax.dot_general(
        select, source, (((0,), (0,)), ((), ())), preferred_element_type=jnp.float32
    ).astype(jnp.bfloat16)


def per_device(patches, keep_order, keep_count, ln_gain, w_in, cotangent):
    own_rows = patches.shape[0]
    col_width = patches.shape[1]
    image_count = keep_order.shape[0]
    patch_count = keep_order.shape[1]
    row_ids = jnp.arange(own_rows, dtype=jnp.int32)
    image_ids = jnp.arange(image_count, dtype=jnp.int32)
    slot_ids = jnp.arange(KMOST, dtype=jnp.int32)
    slot_live = slot_ids[None, :] < keep_count[:, None]
    patch_rows = image_ids[:, None] * patch_count + keep_order[:, :KMOST]
    slot_row = jnp.where(slot_live, patch_rows, -1).reshape(-1)
    select = (slot_row[:, None] == row_ids[None, :]).astype(jnp.bfloat16)
    rows_x = pull_rows(select, patches)
    rows_cot = pull_rows(select, cotangent)
    full_x = lax.all_gather(rows_x, "tensor", axis=1, tiled=True)
    full_weight = lax.all_gather(w_in, "dp", axis=0, tiled=True)
    row_x = full_x.astype(jnp.float32)
    row_mean = jnp.mean(row_x, axis=1, keepdims=True)
    centered = row_x - row_mean
    row_var = jnp.mean(centered * centered, axis=1, keepdims=True)
    inv_std = lax.rsqrt(row_var + 1e-06)
    normal_x = centered * inv_std
    normed = (normal_x * ln_gain[None, :]).astype(jnp.bfloat16)
    pre_act = jnp.dot(normed, full_weight, preferred_element_type=jnp.float32)
    act_value, act_slope = gelu_pair(pre_act)
    hidden_rows = act_value.astype(jnp.bfloat16)
    pre_grad = (rows_cot.astype(jnp.float32) * act_slope).astype(jnp.bfloat16)
    w_grad = lax.psum_scatter(
        lax.dot_general(
            normed, pre_grad, (((0,), (0,)), ((), ())), preferred_element_type=jnp.float32
        ),
        "dp",
        scatter_dimension=0,
        tiled=True,
    )
    partial_grad = lax.dot_general(
        pre_grad, full_weight, (((1,), (1,)), ((), ())), preferred_element_type=jnp.float32
    )
    width_total = full_x.shape[1]
    col_start = lax.axis_index("tensor") * col_width
    share_grad = lax.psum_scatter(
        partial_grad.astype(jnp.bfloat16), "tensor", scatter_dimension=1, tiled=True
    ).astype(jnp.float32)
    share_x = lax.dynamic_slice_in_dim(normal_x, col_start, col_width, 1)
    share_gain = lax.dynamic_slice_in_dim(ln_gain, col_start, col_width, 0)
    scaled = share_grad * share_gain[None, :]
    first_sum, second_sum = lax.psum(
        (jnp.sum(scaled, axis=1), jnp.sum(scaled * share_x, axis=1)), "tensor"
    )
    first_mean = first_sum[:, None] / width_total
    second_mean = second_sum[:, None] / width_total
    grad_rows = (inv_std * (scaled - first_mean - share_x * second_mean)).astype(jnp.bfloat16)
    hidden = push_rows(select, hidden_rows)
    grad_patches = push_rows(select, grad_rows)
    return (hidden, grad_patches, w_grad)


def solution(mesh):
    placed = (P("dp", "tensor"), P("dp", None), P("dp"), P(), P("dp", "tensor"), P("dp", "tensor"))
    return jax.shard_map(
        per_device,
        mesh=mesh,
        in_specs=placed,
        out_specs=(P("dp", "tensor"), P("dp", "tensor"), P("dp", "tensor")),
        check_vma=False,
    )
```

profile of v0, /device:TPU:56, one launch (start us, length us, event | category | flops | bytes accessed | tf_op | source)
XLA Modules:
  0.0 598.8 jit_solution(17853396179948929176)
XLA Ops:
  7.2 0.0 copy-start
  7.2 0.0 copy-start.4
  7.2 0.0 all-gather.3.cloned.1.call-start
  7.9 0.7 compare_select_fusion
  8.6 1.1 convolution_convert_fusion.4
  9.7 0.8 copy.9
  10.5 0.0 all-gather.3.cloned.1.call-update
  10.5 0.0 all-gather.5.cloned.1.call-start
  10.5 0.7 all-gather.5.cloned.1.call-update
  11.2 0.0 reduce-scatter.7.cloned.1.call-start
  11.3 88.1 %all-gather.3.cloned.1.call-done = bf16[192,3072]{0,1:T(8,128)(2,1)} async-done(((bf16[192,192]{0,1:T(8,128)(2,1)}), bf16[192,3072]{0,1:T(8,128)(2,1)}) %all-gather.3.cloned.1.call-update) | async-done | bytes 1179664 | tf_op jit(solution)/shard_map/all_gather | solution.py:39
  99.4 0.0 copy-start.1
  99.4 1.9 convert_reduce_fusion
  101.3 1.9 fusion.2
  103.3 140.9 %all-gather.5.cloned.1.call-done = bf16[3072,768]{1,0:T(8,128)(2,1)} async-done(((bf16[64,768]{1,0:T(8,128)(2,1)}), bf16[3072,768]{1,0:T(8,128)(2,1)}) %all-gather.5.cloned.1.call-update) | async-done | bytes 4718608 | tf_op jit(solution)/shard_map/all_gather | solution.py:40
  244.2 0.0 copy-done.4
  244.2 0.0 copy-done.1
  244.2 0.0 copy-start.5
  244.2 4.1 fusion.11
  248.3 0.0 copy-start.2
  248.3 0.8 copy-done.2
  249.1 0.0 copy-done
  249.1 0.4 fusion.5
  249.5 0.0 copy-done.5
  249.5 1.7 convolution_convert_fusion
  251.2 1.6 copy.11
  252.8 0.0 reduce-scatter.7.cloned.1.call-update
  252.8 0.0 reduce-scatter.5.cloned.1.call-start
  252.8 4.9 fusion.10
  257.7 0.0 reduce-scatter.5.cloned.1.call-update
  257.8 0.0 copy-start.3
  257.8 0.1 dynamic_slice.6
  257.9 1.9 fusion
  259.8 0.0 copy-done.3
  259.8 1.2 convolution_convert_fusion.1
  261.0 75.8 %reduce-scatter.7.cloned.1.call-done = bf16[192,192]{1,0:T(8,128)(2,1)} async-done(((bf16[3072,192]{1,0:T(8,128)(2,1)}), bf16[192,192]{1,0:T(8,128)(2,1)}) %reduce-scatter.7.cloned.1.call-update) | async-done | bytes 73744
  336.8 1.1 fusion.12
  337.9 39.2 %all-reduce = (f32[192]{0:T(256)S(1)}, f32[192]{0:T(256)S(1)}) all-reduce(f32[192]{0:T(256)S(1)} %get-tuple-element.4, f32[192]{0:T(256)S(1)} %get-tuple-element.3), channel_id=1, replica_groups=mesh['dp'=48,'tensor'=16] {'tensor'}, use_global_device_ids=true, to_apply=%region_6.7 | all-reduce | flops 384 | bytes 3072 | tf_op jit(solution)/shard_map/psum | solution.py:71
  377.1 1.9 convolution_convert_fusion.3
  379.0 213.3 %reduce-scatter.5.cloned.1.call-done = f32[64,768]{1,0:T(8,128)} async-done(((f32[3072,768]{1,0:T(8,128)}), f32[64,768]{1,0:T(8,128)}) %reduce-scatter.5.cloned.1.call-update) | async-done | bytes 196624 | tf_op jit(solution)/shard_map/reduce_scatter | solution.py:52
  (3 shorter events, 0.0 us)
Async XLA Ops:
  7.2 241.9 %copy-start = (bf16[256,768]{1,0:T(8,128)(2,1)S(1)}, bf16[256,768]{1,0:T(8,128)(2,1)}, u32[]{:S(2)}) copy-start(bf16[256,768]{1,0:T(8,128)(2,1)} %param.11) | copy-start | bytes 1179652
  7.2 237.0 %copy-start.4 = (f32[3072]{0:T(1024)S(1)}, f32[3072]{0:T(1024)}, u32[]{:S(2)}) copy-start(f32[3072]{0:T(1024)} %param.9) | copy-start | bytes 36868
  7.2 92.2 %all-gather.3.cloned.1.call-start = ((), (), s32[]{:S(2)}) async-start(), calls=%async_computation.2 | async-start | bytes 1671168 | tf_op jit(solution)/shard_map/all_gather | solution.py:39
  10.5 233.7 %all-gather.5.cloned.1.call-start = ((), (), s32[]{:S(2)}) async-start(), calls=%async_computation.3 | async-start | bytes 4816896 | tf_op jit(solution)/shard_map/all_gather | solution.py:40
  11.2 325.5 %reduce-scatter.7.cloned.1.call-start = ((), (), s32[]{:S(2)}) async-start(), calls=%async_computation.5 | async-start | bytes 1671168
  99.4 144.8 %copy-start.1 = (bf16[192,3072]{0,1:T(8,128)(2,1)S(1)}, bf16[192,3072]{0,1:T(8,128)(2,1)}, u32[]{:S(2)}) copy-start(bf16[192,3072]{0,1:T(8,128)(2,1)} %all-gather.3.cloned.1.call-done) | copy-start | bytes 3538948
  244.2 5.3 copy-start.5
  248.3 0.8 copy-start.2
  252.8 339.5 %reduce-scatter.5.cloned.1.call-start = ((), (), s32[]{:S(2)}) async-start(), calls=%async_computation.4 | async-start | bytes 9633792 | tf_op jit(solution)/shard_map/reduce_scatter | solution.py:52
  257.8 2.0 copy-start.3
Sparse Core Ops, SparseCore 0:
  11.0 88.3 all-gather.2
  103.0 141.0 all-gather.4
  252.9 83.8 reduce-scatter.6
  343.7 248.4 reduce-scatter.4
where the time goes:
time: 602 us; the launch traced here: 599 us
  waiting for transfers between devices  519 us (86%)
  blocking collectives  39.2 us (7%)
  matrix products  15.3 us (3%)
  between operations  14.5 us (2%)
  other arithmetic  7.62 us (1%)
    reduce_scatter x1, waiting for transfers between devices, per_device(): lax.psum_scatter(lax.dot_general(normed, pre_grad, (((0,), (0,)), ((), ()...  213 us
    all_gather x1, waiting for transfers between devices, per_device(): full_weight = lax.all_gather(w_in, 'dp', axis=0, tiled=True)  141 us
    all_gather x1, waiting for transfers between devices, per_device(): full_x = lax.all_gather(rows_x, 'tensor', axis=1, tiled=True)  88.1 us
    unnamed x5, waiting for transfers between devices  76.5 us
    psum x1, blocking collectives, per_device(): lax.psum((jnp.sum(scaled, axis=1), jnp.sum(scaled * share_x, axis=1)), 't...  39.2 us
  transfers between devices with their start and end apart: 4, of which 4 were waited for; matrix products, arithmetic and copies ran while one was open for 3% of the time, Pallas kernels for 0%

commit v1 on v0

v1 whole, which is shorter than its diff:
```python
import jax
import jax.numpy as jnp
from jax import lax
from jax.sharding import Mesh, PartitionSpec as P

KMOST = 192
YH, Z, CORE, YL, X = 2, 12, 2, 4, 4
PIECES = 16


def gelu_pair(pre_act):
    normal_cdf = 0.5 * (1.0 + lax.erf(pre_act * 0.7071067811865476))
    density = jnp.exp(-0.5 * pre_act * pre_act) * 0.3989422804014327
    return (pre_act * normal_cdf, normal_cdf + pre_act * density)


def pieces_of(sums):
    high = lax.reduce_precision(sums, 8, 7)
    rest = sums - high
    middle = lax.reduce_precision(rest, 8, 7)
    low = rest - middle
    parts = jnp.concatenate([high, middle, low], axis=-2).astype(jnp.bfloat16)
    pad = [(0, 0)] * (sums.ndim - 2) + [(0, PIECES - 6), (0, 0)]
    return jnp.pad(parts, pad)


def sums_of(parts):
    total = jnp.sum(parts[:, :6].astype(jnp.float32), axis=0)
    return total[0:2] + total[2:4] + total[4:6]


def per_device(patches, keep_order, keep_count, ln_gain, w_in, cotangent):
    own_rows, col_width = patches.shape
    depth, ff_width = w_in.shape
    width = ln_gain.shape[0]
    half = width // CORE
    core = lax.axis_index("core")
    bf16, f32 = jnp.bfloat16, jnp.float32

    with jax.named_scope("weight_gather"):
        pair_weight = lax.all_gather(w_in, "yh", axis=0, tiled=True)
        weight = lax.all_gather(pair_weight, "z", axis=0, tiled=True)

    slot_ids = jnp.arange(KMOST, dtype=jnp.int32)
    row_ids = jnp.arange(own_rows, dtype=jnp.int32)
    slot_row = jnp.where(slot_ids < keep_count[0], keep_order[0, :KMOST], -1)
    select = (slot_row[:, None] == row_ids[None, :]).astype(bf16)

    with jax.named_scope("rows_gather"):
        own_x = lax.dot_general(
            patches, select, (((0,), (1,)), ((), ())), preferred_element_type=f32
        ).astype(bf16)
        block_x = lax.all_gather(own_x, "x", axis=0, tiled=True)
        blocks = block_x.shape[0] // (CORE * depth)
        by_core = block_x.reshape(blocks, CORE, depth, KMOST).transpose(1, 0, 2, 3)
        pair_x = lax.all_to_all(
            by_core.reshape(CORE, blocks * depth, KMOST), "core", split_axis=0, concat_axis=0, tiled=True
        )
        pair_x = jnp.concatenate([pair_x[0], pair_x[1]], axis=1)
        rows = pair_x.shape[1]
        cut = pair_x.shape[0] // 2
        parts = [lax.all_gather(pair_x[i * cut : (i + 1) * cut], "yl", axis=0, tiled=True) for i in range(2)]
        row_x = jnp.stack([p.reshape(YH, 2, blocks // 2, depth, rows) for p in parts])
        row_x = row_x.transpose(2, 0, 3, 1, 4, 5).reshape(half, rows)

    with jax.named_scope("row_moments"):
        x32 = row_x.astype(f32)
        part_mean = jnp.mean(x32, axis=0)
        part_square = jnp.sum(jnp.square(x32 - part_mean[None, :]), axis=0)
        both = lax.all_gather(jnp.stack([part_mean, part_square]), "core", axis=0)
        row_mean = 0.5 * (both[0, 0] + both[1, 0])
        apart = both[0, 0] - both[1, 0]
        row_var = (both[0, 1] + both[1, 1] + apart * apart * (0.5 * half)) / width
        inv_std = lax.rsqrt(row_var + 1e-06)
        gain = ln_gain.reshape(YH, Z, CORE, depth)
        gain = lax.dynamic_index_in_dim(gain, core, 2, keepdims=False)
        gain = gain.transpose(1, 0, 2).reshape(half)
        normal_x = (x32 - row_mean[None, :]) * inv_std[None, :]
        normed = (normal_x * gain[:, None]).astype(bf16)

    with jax.named_scope("forward"):
        rows_cot = jnp.dot(select, cotangent, preferred_element_type=f32)
        part_act = lax.dot_general(normed, weight, (((0,), (0,)), ((), ())), preferred_element_type=f32)
        part_act = lax.all_to_all(
            part_act.reshape(CORE, KMOST, ff_width), "core", split_axis=0, concat_axis=0, tiled=True
        )
        act_value, act_slope = gelu_pair(part_act[0] + part_act[1])
        pre_grad = (rows_cot * act_slope).astype(bf16)
        pair_grad = lax.all_gather(pre_grad, "core", axis=0, tiled=True)

    with jax.named_scope("weight_grad"):
        part_w = jnp.dot(normed, pair_grad, preferred_element_type=f32).astype(bf16)
        part_w, pair_grad = lax.optimization_barrier((part_w, pair_grad))
        pair_w = lax.psum_scatter(part_w, "z", scatter_dimension=0, tiled=True)

    with jax.named_scope("rows_grad"):
        part_x = lax.dot_general(weight, pair_grad, (((1,), (1,)), ((), ())), preferred_element_type=f32)
        part_x = part_x.astype(bf16)
        scaled = part_x.astype(f32) * gain[:, None]
        sums = jnp.stack([jnp.sum(scaled, axis=0), jnp.sum(scaled * normal_x, axis=0)])
        by_yl = part_x.reshape(2, blocks, YH, depth, rows).transpose(2, 0, 1, 3, 4)
        by_yl = by_yl.reshape(YL, blocks * depth, rows)
        extra = jnp.broadcast_to(pieces_of(sums)[None], (YL, PIECES, rows))
        got = lax.all_to_all(
            jnp.concatenate([by_yl, extra], axis=1), "yl", split_axis=0, concat_axis=0, tiled=True
        )
        sums = sums_of(got[:, -PIECES:])
        grad = jnp.sum(got[:, :-PIECES].astype(f32), axis=0).astype(bf16)
        grad = jnp.concatenate([grad, pieces_of(sums)], axis=0)
        by_core = jnp.stack([grad[:, :KMOST], grad[:, KMOST:]])
        got = lax.all_to_all(by_core, "core", split_axis=0, concat_axis=0, tiled=True)
        sums = sums_of(got[:, -PIECES:])
        grad = got[:, :-PIECES].reshape(CORE, blocks, depth, KMOST).transpose(1, 0, 2, 3)
        by_x = grad.reshape(X, col_width, KMOST)
        extra = jnp.broadcast_to(pieces_of(sums)[None], (X, PIECES, KMOST))
        got = lax.all_to_all(
            jnp.concatenate([by_x, extra], axis=1), "x", split_axis=0, concat_axis=0, tiled=True
        )
        sums = sums_of(got[:, -PIECES:])
        share_grad = jnp.sum(got[:, :-PIECES].astype(f32), axis=0)

    with jax.named_scope("rows_out"):
        col_start = (lax.axis_index("yl") * X + lax.axis_index("x")) * col_width
        share_gain = lax.dynamic_slice_in_dim(ln_gain, col_start, col_width, 0)
        own_mean = lax.dynamic_slice_in_dim(row_mean, core * KMOST, KMOST, 0)
        own_inv = lax.dynamic_slice_in_dim(inv_std, core * KMOST, KMOST, 0)
        share_x = (own_x.astype(f32) - own_mean[None, :]) * own_inv[None, :]
        scaled = share_grad * share_gain[:, None]
        means = sums / width
        grad_rows = own_inv[None, :] * (scaled - means[0:1] - share_x * means[1:2])
        grad_patches = lax.dot_general(
            select, grad_rows.astype(bf16), (((0,), (1,)), ((), ())), preferred_element_type=f32
        ).astype(bf16)
        hidden = lax.dot_general(
            select, act_value.astype(bf16), (((0,), (0,)), ((), ())), preferred_element_type=f32
        ).astype(bf16)

    with jax.named_scope("weight_out"):
        yh = lax.axis_index("yh")
        kept_w = lax.dynamic_slice_in_dim(pair_w, yh * depth, depth, 0)
        sent_w = lax.dynamic_slice_in_dim(pair_w, (1 - yh) * depth, depth, 0)
        met_w = lax.ppermute(sent_w, "yh", [(0, 1), (1, 0)])
        w_grad = kept_w.astype(f32) + met_w.astype(f32)
    return (hidden, grad_patches, w_grad)


def solution(mesh):
    fine = Mesh(mesh.devices.reshape(YH, Z, CORE, YL, X), ("yh", "z", "core", "yl", "x"))
    dp, tensor = ("yh", "z", "core"), ("yl", "x")
    both = P(dp, tensor)
    return jax.shard_map(
        per_device,
        mesh=fine,
        in_specs=(both, P(dp, None), P(dp), P(), both, both),
        out_specs=(both, both, both),
        check_vma=False,
    )
```

time: 602 us -> 200 us (0.33)
  waiting for transfers between devices: 519 us -> 59.8 us
  blocking collectives: 39.2 us -> 72.7 us
  starting transfers between devices: 0.16 us -> 19.6 us
  local copies, waits for them, and re-layouts: 3.23 us -> 11.1 us
    all_gather x2 -> x1, waiting for transfers between devices: 229 us -> 3.52 us  [per_device(): weight = lax.all_gather(pair_weight, 'z', axis=0, tiled=True)]
    reduce_scatter x1, waiting for transfers between devices: 213 us -> 14.9 us  [per_device(): pair_w = lax.psum_scatter(part_w, 'z', scatter_dimension=0, tiled=True)]
    unnamed x5 -> x2, waiting for transfers between devices: 76.5 us -> 0.74 us
    all_gather x0 -> x6, blocking collectives: none -> 63.9 us  [the longest x2 35.8 us: per_device(): lax.all_gather(pair_x[i * cut:(i + 1) * cut], 'yl', axis=0, tiled=True)]
    psum x1 -> x0, blocking collectives: 39.2 us -> none  [per_device(): lax.psum((jnp.sum(scaled, axis=1), jnp.sum(scaled * share_x, axis=1)), 't...]
    all_to_all x0 -> x3, waiting for transfers between devices: none -> 35.4 us  [the longest x1 26.9 us: per_device(): lax.all_to_all(jnp.concatenate([by_yl, extra], axis=1), 'yl', split_axis=...]
    all_to_all x0 -> x3, starting transfers between devices: none -> 14.4 us  [the longest x1 6.7 us: per_device(): lax.all_to_all(jnp.concatenate([by_yl, extra], axis=1), 'yl', split_axis=...]
    all_to_all x0 -> x2, blocking collectives: none -> 8.86 us  [the longest x1 4.81 us: per_device(): lax.all_to_all(part_act.reshape(CORE, KMOST, ff_width), 'core', split_axi...]
  transfers between devices with their start and end apart: 4 -> 6, of which waited for: 4 -> 6; matrix products, arithmetic and copies ran while one was open for 3% -> 7% of each run, Pallas kernels for 0% -> 0%
where the time goes in v1:
time: 200 us; the launch traced here: 199 us
  blocking collectives  72.7 us (36%)
  waiting for transfers between devices  59.8 us (30%)
  starting transfers between devices  19.6 us (10%)
  between operations  15 us (8%)
  matrix products  13.6 us (7%)
  local copies, waits for them, and re-layouts  11.1 us (6%)
  other arithmetic  6.66 us (3%)
    all_gather x2, blocking collectives, per_device(): lax.all_gather(pair_x[i * cut:(i + 1) * cut], 'yl', axis=0, tiled=True)  35.8 us
    all_to_all x1, waiting for transfers between devices, per_device(): lax.all_to_all(jnp.concatenate([by_yl, extra], axis=1), 'yl', split_axis=...  26.9 us
    reduce_scatter x1, waiting for transfers between devices, per_device(): pair_w = lax.psum_scatter(part_w, 'z', scatter_dimension=0, tiled=True)  14.9 us
    all_gather x1, blocking collectives, per_device(): block_x = lax.all_gather(own_x, 'x', axis=0, tiled=True)  13 us
    all_gather x1, blocking collectives, per_device(): pair_weight = lax.all_gather(w_in, 'yh', axis=0, tiled=True)  11.1 us
    all_to_all x1, waiting for transfers between devices, per_device(): lax.all_to_all(jnp.concatenate([by_x, extra], axis=1), 'x', split_axis=0,...  7.17 us
    all_to_all x1, starting transfers between devices, per_device(): lax.all_to_all(jnp.concatenate([by_yl, extra], axis=1), 'yl', split_axis=...  6.7 us
    ppermute x1, waiting for transfers between devices, per_device(): met_w = lax.ppermute(sent_w, 'yh', [(0, 1), (1, 0)])  5.27 us
  transfers between devices with their start and end apart: 6, of which 6 were waited for; matrix products, arithmetic and copies ran while one was open for 7% of the time, Pallas kernels for 0%

profile of v1, /device:TPU:56, one launch (start us, length us, event | category | flops | bytes accessed | tf_op | source)
XLA Modules:
  0.0 198.5 jit_solution(4489095036488498978)
XLA Ops:
  7.2 11.1 %all_gather.29 = bf16[128,768]{1,0:T(8,128)(2,1)} all-gather(bf16[64,768]{1,0:T(8,128)(2,1)} %param.10), channel_id=1, replica_groups=mesh['yh'=2,'z'=12,'core'=2,'yl'=4,'x'=4] {'yh'}, dimensions={0}, use_global_device_ids=true | all-gather | bytes 294912 | tf_op jit(solution)/shard_map/weight_gather/all_gather | solution.py:41
  19.0 0.7 compare_select_fusion
  19.6 1.1 fusion.7
  20.9 13.0 %all_gather.24 = bf16[768,192]{1,0:T(8,128)(2,1)S(1)} all-gather(bf16[192,192]{1,0:T(8,128)(2,1)S(1)} %copy.91), channel_id=1, replica_groups=mesh['yh'=2,'z'=12,'core'=2,'yl'=4,'x'=4] {'x'}, dimensions={0}, use_global_device_ids=true | all-gather | bytes 368640 | tf_op jit(solution)/shard_map/rows_gather/all_gather | solution.py:53
  33.9 0.9 copy.93
  34.8 3.4 %all-to-all-start = ((bf16[2,384,192]{1,2,0:T(8,128)(2,1)}), bf16[2,384,192]{1,2,0:T(8,128)(2,1)S(1)}, u32[]{:S(2)}, u32[]{:S(2)}) async-start(bf16[2,384,192]{1,2,0:T(8,128)(2,1)} %copy.93), calls=%async_computation | async-start | bytes 589824 | tf_op jit(solution)/shard_map/rows_gather/all_to_all | solution.py:56
  38.5 1.3 all-to-all-done
  39.9 0.1 copy.111
  40.0 0.1 copy.112
  40.3 19.1 %all_gather.25 = bf16[768,384]{1,0:T(8,128)(2,1)S(1)} all-gather(bf16[192,384]{1,0:T(8,128)(2,1)S(1)} %get-tuple-element.19), channel_id=1, replica_groups=mesh['yh'=2,'z'=12,'core'=2,'yl'=4,'x'=4] {'yl'}, dimensions={0}, use_global_device_ids=true | all-gather | bytes 737280 | tf_op jit(solution)/shard_map/rows_gather/all_gather | solution.py:62
  59.3 16.7 %all_gather.26 = bf16[768,384]{1,0:T(8,128)(2,1)S(1)} all-gather(bf16[192,384]{1,0:T(8,128)(2,1)S(1)} %get-tuple-element.20), channel_id=1, replica_groups=mesh['yh'=2,'z'=12,'core'=2,'yl'=4,'x'=4] {'yl'}, dimensions={0}, use_global_device_ids=true | all-gather | bytes 737280 | tf_op jit(solution)/shard_map/rows_gather/all_gather | solution.py:62
  76.1 0.2 convert_reduce_fusion
  76.3 0.4 fusion.2
  76.8 0.2 convert_bitcast_fusion
  76.9 1.6 copy.96
  78.6 2.0 %copy.97 = f32[1536,384]{0,1:T(8,128)S(1)} copy(f32[1536,384]{1,0:T(8,128)} %bitcast.73) | data formatting | bytes 4718592 | tf_op jit(solution)/shard_map/row_moments/convert_element_type | solution.py:67
  80.6 1.8 all-gather.1
  82.4 1.4 multiply_convert_fusion
  83.8 3.5 %all-gather.4.cloned.1.call-done = bf16[1536,768]{1,0:T(8,128)(2,1)} async-done(((bf16[128,768]{1,0:T(8,128)(2,1)}), bf16[1536,768]{1,0:T(8,128)(2,1)}) %all-gather.4.cloned.1.call-update) | async-done | bytes 2359312 | tf_op jit(solution)/shard_map/weight_gather/all_gather | solution.py:42
  87.4 3.1 %fusion.3 = f32[2,192,768]{2,1,0:T(8,128)S(1)} fusion(bf16[2,192,1536]{2,1,0:T(8,128)(2,1)} %bitcast.80, bf16[1536,768]{1,0:T(8,128)(2,1)} %all-gather.4.cloned.1.call-done), kind=kOutput, calls=%fused_computation.8 | convolution fusion | flops 905969664 | bytes 4718592 | tf_op jit(solution)/shard_map/forward/dot_general | solution.py:83
  90.5 4.8 %all_to_all.25 = f32[2,192,768]{2,1,0:T(8,128)S(1)} all-to-all(f32[2,192,768]{2,1,0:T(8,128)S(1)} %fusion.3), channel_id=1, replica_groups=mesh['yh'=2,'z'=12,'core'=2,'yl'=4,'x'=4] {'core'}, dimensions={0} | all-to-all | bytes 2359296 | tf_op jit(solution)/shard_map/forward/all_to_all | solution.py:84
  95.3 1.1 copy-done.1
  96.3 0.4 fusion.6
  96.7 2.2 %all_gather.31 = bf16[384,768]{1,0:T(8,128)(2,1)S(1)} all-gather(bf16[192,768]{1,0:T(8,128)(2,1)S(1)} %fusion.6), channel_id=1, replica_groups=mesh['yh'=2,'z'=12,'core'=2,'yl'=4,'x'=4] {'core'}, dimensions={0}, use_global_device_ids=true | all-gather | bytes 884736 | tf_op jit(solution)/shard_map/forward/all_gather | solution.py:89
  99.0 2.8 %convolution_convert_fusion = bf16[1536,768]{1,0:T(8,128)(2,1)} fusion(bf16[1536,384]{0,1:T(8,128)(2,1)S(1)} %copy-done.3, bf16[384,768]{1,0:T(8,128)(2,1)S(1)} %all_gather.31), kind=kOutput, calls=%fused_computation.3 | convolution fusion | flops 907149312 | bytes 4128768 | tf_op jit(solution)/shard_map/weight_grad/dot_general | solution.py:92
  101.8 3.9 %fusion.5 = (f32[384]{0:T(512)S(1)}, f32[384]{0:T(512)S(1)}, bf16[1536,384]{0,1:T(8,128)(2,1)}) fusion(f32[1536]{0:T(1024)S(1)} %mul.151, f32[384]{0:T(512)S(1)} %get-tuple-element.28, f32[1536,384]{0,1:T(8,128)S(1)} %copy.97, f32[384]{0:T(512)S(1)} %get-tuple-element.15, bf16[384,768]{1,0:T(8,128)(2,1)S(1)} %all_gather.31, ...), kind=kOutput, calls=%fused_computation.12 | convolution fusion | flops 910687488 | bytes 6500352 | tf_op jit(solution)/shard_map/rows_grad/dot_general | solution.py:97
  105.7 1.7 copy.99
  107.4 0.1 copy.100
  107.6 1.2 pad_maximum_fusion
  108.8 6.7 %all-to-all-start.2 = ((bf16[4,400,384]{2,1,0:T(8,128)(2,1)}), bf16[4,400,384]{2,1,0:T(8,128)(2,1)S(1)}, u32[]{:S(2)}, u32[]{:S(2)}) async-start(bf16[4,400,384]{2,1,0:T(8,128)(2,1)} %pad_maximum_fusion), calls=%async_computation.2 | async-start | bytes 2457600 | tf_op jit(solution)/shard_map/rows_grad/all_to_all | solution.py:104
  115.5 0.7 reduce-scatter.2.cloned.1.call-update
  116.4 26.9 %all-to-all-done.2 = bf16[4,400,384]{2,1,0:T(8,128)(2,1)S(1)} async-done(((bf16[4,400,384]{2,1,0:T(8,128)(2,1)}), bf16[4,400,384]{2,1,0:T(8,128)(2,1)S(1)}, u32[]{:S(2)}, u32[]{:S(2)}) %all-to-all-start.2) | async-done | bytes 1228832 | tf_op jit(solution)/shard_map/rows_grad/all_to_all | solution.py:104
  143.3 0.2 slice_reduce_fusion
  143.5 0.1 fusion.14
  143.7 0.2 copy.101
  143.9 4.0 %all_to_all.26 = bf16[2,400,192]{1,2,0:T(8,128)(2,1)S(1)} all-to-all(bf16[2,400,192]{1,2,0:T(8,128)(2,1)S(1)} %copy.101), channel_id=1, replica_groups=mesh['yh'=2,'z'=12,'core'=2,'yl'=4,'x'=4] {'core'}, dimensions={0} | all-to-all | bytes 614400 | tf_op jit(solution)/shard_map/rows_grad/all_to_all | solution.py:111
  148.0 0.2 copy.113
  148.8 1.0 copy.107
  149.7 4.2 %all-to-all-start.4 = ((bf16[4,208,192]{1,2,0:T(8,128)(2,1)}), bf16[4,208,192]{1,2,0:T(8,128)(2,1)S(1)}, u32[]{:S(2)}, u32[]{:S(2)}) async-start(bf16[4,208,192]{1,2,0:T(8,128)(2,1)} %copy.107), calls=%async_computation.4 | async-start | bytes 786432 | tf_op jit(solution)/shard_map/rows_grad/all_to_all | solution.py:116
  154.0 1.2 convolution_convert_fusion.2
  155.2 7.2 %all-to-all-done.4 = bf16[4,208,192]{1,2,0:T(8,128)(2,1)S(1)} async-done(((bf16[4,208,192]{1,2,0:T(8,128)(2,1)}), bf16[4,208,192]{1,2,0:T(8,128)(2,1)S(1)}, u32[]{:S(2)}, u32[]{:S(2)}) %all-to-all-start.4) | async-done | bytes 319520 | tf_op jit(solution)/shard_map/rows_grad/all_to_all | solution.py:116
  162.6 0.2 slice_reduce_fusion.2
  162.9 14.9 %reduce-scatter.2.cloned.1.call-done = bf16[128,768]{1,0:T(8,128)(2,1)} async-done(((bf16[1536,768]{1,0:T(8,128)(2,1)}), bf16[128,768]{1,0:T(8,128)(2,1)}) %reduce-scatter.2.cloned.1.call-update) | async-done | bytes 196624 | tf_op jit(solution)/shard_map/weight_grad/reduce_scatter | solution.py:94
  177.8 0.9 constant_dynamic-slice_fusion.1
  178.7 5.1 %collective-permute-start = (bf16[64,768]{1,0:T(8,128)(2,1)S(1)}, bf16[64,768]{1,0:T(8,128)(2,1)S(1)}, u32[]{:S(2)}, u32[]{:S(2)}) collective-permute-start(bf16[64,768]{1,0:T(8,128)(2,1)S(1)} %constant_dynamic-slice_fusion.1), channel_id=1, source_target_pairs={{0,384},{384,0},{1,385},{385,1},{2,386},{386,2},{3,387},{387,3},{4... | collective-permute-start | bytes 294920 | tf_op jit(solution)/shard_map/weight_out/ppermute | solution.py:142
  183.8 1.0 convolution_convert_fusion.3
  184.8 5.3 %collective-permute-done = bf16[64,768]{1,0:T(8,128)(2,1)S(1)} collective-permute-done((bf16[64,768]{1,0:T(8,128)(2,1)S(1)}, bf16[64,768]{1,0:T(8,128)(2,1)S(1)}, u32[]{:S(2)}, u32[]{:S(2)}) %collective-permute-start) | collective-permute-done | bytes 98336 | tf_op jit(solution)/shard_map/weight_out/ppermute | solution.py:142
  190.1 1.6 convert_add_fusion
  (52 shorter events, 1.8 us)
Async XLA Ops:
  7.2 89.2 %copy-start = (bf16[256,768]{1,0:T(8,128)(2,1)S(1)}, bf16[256,768]{1,0:T(8,128)(2,1)}, u32[]{:S(2)}) copy-start(bf16[256,768]{1,0:T(8,128)(2,1)} %param.11) | copy-start | bytes 1179652
  7.2 31.1 %copy-start.4 = (f32[3072]{0:T(1024)S(1)}, f32[3072]{0:T(1024)}, u32[]{:S(2)}) copy-start(f32[3072]{0:T(1024)} %param.9) | copy-start | bytes 36868
  7.2 80.2 %all-gather.4.cloned.1.call-start = ((), (), s32[]{:S(2)}) async-start(), calls=%async_computation.6 | async-start | bytes 2555904 | tf_op jit(solution)/shard_map/weight_gather/all_gather | solution.py:42
  34.8 5.0 %all-to-all-start = ((bf16[2,384,192]{1,2,0:T(8,128)(2,1)}), bf16[2,384,192]{1,2,0:T(8,128)(2,1)S(1)}, u32[]{:S(2)}, u32[]{:S(2)}) async-start(bf16[2,384,192]{1,2,0:T(8,128)(2,1)} %copy.93), calls=%async_computation | async-start | bytes 589824 | tf_op jit(solution)/shard_map/rows_gather/all_to_all | solution.py:56
  90.5 8.5 %copy-start.3 = (bf16[1536,384]{0,1:T(8,128)(2,1)S(1)}, bf16[1536,384]{0,1:T(8,128)(2,1)}, u32[]{:S(2)}) copy-start(bf16[1536,384]{0,1:T(8,128)(2,1)} %multiply_convert_fusion) | copy-start | bytes 3538948
  95.3 1.1 copy-start.1
  108.8 34.5 %all-to-all-start.2 = ((bf16[4,400,384]{2,1,0:T(8,128)(2,1)}), bf16[4,400,384]{2,1,0:T(8,128)(2,1)S(1)}, u32[]{:S(2)}, u32[]{:S(2)}) async-start(bf16[4,400,384]{2,1,0:T(8,128)(2,1)} %pad_maximum_fusion), calls=%async_computation.2 | async-start | bytes 2457600 | tf_op jit(solution)/shard_map/rows_grad/all_to_all | solution.py:104
  115.5 62.3 %reduce-scatter.2.cloned.1.call-start = ((), (), s32[]{:S(2)}) async-start(), calls=%async_computation.7 | async-start | bytes 2555904 | tf_op jit(solution)/shard_map/weight_grad/reduce_scatter | solution.py:94
  148.2 5.8 %copy-start.2 = (f32[2,192,768]{2,1,0:T(8,128)S(1)}, f32[2,192,768]{2,1,0:T(8,128)}, u32[]{:S(2)}) copy-start(f32[2,192,768]{2,1,0:T(8,128)} %copy-done.1) | copy-start | bytes 3538948
  149.7 12.6 %all-to-all-start.4 = ((bf16[4,208,192]{1,2,0:T(8,128)(2,1)}), bf16[4,208,192]{1,2,0:T(8,128)(2,1)S(1)}, u32[]{:S(2)}, u32[]{:S(2)}) async-start(bf16[4,208,192]{1,2,0:T(8,128)(2,1)} %copy.107), calls=%async_computation.4 | async-start | bytes 786432 | tf_op jit(solution)/shard_map/rows_grad/all_to_all | solution.py:116
  178.7 11.5 %collective-permute-start = (bf16[64,768]{1,0:T(8,128)(2,1)S(1)}, bf16[64,768]{1,0:T(8,128)(2,1)S(1)}, u32[]{:S(2)}, u32[]{:S(2)}) collective-permute-start(bf16[64,768]{1,0:T(8,128)(2,1)S(1)} %constant_dynamic-slice_fusion.1), channel_id=1, source_target_pairs={{0,384},{384,0},{1,385},{385,1},{2,386},{386,2},{3,387},{387,3},{4... | collective-permute-start | bytes 294920 | tf_op jit(solution)/shard_map/weight_out/ppermute | solution.py:142
Sparse Core Ops, SparseCore 0:
  18.4 68.8 all-gather.3
  119.5 58.2 reduce-scatter.1

commit v2 on v1

--- a/solution.py
+++ b/solution.py
@@ -93,7 +93,7 @@
         part_w, pair_grad = lax.optimization_barrier((part_w, pair_grad))
         pair_w = lax.psum_scatter(part_w, "z", scatter_dimension=0, tiled=True)
 
-    with jax.named_scope("rows_grad"):
+    def rows_grad(pair_grad):
         part_x = lax.dot_general(weight, pair_grad, (((1,), (1,)), ((), ())), preferred_element_type=f32)
         part_x = part_x.astype(bf16)
         scaled = part_x.astype(f32) * gain[:, None]
@@ -118,6 +118,17 @@
         )
         sums = sums_of(got[:, -PIECES:])
         share_grad = jnp.sum(got[:, :-PIECES].astype(f32), axis=0)
+
+
+        return sums, share_grad
+
+    with jax.named_scope("rows_grad"):
+        sums, share_grad = lax.cond(
+            keep_count[0] > 0,
+            rows_grad,
+            lambda g: (jnp.zeros((2, KMOST), f32), jnp.zeros((col_width, KMOST), f32)),
+            pair_grad,
+        )
 
     with jax.named_scope("rows_out"):
         col_start = (lax.axis_index("yl") * X + lax.axis_index("x")) * col_width

time: 200 us -> 187 us (0.935)
  waiting for transfers between devices: 59.8 us -> 10.2 us
  blocking collectives: 72.7 us -> 118 us
  starting transfers between devices: 19.6 us -> 8.61 us
    all_to_all x1 -> x3, blocking collectives: 4.05 us -> 49.9 us  [the longest x1 33.4 us: rows_grad(): lax.all_to_all(jnp.concatenate([by_yl, extra], axis=1), 'yl', split_axis=...]
    all_to_all x2 -> x0, waiting for transfers between devices: 34.1 us -> none  [the longest x1 26.9 us: per_device(): lax.all_to_all(jnp.concatenate([by_yl, extra], axis=1), 'yl', split_axis=...]
    reduce_scatter x1, waiting for transfers between devices: 14.9 us -> 2.95 us  [per_device(): pair_w = lax.psum_scatter(part_w, 'z', scatter_dimension=0, tiled=True)]
    all_to_all x2 -> x0, starting transfers between devices: 10.9 us -> none  [the longest x1 6.7 us: per_device(): lax.all_to_all(jnp.concatenate([by_yl, extra], axis=1), 'yl', split_axis=...]
    dot_general x0 -> x1, other arithmetic: none -> 3.07 us  [per_device(): lax.dot_general(normed, weight, (((0,), (0,)), ((), ())), preferred_eleme...]
    dot_general x0 -> x1, local copies, waits for them, and re-layouts: none -> 2.39 us  [per_device(): lax.dot_general(normed, weight, (((0,), (0,)), ((), ())), preferred_eleme...]
    all_gather x1, waiting for transfers between devices: 3.52 us -> 1.29 us  [per_device(): weight = lax.all_gather(pair_weight, 'z', axis=0, tiled=True)]
    convert_element_type x2 -> x1, local copies, waits for them, and re-layouts: 3.68 us -> 1.62 us  [per_device(): x32 = row_x.astype(f32)]
  transfers between devices with their start and end apart: 6 -> 4, of which waited for: 6 -> 4; matrix products, arithmetic and copies ran while one was open for 7% -> 13% of each run, Pallas kernels for 0% -> 0%
where the time goes in v2:
time: 187 us; the launch traced here: 185 us
  blocking collectives  118 us (63%)
  matrix products  15 us (8%)
  between operations  14.8 us (8%)
  local copies, waits for them, and re-layouts  10.2 us (5%)
  waiting for transfers between devices  10.2 us (5%)
  starting transfers between devices  8.61 us (5%)
  other arithmetic  8 us (4%)
    all_gather x2, blocking collectives, per_device(): lax.all_gather(pair_x[i * cut:(i + 1) * cut], 'yl', axis=0, tiled=True)  35.8 us
    all_to_all x1, blocking collectives, rows_grad(): lax.all_to_all(jnp.concatenate([by_yl, extra], axis=1), 'yl', split_axis=...  33.4 us
    all_gather x1, blocking collectives, per_device(): block_x = lax.all_gather(own_x, 'x', axis=0, tiled=True)  13 us
    all_to_all x1, blocking collectives, rows_grad(): lax.all_to_all(jnp.concatenate([by_x, extra], axis=1), 'x', split_axis=0,...  12.4 us
    all_gather x1, blocking collectives, per_device(): pair_weight = lax.all_gather(w_in, 'yh', axis=0, tiled=True)  11.1 us
    ppermute x1, starting transfers between devices, per_device(): met_w = lax.ppermute(sent_w, 'yh', [(0, 1), (1, 0)])  5.08 us
    all_to_all x1, blocking collectives, per_device(): lax.all_to_all(part_act.reshape(CORE, KMOST, ff_width), 'core', split_axi...  4.68 us
    ppermute x1, waiting for transfers between devices, per_device(): met_w = lax.ppermute(sent_w, 'yh', [(0, 1), (1, 0)])  4.41 us
  transfers between devices with their start and end apart: 4, of which 4 were waited for; matrix products, arithmetic and copies ran while one was open for 13% of the time, Pallas kernels for 0%

profile of v2, /device:TPU:56, one launch (start us, length us, event | category | flops | bytes accessed | tf_op | source)
XLA Modules:
  0.0 185.4 jit_solution(2266320607036216172)
XLA Ops:
  7.2 11.1 %all_gather.29 = bf16[128,768]{1,0:T(8,128)(2,1)} all-gather(bf16[64,768]{1,0:T(8,128)(2,1)} %param.12), channel_id=1, replica_groups=mesh['yh'=2,'z'=12,'core'=2,'yl'=4,'x'=4] {'yh'}, dimensions={0}, use_global_device_ids=true | all-gather | bytes 294912 | tf_op jit(solution)/shard_map/weight_gather/all_gather | solution.py:41
  18.9 0.7 compare_select_fusion
  19.6 1.1 fusion.28
  20.9 13.0 %all_gather.24 = bf16[768,192]{1,0:T(8,128)(2,1)S(1)} all-gather(bf16[192,192]{1,0:T(8,128)(2,1)S(1)} %copy.89), channel_id=1, replica_groups=mesh['yh'=2,'z'=12,'core'=2,'yl'=4,'x'=4] {'x'}, dimensions={0}, use_global_device_ids=true | all-gather | bytes 368640 | tf_op jit(solution)/shard_map/rows_gather/all_gather | solution.py:53
  33.9 0.9 copy.91
  34.8 3.4 %all-to-all-start.3 = ((bf16[2,384,192]{1,2,0:T(8,128)(2,1)}), bf16[2,384,192]{1,2,0:T(8,128)(2,1)S(1)}, u32[]{:S(2)}, u32[]{:S(2)}) async-start(bf16[2,384,192]{1,2,0:T(8,128)(2,1)} %copy.91), calls=%async_computation.3 | async-start | bytes 589824 | tf_op jit(solution)/shard_map/rows_gather/all_to_all | solution.py:56
  38.3 1.5 all-to-all-done.3
  39.9 0.1 copy.101
  40.0 0.1 copy.102
  40.3 19.1 %all_gather.25 = bf16[768,384]{1,0:T(8,128)(2,1)S(1)} all-gather(bf16[192,384]{1,0:T(8,128)(2,1)S(1)} %get-tuple-element.54), channel_id=1, replica_groups=mesh['yh'=2,'z'=12,'core'=2,'yl'=4,'x'=4] {'yl'}, dimensions={0}, use_global_device_ids=true | all-gather | bytes 737280 | tf_op jit(solution)/shard_map/rows_gather/all_gather | solution.py:62
  59.3 16.7 %all_gather.26 = bf16[768,384]{1,0:T(8,128)(2,1)S(1)} all-gather(bf16[192,384]{1,0:T(8,128)(2,1)S(1)} %get-tuple-element.55), channel_id=1, replica_groups=mesh['yh'=2,'z'=12,'core'=2,'yl'=4,'x'=4] {'yl'}, dimensions={0}, use_global_device_ids=true | all-gather | bytes 737280 | tf_op jit(solution)/shard_map/rows_gather/all_gather | solution.py:62
  76.1 0.2 convert_reduce_fusion.4
  76.3 0.4 fusion.23
  76.7 0.2 convert_bitcast_fusion
  76.9 1.6 copy.94
  78.8 1.8 all-gather.1
  80.6 3.1 %fusion.45 = (bf16[384,1536]{0,1:T(8,128)(2,1)}, f32[1536,384]{1,0:T(8,128)S(1)}) fusion(f32[1536]{0:T(1024)S(1)} %mul.155, f32[384]{0:T(512)S(1)} %get-tuple-element.58, f32[384]{0:T(512)S(1)} %get-tuple-element.37, f32[2,2,3,2,64,384]{5,4,3,2,1,0:T(8,128)} %copy.94), kind=kLoop, calls=%fused_computation.114 | loop fusion | flops 2359296 | bytes 5907456 | tf_op jit(solution)/shard_map/forward/dot_general | solution.py:83
  83.7 2.4 %copy.96 = bf16[384,1536]{1,0:T(8,128)(2,1)} copy(bf16[384,1536]{0,1:T(8,128)(2,1)} %get-tuple-element.35) | data formatting | bytes 2359296 | tf_op jit(solution)/shard_map/forward/dot_general | solution.py:83
  86.0 1.3 all-gather.4.cloned.1.call-done
  87.3 3.1 %fusion.24 = f32[2,192,768]{2,1,0:T(8,128)S(1)} fusion(bf16[2,192,1536]{2,1,0:T(8,128)(2,1)} %bitcast.81, bf16[1536,768]{1,0:T(8,128)(2,1)} %all-gather.4.cloned.1.call-done), kind=kOutput, calls=%fused_computation.62 | convolution fusion | flops 905969664 | bytes 4718592 | tf_op jit(solution)/shard_map/forward/dot_general | solution.py:83
  90.4 4.7 %all_to_all.25 = f32[2,192,768]{2,1,0:T(8,128)S(1)} all-to-all(f32[2,192,768]{2,1,0:T(8,128)S(1)} %fusion.24), channel_id=1, replica_groups=mesh['yh'=2,'z'=12,'core'=2,'yl'=4,'x'=4] {'core'}, dimensions={0} | all-to-all | bytes 2359296 | tf_op jit(solution)/shard_map/forward/all_to_all | solution.py:84
  95.1 1.1 copy-done.1
  96.2 0.4 fusion.27
  96.6 2.2 %all_gather.31 = bf16[384,768]{1,0:T(8,128)(2,1)S(1)} all-gather(bf16[192,768]{1,0:T(8,128)(2,1)S(1)} %fusion.27), channel_id=1, replica_groups=mesh['yh'=2,'z'=12,'core'=2,'yl'=4,'x'=4] {'core'}, dimensions={0}, use_global_device_ids=true | all-gather | bytes 884736 | tf_op jit(solution)/shard_map/forward/all_gather | solution.py:89
  98.8 2.8 %convolution_convert_fusion.1 = bf16[1536,768]{1,0:T(8,128)(2,1)} fusion(bf16[384,768]{1,0:T(8,128)(2,1)S(1)} %all_gather.31, f32[1536,384]{1,0:T(8,128)S(1)} %get-tuple-element.36, f32[1536]{0:T(1024)S(1)} %mul.155), kind=kOutput, calls=%fused_computation.59 | convolution fusion | flops 908328960 | bytes 5314560 | tf_op jit(solution)/shard_map/weight_grad/dot_general | solution.py:92
  101.7 0.7 dynamic_slice.23
  102.4 0.6 constant_dynamic-slice_fusion
  103.0 56.1 %conditional.1 = (f32[2,192]{0,1:T(8,128)S(1)}, f32[192,192]{0,1:T(8,128)}) conditional(s32[]{:T(128)} %convert_element_type.91, () %tuple.17, (bf16[1536,768]{1,0:T(8,128)(2,1)}, bf16[384,768]{1,0:T(8,128)(2,1)S(1)}, f32[12,2,64]{2,1,0:T(2,128)S(1)}, f32[1536,384]{1,0:T(8,128)S(1)}) %tuple.48), branch_computations={%region_2.3_spmd, %region_3.11_spmd} | conditional | flops 914272512 | bytes 22098448 | solution.py:126
  103.1 3.1 %fusion = (f32[384]{0:T(512)S(1)}, f32[384]{0:T(512)S(1)}, bf16[1536,384]{1,0:T(8,128)(2,1)S(1)}) fusion(f32[1536]{0:T(1024)S(1)} %mul.107, f32[1536,384]{1,0:T(8,128)S(1)} %get-tuple-element.11, bf16[1536,768]{1,0:T(8,128)(2,1)} %get-tuple-element.8, bf16[384,768]{1,0:T(8,128)(2,1)S(1)} %get-tuple-element.9), kind=kOutput, calls=%fused_computation.3 | convolution fusion | flops 909507840 | bytes 6497280 | tf_op jit(solution)/shard_map/rows_grad/cond/branch_1_fun/dot_general | solution.py:97
  106.2 0.1 copy.81
  106.4 0.1 pad_maximum_fusion
  106.5 33.4 %all_to_all.22 = bf16[4,400,384]{2,1,0:T(8,128)(2,1)S(1)} all-to-all(bf16[4,400,384]{2,1,0:T(8,128)(2,1)S(1)} %pad_maximum_fusion), channel_id=1, replica_groups=mesh['yh'=2,'z'=12,'core'=2,'yl'=4,'x'=4] {'yl'}, dimensions={0} | all-to-all | bytes 2457600 | tf_op jit(solution)/shard_map/rows_grad/cond/branch_1_fun/all_to_all | solution.py:104
  140.0 0.2 slice_reduce_fusion
  140.2 0.1 fusion.2
  140.4 0.2 copy.82
  140.6 4.0 %all_to_all.23 = bf16[2,400,192]{1,2,0:T(8,128)(2,1)S(1)} all-to-all(bf16[2,400,192]{1,2,0:T(8,128)(2,1)S(1)} %copy.82), channel_id=1, replica_groups=mesh['yh'=2,'z'=12,'core'=2,'yl'=4,'x'=4] {'core'}, dimensions={0} | all-to-all | bytes 614400 | tf_op jit(solution)/shard_map/rows_grad/cond/branch_1_fun/all_to_all | solution.py:111
  144.7 0.2 copy.97
  145.4 0.2 copy.88
  145.6 12.4 %all_to_all.24 = bf16[4,208,192]{1,2,0:T(8,128)(2,1)S(1)} all-to-all(bf16[4,208,192]{1,2,0:T(8,128)(2,1)S(1)} %copy.88), channel_id=1, replica_groups=mesh['yh'=2,'z'=12,'core'=2,'yl'=4,'x'=4] {'x'}, dimensions={0} | all-to-all | bytes 638976 | tf_op jit(solution)/shard_map/rows_grad/cond/branch_1_fun/all_to_all | solution.py:116
  158.3 0.7 convert_reduce_fusion
  159.0 0.2 slice_reduce_fusion.2
  159.2 2.5 %convolution_convert_fusion.2 = bf16[256,768]{1,0:T(8,128)(2,1)} fusion(s32[192]{0:T(256)S(1)} %compare_select_fusion, f32[2,192,768]{2,1,0:T(8,128)} %copy-done.1), kind=kOutput, calls=%fused_computation.68 | convolution fusion | flops 76627968 | bytes 1573632 | tf_op jit(solution)/shard_map/rows_out/dot_general | solution.py:145
  161.7 2.9 %reduce-scatter.2.cloned.1.call-done = bf16[128,768]{1,0:T(8,128)(2,1)} async-done(((bf16[1536,768]{1,0:T(8,128)(2,1)}), bf16[128,768]{1,0:T(8,128)(2,1)}) %reduce-scatter.2.cloned.1.call-update) | async-done | bytes 196624 | tf_op jit(solution)/shard_map/weight_grad/reduce_scatter | solution.py:94
  164.7 0.9 constant_dynamic-slice_fusion.1
  165.6 5.1 %collective-permute-start = (bf16[64,768]{1,0:T(8,128)(2,1)S(1)}, bf16[64,768]{1,0:T(8,128)(2,1)S(1)}, u32[]{:S(2)}, u32[]{:S(2)}) collective-permute-start(bf16[64,768]{1,0:T(8,128)(2,1)S(1)} %constant_dynamic-slice_fusion.1), channel_id=1, source_target_pairs={{0,384},{384,0},{1,385},{385,1},{2,386},{386,2},{3,387},{387,3},{4... | collective-permute-start | bytes 294920 | tf_op jit(solution)/shard_map/weight_out/ppermute | solution.py:153
  170.6 2.0 %convolution_convert_fusion.3 = bf16[256,192]{0,1:T(8,128)(2,1)} fusion(bf16[192,192]{0,1:T(8,128)(2,1)S(1)} %fusion.28, f32[192,192]{0,1:T(8,128)} %get-tuple-element.20, f32[192]{0:T(256)S(1)} %get-tuple-element.30, f32[192]{0:T(256)} %bitcast.88, f32[192]{0:T(256)S(1)} %get-tuple-element.29, f32[192]{0:T(256)} %dynamic_slice.23, f32[192]{0:T(256)} %bitcast.87, ...), kind=kOutput, calls=%fused_computation.71 | convolution fusion | flops 19304448 | bytes 324096 | tf_op jit(solution)/shard_map/rows_out/dot_general | solution.py:142
  172.6 4.4 %collective-permute-done = bf16[64,768]{1,0:T(8,128)(2,1)S(1)} collective-permute-done((bf16[64,768]{1,0:T(8,128)(2,1)S(1)}, bf16[64,768]{1,0:T(8,128)(2,1)S(1)}, u32[]{:S(2)}, u32[]{:S(2)}) %collective-permute-start) | collective-permute-done | bytes 98336 | tf_op jit(solution)/shard_map/weight_out/ppermute | solution.py:153
  177.0 1.6 convert_add_fusion
  (48 shorter events, 1.7 us)
Async XLA Ops:
  7.2 89.0 %copy-start = (bf16[256,768]{1,0:T(8,128)(2,1)S(1)}, bf16[256,768]{1,0:T(8,128)(2,1)}, u32[]{:S(2)}) copy-start(bf16[256,768]{1,0:T(8,128)(2,1)} %param.13) | copy-start | bytes 1179652
  7.2 80.2 %all-gather.4.cloned.1.call-start = ((), (), s32[]{:S(2)}) async-start(), calls=%async_computation.6 | async-start | bytes 2555904 | tf_op jit(solution)/shard_map/weight_gather/all_gather | solution.py:42
  34.8 5.0 %all-to-all-start.3 = ((bf16[2,384,192]{1,2,0:T(8,128)(2,1)}), bf16[2,384,192]{1,2,0:T(8,128)(2,1)S(1)}, u32[]{:S(2)}, u32[]{:S(2)}) async-start(bf16[2,384,192]{1,2,0:T(8,128)(2,1)} %copy.91), calls=%async_computation.3 | async-start | bytes 589824 | tf_op jit(solution)/shard_map/rows_gather/all_to_all | solution.py:56
  38.3 126.4 %reduce-scatter.2.cloned.1.call-start = ((), (), s32[]{:S(2)}) async-start(), calls=%async_computation.7 | async-start | bytes 2555904 | tf_op jit(solution)/shard_map/weight_grad/reduce_scatter | solution.py:94
  76.9 1.6 copy-start.2
  95.1 1.1 copy-start.1
  165.6 11.5 %collective-permute-start = (bf16[64,768]{1,0:T(8,128)(2,1)S(1)}, bf16[64,768]{1,0:T(8,128)(2,1)S(1)}, u32[]{:S(2)}, u32[]{:S(2)}) collective-permute-start(bf16[64,768]{1,0:T(8,128)(2,1)S(1)} %constant_dynamic-slice_fusion.1), channel_id=1, source_target_pairs={{0,384},{384,0},{1,385},{385,1},{2,386},{386,2},{3,387},{387,3},{4... | collective-permute-start | bytes 294920 | tf_op jit(solution)/shard_map/weight_out/ppermute | solution.py:153
Sparse Core Ops, SparseCore 0:
  18.4 68.8 all-gather.3
  101.8 62.8 reduce-scatter.1

commit v3 on v2

--- a/solution.py
+++ b/solution.py
@@ -29,6 +29,20 @@
     return total[0:2] + total[2:4] + total[4:6]
 
 
+def gather_weight(shard):
+    f32 = jnp.float32
+    count, ff_width = shard.shape
+    shard = shard.astype(f32)
+    top = jnp.maximum(jnp.max(jnp.abs(shard)), 1e-33)
+    scale = lax.reduce_precision(16384.0 / top, 8, 0)
+    power = jnp.broadcast_to(jnp.round(jnp.log2(scale)), (16, ff_width))
+    sent = jnp.concatenate([shard * scale, power]).astype(jnp.float16)
+    got = lax.all_gather(sent, "z", axis=0)
+    shrink = lax.reduce_precision(jnp.exp2(-got[:, count : count + 1].astype(f32)), 8, 0)
+    weight = (got[:, :count].astype(f32) * shrink).astype(jnp.bfloat16)
+    return weight.reshape(-1, ff_width)
+
+
 def per_device(patches, keep_order, keep_count, ln_gain, w_in, cotangent):
     own_rows, col_width = patches.shape
     depth, ff_width = w_in.shape
@@ -37,31 +51,39 @@
     core = lax.axis_index("core")
     bf16, f32 = jnp.bfloat16, jnp.float32
 
-    with jax.named_scope("weight_gather"):
-        pair_weight = lax.all_gather(w_in, "yh", axis=0, tiled=True)
-        weight = lax.all_gather(pair_weight, "z", axis=0, tiled=True)
-
     slot_ids = jnp.arange(KMOST, dtype=jnp.int32)
     row_ids = jnp.arange(own_rows, dtype=jnp.int32)
     slot_row = jnp.where(slot_ids < keep_count[0], keep_order[0, :KMOST], -1)
     select = (slot_row[:, None] == row_ids[None, :]).astype(bf16)
+    blocks = Z // 2
+    rows = CORE * KMOST
+
+    with jax.named_scope("weight_pair"):
+        met_weight = lax.ppermute(w_in, "yh", [(0, 1), (1, 0)])
 
     with jax.named_scope("rows_gather"):
         own_x = lax.dot_general(
             patches, select, (((0,), (1,)), ((), ())), preferred_element_type=f32
         ).astype(bf16)
-        block_x = lax.all_gather(own_x, "x", axis=0, tiled=True)
-        blocks = block_x.shape[0] // (CORE * depth)
-        by_core = block_x.reshape(blocks, CORE, depth, KMOST).transpose(1, 0, 2, 3)
-        pair_x = lax.all_to_all(
-            by_core.reshape(CORE, blocks * depth, KMOST), "core", split_axis=0, concat_axis=0, tiled=True
+        pair_x = lax.all_gather(own_x, "core", axis=0)
+        pair_x = jnp.concatenate([pair_x[0], pair_x[1]], axis=1).reshape(3, depth, rows)
+        two = (lax.axis_index("x") + core) % 2 == 0
+        runs = jnp.stack([jnp.where(two, pair_x[0], pair_x[1]), pair_x[2]])
+        runs = jnp.broadcast_to(runs.reshape(1, 2 * depth, rows), (YL * X, 2 * depth, rows))
+        got_x = lax.all_to_all(runs, ("yl", "x"), split_axis=0, concat_axis=0, tiled=True)
+
+    with jax.named_scope("weight_gather"):
+        first = lax.axis_index("yh") == 0
+        pair_weight = jnp.concatenate([jnp.where(first, w_in, met_weight), jnp.where(first, met_weight, w_in)])
+        weight = gather_weight(pair_weight)
+
+    with jax.named_scope("rows_order"):
+        got_x = got_x.reshape(YL * X // 2, 4, depth, rows)
+        low = core == 0
+        row_x = jnp.stack(
+            [got_x[:, 0], jnp.where(low, got_x[:, 1], got_x[:, 2]), jnp.where(low, got_x[:, 2], got_x[:, 3])], axis=1
         )
-        pair_x = jnp.concatenate([pair_x[0], pair_x[1]], axis=1)
-        rows = pair_x.shape[1]
-        cut = pair_x.shape[0] // 2
-        parts = [lax.all_gather(pair_x[i * cut : (i + 1) * cut], "yl", axis=0, tiled=True) for i in range(2)]
-        row_x = jnp.stack([p.reshape(YH, 2, blocks // 2, depth, rows) for p in parts])
-        row_x = row_x.transpose(2, 0, 3, 1, 4, 5).reshape(half, rows)
+        row_x = row_x.reshape(YH, Z, depth, rows).transpose(1, 0, 2, 3).reshape(half, rows)
 
     with jax.named_scope("row_moments"):
         x32 = row_x.astype(f32)

time: 187 us -> 215 us (1.15)
  waiting for transfers between devices: 10.2 us -> 32.2 us
  starting transfers between devices: 8.61 us -> 22.6 us
  blocking collectives: 118 us -> 106 us
  other arithmetic: 8 us -> 10.3 us
    ppermute x0 -> x1, waiting for transfers between devices: none -> 28.5 us  [per_device(): met_weight = lax.ppermute(w_in, 'yh', [(0, 1), (1, 0)])]
    all_gather x4 -> x2, blocking collectives: 59.9 us -> 48.3 us  [the longest x1 46.4 us: gather_weight(): got = lax.all_gather(sent, 'z', axis=0)]
    ppermute x0 -> x1, starting transfers between devices: none -> 9.94 us  [per_device(): met_weight = lax.ppermute(w_in, 'yh', [(0, 1), (1, 0)])]
    all_to_all x1, starting transfers between devices: 3.45 us -> 7.58 us  [per_device(): lax.all_to_all(runs, ('yl', 'x'), split_axis=0, concat_axis=0, tiled=True)]
    reduce_scatter x1, waiting for transfers between devices: 2.95 us -> 0.01 us  [per_device(): pair_w = lax.psum_scatter(part_w, 'z', scatter_dimension=0, tiled=True)]
  transfers between devices with their start and end apart: 4 -> 4, of which waited for: 4 -> 2; matrix products, arithmetic and copies ran while one was open for 13% -> 8% of each run, Pallas kernels for 0% -> 0%
where the time goes in v3:
time: 215 us; the launch traced here: 213 us
  blocking collectives  106 us (49%)
  waiting for transfers between devices  32.2 us (15%)
  starting transfers between devices  22.6 us (11%)
  between operations  16.9 us (8%)
  matrix products  15 us (7%)
  other arithmetic  10.3 us (5%)
  local copies, waits for them, and re-layouts  9.76 us (5%)
    all_gather x1, blocking collectives, gather_weight(): got = lax.all_gather(sent, 'z', axis=0)  46.4 us
    all_to_all x1, blocking collectives, rows_grad(): lax.all_to_all(jnp.concatenate([by_yl, extra], axis=1), 'yl', split_axis=...  32.4 us
    ppermute x1, waiting for transfers between devices, per_device(): met_weight = lax.ppermute(w_in, 'yh', [(0, 1), (1, 0)])  28.5 us
    all_to_all x1, blocking collectives, rows_grad(): lax.all_to_all(jnp.concatenate([by_x, extra], axis=1), 'x', split_axis=0,...  12.4 us
    ppermute x1, starting transfers between devices, per_device(): met_weight = lax.ppermute(w_in, 'yh', [(0, 1), (1, 0)])  9.94 us
    all_to_all x1, starting transfers between devices, per_device(): lax.all_to_all(runs, ('yl', 'x'), split_axis=0, concat_axis=0, tiled=True)  7.58 us
    ppermute x1, starting transfers between devices, per_device(): met_w = lax.ppermute(sent_w, 'yh', [(0, 1), (1, 0)])  5 us
    all_to_all x1, blocking collectives, per_device(): lax.all_to_all(part_act.reshape(CORE, KMOST, ff_width), 'core', split_axi...  4.68 us
  transfers between devices with their start and end apart: 4, of which 2 were waited for; matrix products, arithmetic and copies ran while one was open for 8% of the time, Pallas kernels for 0%

profile of v3, /device:TPU:56, one launch (start us, length us, event | category | flops | bytes accessed | tf_op | source)
XLA Modules:
  0.0 212.7 jit_solution(17611744060913486786)
XLA Ops:
  7.9 0.7 compare_select_fusion
  8.6 1.1 fusion.26
  9.8 1.9 all-gather
  11.9 1.4 broadcast_in_dim.14
  13.3 7.6 %all-to-all-start.3 = ((bf16[16,128,384]{2,1,0:T(8,128)(2,1)}), bf16[16,128,384]{2,1,0:T(8,128)(2,1)S(1)}, u32[]{:S(2)}, u32[]{:S(2)}) async-start(bf16[16,128,384]{2,1,0:T(8,128)(2,1)} %broadcast_in_dim.14), calls=%async_computation.3 | async-start | bytes 3145728 | tf_op jit(solution)/shard_map/rows_gather/all_to_all | solution.py:73
  20.9 9.9 %collective-permute-start = (bf16[64,768]{1,0:T(8,128)(2,1)S(1)}, bf16[64,768]{1,0:T(8,128)(2,1)S(1)}, u32[]{:S(2)}, u32[]{:S(2)}) collective-permute-start(bf16[64,768]{1,0:T(8,128)(2,1)S(1)} %copy-done.2), channel_id=1, source_target_pairs={{0,384},{384,0},{1,385},{385,1},{2,386},{386,2},{3,387},{387,3},{4... | collective-permute-start | bytes 294920 | tf_op jit(solution)/shard_map/weight_pair/ppermute | solution.py:62
  31.1 28.5 %collective-permute-done = bf16[64,768]{1,0:T(8,128)(2,1)S(1)} collective-permute-done((bf16[64,768]{1,0:T(8,128)(2,1)S(1)}, bf16[64,768]{1,0:T(8,128)(2,1)S(1)}, u32[]{:S(2)}, u32[]{:S(2)}) %collective-permute-start) | collective-permute-done | bytes 98336 | tf_op jit(solution)/shard_map/weight_pair/ppermute | solution.py:62
  59.6 0.6 fusion.32
  62.1 0.7 fusion.33
  62.8 46.4 %all-gather.5 = f16[1728,768]{1,0:T(8,128)(2,1)S(1)} all-gather(f16[144,768]{1,0:T(8,128)(2,1)S(1)} %concatenate.32), channel_id=4, replica_groups=mesh['yh'=2,'z'=12,'core'=2,'yl'=4,'x'=4] {'z'}, dimensions={0}, use_global_device_ids=true | all-gather | bytes 2875392 | tf_op jit(solution)/shard_map/weight_gather/all_gather | solution.py:40
  109.4 1.9 multiply_convert_fusion
  111.4 0.2 maximum_convert_fusion
  111.6 0.2 fusion.53
  111.8 0.2 copy.72
  112.0 0.3 fusion.24
  112.4 1.8 all-gather.3
  114.2 0.6 fusion.57
  114.8 1.4 fusion.54
  116.1 2.4 %copy.74 = bf16[384,1536]{1,0:T(8,128)(2,1)} copy(bf16[384,1536]{0,1:T(8,128)(2,1)} %get-tuple-element.35) | data formatting | bytes 2359296 | tf_op jit(solution)/shard_map/forward/dot_general | solution.py:105
  118.5 3.1 %fusion.62 = f32[2,192,768]{2,1,0:T(8,128)S(1)} fusion(bf16[2,192,1536]{2,1,0:T(8,128)(2,1)} %bitcast.90, bf16[1536,768,1]{1,0,2:T(8,128)(2,1)} %bitcast.85), kind=kOutput, calls=%fused_computation.140 | convolution fusion | flops 905969664 | bytes 4718592 | tf_op jit(solution)/shard_map/forward/dot_general | solution.py:105
  121.7 4.7 %all_to_all.25 = f32[2,192,768]{2,1,0:T(8,128)S(1)} all-to-all(f32[2,192,768]{2,1,0:T(8,128)S(1)} %fusion.62), channel_id=1, replica_groups=mesh['yh'=2,'z'=12,'core'=2,'yl'=4,'x'=4] {'core'}, dimensions={0} | all-to-all | bytes 2359296 | tf_op jit(solution)/shard_map/forward/all_to_all | solution.py:106
  126.4 1.1 copy-done.1
  127.4 0.4 fusion.25
  127.8 2.2 %all_gather.27 = bf16[384,768]{1,0:T(8,128)(2,1)S(1)} all-gather(bf16[192,768]{1,0:T(8,128)(2,1)S(1)} %fusion.25), channel_id=1, replica_groups=mesh['yh'=2,'z'=12,'core'=2,'yl'=4,'x'=4] {'core'}, dimensions={0}, use_global_device_ids=true | all-gather | bytes 884736 | tf_op jit(solution)/shard_map/forward/all_gather | solution.py:111
  130.0 2.8 %convolution_convert_fusion.1 = bf16[1536,768]{1,0:T(8,128)(2,1)} fusion(bf16[384,768]{1,0:T(8,128)(2,1)S(1)} %all_gather.27, f32[1536,384]{1,0:T(8,128)S(1)} %get-tuple-element.36, f32[1536]{0:T(1024)S(1)} %copy-done.4), kind=kOutput, calls=%fused_computation.57 | convolution fusion | flops 908328960 | bytes 5314560 | tf_op jit(solution)/shard_map/weight_grad/dot_general | solution.py:114
  132.9 1.3 dynamic_slice.23
  134.2 55.1 %conditional.1 = (f32[2,192]{0,1:T(8,128)S(1)}, f32[192,192]{0,1:T(8,128)}) conditional(s32[]{:T(128)} %convert_element_type.116, () %tuple.17, (bf16[1536,768]{1,0:T(8,128)(2,1)}, bf16[384,768]{1,0:T(8,128)(2,1)S(1)}, f32[12,2,64]{2,1,0:T(2,128)S(1)}, f32[1536,384]{1,0:T(8,128)S(1)}) %tuple.50), branch_computations={%region_3.4_spmd, %region_4.12_spmd} | conditional | flops 914272512 | bytes 22098448 | solution.py:148
  134.3 3.1 %fusion = (f32[384]{0:T(512)S(1)}, f32[384]{0:T(512)S(1)}, bf16[1536,384]{1,0:T(8,128)(2,1)S(1)}) fusion(f32[1536]{0:T(1024)S(1)} %mul.118, f32[1536,384]{1,0:T(8,128)S(1)} %get-tuple-element.11, bf16[1536,768]{1,0:T(8,128)(2,1)} %get-tuple-element.8, bf16[384,768]{1,0:T(8,128)(2,1)S(1)} %get-tuple-element.9), kind=kOutput, calls=%fused_computation.3 | convolution fusion | flops 909507840 | bytes 6497280 | tf_op jit(solution)/shard_map/rows_grad/cond/branch_1_fun/dot_general | solution.py:119
  137.4 0.1 copy.63
  137.6 0.1 pad_maximum_fusion
  137.8 32.4 %all_to_all.22 = bf16[4,400,384]{2,1,0:T(8,128)(2,1)S(1)} all-to-all(bf16[4,400,384]{2,1,0:T(8,128)(2,1)S(1)} %pad_maximum_fusion), channel_id=1, replica_groups=mesh['yh'=2,'z'=12,'core'=2,'yl'=4,'x'=4] {'yl'}, dimensions={0} | all-to-all | bytes 2457600 | tf_op jit(solution)/shard_map/rows_grad/cond/branch_1_fun/all_to_all | solution.py:126
  170.3 0.2 slice_reduce_fusion
  170.4 0.1 fusion.2
  170.6 0.2 copy.64
  170.8 4.0 %all_to_all.23 = bf16[2,400,192]{1,2,0:T(8,128)(2,1)S(1)} all-to-all(bf16[2,400,192]{1,2,0:T(8,128)(2,1)S(1)} %copy.64), channel_id=1, replica_groups=mesh['yh'=2,'z'=12,'core'=2,'yl'=4,'x'=4] {'core'}, dimensions={0} | all-to-all | bytes 614400 | tf_op jit(solution)/shard_map/rows_grad/cond/branch_1_fun/all_to_all | solution.py:133
  174.9 0.2 copy.75
  175.7 0.2 copy.70
  175.9 12.4 %all_to_all.24 = bf16[4,208,192]{1,2,0:T(8,128)(2,1)S(1)} all-to-all(bf16[4,208,192]{1,2,0:T(8,128)(2,1)S(1)} %copy.70), channel_id=1, replica_groups=mesh['yh'=2,'z'=12,'core'=2,'yl'=4,'x'=4] {'x'}, dimensions={0} | all-to-all | bytes 638976 | tf_op jit(solution)/shard_map/rows_grad/cond/branch_1_fun/all_to_all | solution.py:138
  188.3 0.1 convert_reduce_fusion.1
  188.6 0.7 convert_reduce_fusion
  189.3 0.8 constant_dynamic-slice_fusion
  190.1 0.2 slice_reduce_fusion.2
  190.3 2.5 %convolution_convert_fusion.2 = bf16[256,768]{1,0:T(8,128)(2,1)} fusion(s32[192]{0:T(256)} %copy-done.6, f32[2,192,768]{2,1,0:T(8,128)} %copy-done.1), kind=kOutput, calls=%fused_computation.65 | convolution fusion | flops 76627968 | bytes 1573632 | tf_op jit(solution)/shard_map/rows_out/dot_general | solution.py:167
  192.7 0.9 constant_dynamic-slice_fusion.1
  193.6 5.0 %collective-permute-start.1 = (bf16[64,768]{1,0:T(8,128)(2,1)S(1)}, bf16[64,768]{1,0:T(8,128)(2,1)S(1)}, u32[]{:S(2)}, u32[]{:S(2)}) collective-permute-start(bf16[64,768]{1,0:T(8,128)(2,1)S(1)} %constant_dynamic-slice_fusion.1), channel_id=1, source_target_pairs={{0,384},{384,0},{1,385},{385,1},{2,386},{386,2},{3,387},{387,3},{4... | collective-permute-start | bytes 294920 | tf_op jit(solution)/shard_map/weight_out/ppermute | solution.py:175
  198.6 2.0 convolution_convert_fusion.3
  200.6 3.7 %collective-permute-done.1 = bf16[64,768]{1,0:T(8,128)(2,1)S(1)} collective-permute-done((bf16[64,768]{1,0:T(8,128)(2,1)S(1)}, bf16[64,768]{1,0:T(8,128)(2,1)S(1)}, u32[]{:S(2)}, u32[]{:S(2)}) %collective-permute-start.1) | collective-permute-done | bytes 98336 | tf_op jit(solution)/shard_map/weight_out/ppermute | solution.py:175
  204.3 1.6 convert_add_fusion
  (59 shorter events, 1.7 us)
Async XLA Ops:
  7.2 120.2 %copy-start = (bf16[256,768]{1,0:T(8,128)(2,1)S(1)}, bf16[256,768]{1,0:T(8,128)(2,1)}, u32[]{:S(2)}) copy-start(bf16[256,768]{1,0:T(8,128)(2,1)} %param.13) | copy-start | bytes 1179652
  8.6 117.8 %copy-start.6 = (s32[192]{0:T(256)}, s32[192]{0:T(256)S(1)}, u32[]{:S(2)}) copy-start(s32[192]{0:T(256)S(1)} %compare_select_fusion) | copy-start | bytes 2308
  11.9 9.0 %copy-start.2 = (bf16[64,768]{1,0:T(8,128)(2,1)S(1)}, bf16[64,768]{1,0:T(8,128)(2,1)}, u32[]{:S(2)}) copy-start(bf16[64,768]{1,0:T(8,128)(2,1)} %param.12) | copy-start | bytes 294916
  11.9 19.0 %copy-start.5 = (f32[3072]{0:T(1024)S(1)}, f32[3072]{0:T(1024)}, u32[]{:S(2)}) copy-start(f32[3072]{0:T(1024)} %param.11) | copy-start | bytes 36868
  13.3 98.0 %all-to-all-start.3 = ((bf16[16,128,384]{2,1,0:T(8,128)(2,1)}), bf16[16,128,384]{2,1,0:T(8,128)(2,1)S(1)}, u32[]{:S(2)}, u32[]{:S(2)}) async-start(bf16[16,128,384]{2,1,0:T(8,128)(2,1)} %broadcast_in_dim.14), calls=%async_computation.3 | async-start | bytes 3145728 | tf_op jit(solution)/shard_map/rows_gather/all_to_all | solution.py:73
  20.9 171.9 %reduce-scatter.2.cloned.1.call-start = ((), (), s32[]{:S(2)}) async-start(), calls=%async_computation.6 | async-start | bytes 2555904 | tf_op jit(solution)/shard_map/weight_grad/reduce_scatter | solution.py:116
  20.9 38.6 %collective-permute-start = (bf16[64,768]{1,0:T(8,128)(2,1)S(1)}, bf16[64,768]{1,0:T(8,128)(2,1)S(1)}, u32[]{:S(2)}, u32[]{:S(2)}) collective-permute-start(bf16[64,768]{1,0:T(8,128)(2,1)S(1)} %copy-done.2), channel_id=1, source_target_pairs={{0,384},{384,0},{1,385},{385,1},{2,386},{386,2},{3,387},{387,3},{4... | collective-permute-start | bytes 294920 | tf_op jit(solution)/shard_map/weight_pair/ppermute | solution.py:62
  31.1 83.7 %copy-start.3 = (f32[1536]{0:T(1024)}, f32[1536]{0:T(1024)S(1)}, u32[]{:S(2)}) copy-start(f32[1536]{0:T(1024)S(1)} %mul.171) | copy-start | bytes 18436
  121.7 8.4 %copy-start.4 = (f32[1536]{0:T(1024)S(1)}, f32[1536]{0:T(1024)}, u32[]{:S(2)}) copy-start(f32[1536]{0:T(1024)} %copy-done.3) | copy-start | bytes 18436
  126.4 1.1 copy-start.1
  193.6 10.7 %collective-permute-start.1 = (bf16[64,768]{1,0:T(8,128)(2,1)S(1)}, bf16[64,768]{1,0:T(8,128)(2,1)S(1)}, u32[]{:S(2)}, u32[]{:S(2)}) collective-permute-start(bf16[64,768]{1,0:T(8,128)(2,1)S(1)} %constant_dynamic-slice_fusion.1), channel_id=1, source_target_pairs={{0,384},{384,0},{1,385},{385,1},{2,386},{386,2},{3,387},{387,3},{4... | collective-permute-start | bytes 294920 | tf_op jit(solution)/shard_map/weight_out/ppermute | solution.py:175
Sparse Core Ops, SparseCore 0:
  133.0 54.9 reduce-scatter.1

commit v4 on v3

--- a/solution.py
+++ b/solution.py
@@ -69,6 +69,7 @@
         pair_x = jnp.concatenate([pair_x[0], pair_x[1]], axis=1).reshape(3, depth, rows)
         two = (lax.axis_index("x") + core) % 2 == 0
         runs = jnp.stack([jnp.where(two, pair_x[0], pair_x[1]), pair_x[2]])
+        runs, met_weight = lax.optimization_barrier((runs, met_weight))
         runs = jnp.broadcast_to(runs.reshape(1, 2 * depth, rows), (YL * X, 2 * depth, rows))
         got_x = lax.all_to_all(runs, ("yl", "x"), split_axis=0, concat_axis=0, tiled=True)
 

time: 215 us -> 187 us (0.87)
  waiting for transfers between devices: 32.2 us -> 8.75 us
  starting transfers between devices: 22.6 us -> 18.5 us
    ppermute x1, waiting for transfers between devices: 28.5 us -> 3.21 us  [per_device(): met_weight = lax.ppermute(w_in, 'yh', [(0, 1), (1, 0)])]
    ppermute x1, starting transfers between devices: 9.94 us -> 4.85 us  [per_device(): met_weight = lax.ppermute(w_in, 'yh', [(0, 1), (1, 0)])]
  transfers between devices with their start and end apart: 4 -> 4, of which waited for: 2 -> 2; matrix products, arithmetic and copies ran while one was open for 8% -> 10% of each run, Pallas kernels for 0% -> 0%
where the time goes in v4:
time: 187 us
  blocking collectives  107 us (57%)
  starting transfers between devices  18.5 us (10%)
  between operations  16.8 us (9%)
  matrix products  15 us (8%)
  other arithmetic  10.3 us (6%)
  local copies, waits for them, and re-layouts  9.75 us (5%)
  waiting for transfers between devices  8.75 us (5%)
    all_gather x1, blocking collectives, gather_weight(): got = lax.all_gather(sent, 'z', axis=0)  48 us
    all_to_all x1, blocking collectives, rows_grad(): lax.all_to_all(jnp.concatenate([by_yl, extra], axis=1), 'yl', split_axis=...  32.4 us
    all_to_all x1, blocking collectives, rows_grad(): lax.all_to_all(jnp.concatenate([by_x, extra], axis=1), 'x', split_axis=0,...  12.3 us
    all_to_all x1, starting transfers between devices, per_device(): lax.all_to_all(runs, ('yl', 'x'), split_axis=0, concat_axis=0, tiled=True)  9.62 us
    ppermute x1, waiting for transfers between devices, per_device(): met_w = lax.ppermute(sent_w, 'yh', [(0, 1), (1, 0)])  5.52 us
    ppermute x1, starting transfers between devices, per_device(): met_weight = lax.ppermute(w_in, 'yh', [(0, 1), (1, 0)])  4.85 us
    all_to_all x1, blocking collectives, per_device(): lax.all_to_all(part_act.reshape(CORE, KMOST, ff_width), 'core', split_axi...  4.68 us
    all_to_all x1, blocking collectives, rows_grad(): lax.all_to_all(by_core, 'core', split_axis=0, concat_axis=0, tiled=True)  4.05 us
  transfers between devices with their start and end apart: 4, of which 2 were waited for; matrix products, arithmetic and copies ran while one was open for 10% of the time, Pallas kernels for 0%

profile of v4, /device:TPU:56, one launch (start us, length us, event | category | flops | bytes accessed | tf_op | source)
XLA Modules:
  0.0 186.7 jit_solution(16648172980805146118)
XLA Ops:
  7.2 4.8 %collective-permute-start = (bf16[64,768]{1,0:T(8,128)(2,1)}, bf16[64,768]{1,0:T(8,128)(2,1)S(1)}, u32[]{:S(2)}, u32[]{:S(2)}) collective-permute-start(bf16[64,768]{1,0:T(8,128)(2,1)} %param.12), channel_id=1, source_target_pairs={{0,384},{384,0},{1,385},{385,1},{2,386},{386,2},{3,387},{387,3},{4... | collective-permute-start | bytes 294920 | tf_op jit(solution)/shard_map/weight_pair/ppermute | solution.py:62
  12.7 0.7 compare_select_fusion
  13.4 1.1 fusion.26
  14.6 1.9 %all-gather = bf16[384,192]{1,0:T(8,128)(2,1)S(1)} all-gather(bf16[192,192]{1,0:T(8,128)(2,1)S(1)} %copy.71), channel_id=2, replica_groups=mesh['yh'=2,'z'=12,'core'=2,'yl'=4,'x'=4] {'core'}, dimensions={0}, use_global_device_ids=true | all-gather | bytes 221184 | tf_op jit(solution)/shard_map/rows_gather/all_gather | solution.py:68
  16.7 3.2 %collective-permute-done = bf16[64,768]{1,0:T(8,128)(2,1)S(1)} collective-permute-done((bf16[64,768]{1,0:T(8,128)(2,1)}, bf16[64,768]{1,0:T(8,128)(2,1)S(1)}, u32[]{:S(2)}, u32[]{:S(2)}) %collective-permute-start) | collective-permute-done | bytes 98336 | tf_op jit(solution)/shard_map/weight_pair/ppermute | solution.py:62
  19.9 1.4 broadcast_in_dim.14
  21.3 9.6 %all-to-all-start.3 = ((bf16[16,128,384]{2,1,0:T(8,128)(2,1)}), bf16[16,128,384]{2,1,0:T(8,128)(2,1)S(1)}, u32[]{:S(2)}, u32[]{:S(2)}) async-start(bf16[16,128,384]{2,1,0:T(8,128)(2,1)} %broadcast_in_dim.14), calls=%async_computation.3 | async-start | bytes 3145728 | tf_op jit(solution)/shard_map/rows_gather/all_to_all | solution.py:74
  31.2 0.6 fusion.32
  33.7 0.7 fusion.33
  34.5 48.0 %all-gather.5 = f16[1728,768]{1,0:T(8,128)(2,1)S(1)} all-gather(f16[144,768]{1,0:T(8,128)(2,1)S(1)} %concatenate.32), channel_id=4, replica_groups=mesh['yh'=2,'z'=12,'core'=2,'yl'=4,'x'=4] {'z'}, dimensions={0}, use_global_device_ids=true | all-gather | bytes 2875392 | tf_op jit(solution)/shard_map/weight_gather/all_gather | solution.py:40
  82.6 1.9 %multiply_convert_fusion = bf16[12,128,768]{2,1,0:T(8,128)(2,1)} fusion(f16[12,144,768]{2,1,0:T(8,128)(2,1)S(1)} %bitcast.82, f32[12,768]{1,0:T(8,128)S(1)} %bitcast.92), kind=kLoop, calls=%fused_computation.56 | loop fusion | flops 3538944 | bytes 4755456 | tf_op jit(solution)/shard_map/weight_gather/convert_element_type | solution.py:42
  84.7 0.2 maximum_convert_fusion
  84.8 0.2 fusion.53
  85.1 0.2 copy.72
  85.3 0.3 fusion.24
  85.6 1.8 all-gather.3
  87.4 0.6 fusion.57
  88.0 1.4 fusion.54
  89.4 2.4 %copy.74 = bf16[384,1536]{1,0:T(8,128)(2,1)} copy(bf16[384,1536]{0,1:T(8,128)(2,1)} %get-tuple-element.39) | data formatting | bytes 2359296 | tf_op jit(solution)/shard_map/forward/dot_general | solution.py:106
  91.8 3.1 %fusion.62 = f32[2,192,768]{2,1,0:T(8,128)S(1)} fusion(bf16[2,192,1536]{2,1,0:T(8,128)(2,1)} %bitcast.90, bf16[1536,768,1]{1,0,2:T(8,128)(2,1)} %bitcast.85), kind=kOutput, calls=%fused_computation.140 | convolution fusion | flops 905969664 | bytes 4718592 | tf_op jit(solution)/shard_map/forward/dot_general | solution.py:106
  94.9 4.7 %all_to_all.25 = f32[2,192,768]{2,1,0:T(8,128)S(1)} all-to-all(f32[2,192,768]{2,1,0:T(8,128)S(1)} %fusion.62), channel_id=1, replica_groups=mesh['yh'=2,'z'=12,'core'=2,'yl'=4,'x'=4] {'core'}, dimensions={0} | all-to-all | bytes 2359296 | tf_op jit(solution)/shard_map/forward/all_to_all | solution.py:107
  99.6 1.1 copy-done.1
  100.7 0.4 fusion.25
  101.1 2.2 %all_gather.27 = bf16[384,768]{1,0:T(8,128)(2,1)S(1)} all-gather(bf16[192,768]{1,0:T(8,128)(2,1)S(1)} %fusion.25), channel_id=1, replica_groups=mesh['yh'=2,'z'=12,'core'=2,'yl'=4,'x'=4] {'core'}, dimensions={0}, use_global_device_ids=true | all-gather | bytes 884736 | tf_op jit(solution)/shard_map/forward/all_gather | solution.py:112
  103.3 2.8 %convolution_convert_fusion.1 = bf16[1536,768]{1,0:T(8,128)(2,1)} fusion(bf16[384,768]{1,0:T(8,128)(2,1)S(1)} %all_gather.27, f32[1536,384]{1,0:T(8,128)S(1)} %get-tuple-element.40, f32[1536]{0:T(1024)S(1)} %copy-done.4), kind=kOutput, calls=%fused_computation.57 | convolution fusion | flops 908328960 | bytes 5314560 | tf_op jit(solution)/shard_map/weight_grad/dot_general | solution.py:115
  106.2 1.3 dynamic_slice.23
  107.5 55.0 %conditional.1 = (f32[2,192]{0,1:T(8,128)S(1)}, f32[192,192]{0,1:T(8,128)}) conditional(s32[]{:T(128)} %convert_element_type.116, () %tuple.19, (bf16[1536,768]{1,0:T(8,128)(2,1)}, bf16[384,768]{1,0:T(8,128)(2,1)S(1)}, f32[12,2,64]{2,1,0:T(2,128)S(1)}, f32[1536,384]{1,0:T(8,128)S(1)}) %tuple.52), branch_computations={%region_3.4_spmd, %region_4.12_spmd} | conditional | flops 914272512 | bytes 22098448 | solution.py:149
  107.6 3.1 %fusion = (f32[384]{0:T(512)S(1)}, f32[384]{0:T(512)S(1)}, bf16[1536,384]{1,0:T(8,128)(2,1)S(1)}) fusion(f32[1536]{0:T(1024)S(1)} %mul.118, f32[1536,384]{1,0:T(8,128)S(1)} %get-tuple-element.11, bf16[1536,768]{1,0:T(8,128)(2,1)} %get-tuple-element.8, bf16[384,768]{1,0:T(8,128)(2,1)S(1)} %get-tuple-element.9), kind=kOutput, calls=%fused_computation.3 | convolution fusion | flops 909507840 | bytes 6497280 | tf_op jit(solution)/shard_map/rows_grad/cond/branch_1_fun/dot_general | solution.py:120
  110.7 0.1 copy.63
  110.9 0.1 pad_maximum_fusion
  111.0 32.4 %all_to_all.22 = bf16[4,400,384]{2,1,0:T(8,128)(2,1)S(1)} all-to-all(bf16[4,400,384]{2,1,0:T(8,128)(2,1)S(1)} %pad_maximum_fusion), channel_id=1, replica_groups=mesh['yh'=2,'z'=12,'core'=2,'yl'=4,'x'=4] {'yl'}, dimensions={0} | all-to-all | bytes 2457600 | tf_op jit(solution)/shard_map/rows_grad/cond/branch_1_fun/all_to_all | solution.py:127
  143.5 0.2 slice_reduce_fusion
  143.7 0.1 fusion.2
  143.9 0.2 copy.64
  144.1 4.0 %all_to_all.23 = bf16[2,400,192]{1,2,0:T(8,128)(2,1)S(1)} all-to-all(bf16[2,400,192]{1,2,0:T(8,128)(2,1)S(1)} %copy.64), channel_id=1, replica_groups=mesh['yh'=2,'z'=12,'core'=2,'yl'=4,'x'=4] {'core'}, dimensions={0} | all-to-all | bytes 614400 | tf_op jit(solution)/shard_map/rows_grad/cond/branch_1_fun/all_to_all | solution.py:134
  148.2 0.2 copy.75
  148.9 0.2 copy.70
  149.1 12.3 %all_to_all.24 = bf16[4,208,192]{1,2,0:T(8,128)(2,1)S(1)} all-to-all(bf16[4,208,192]{1,2,0:T(8,128)(2,1)S(1)} %copy.70), channel_id=1, replica_groups=mesh['yh'=2,'z'=12,'core'=2,'yl'=4,'x'=4] {'x'}, dimensions={0} | all-to-all | bytes 638976 | tf_op jit(solution)/shard_map/rows_grad/cond/branch_1_fun/all_to_all | solution.py:139
  161.5 0.1 convert_reduce_fusion.1
  161.7 0.7 convert_reduce_fusion
  162.5 0.8 constant_dynamic-slice_fusion
  163.2 0.2 slice_reduce_fusion.2
  163.4 2.5 %convolution_convert_fusion.2 = bf16[256,768]{1,0:T(8,128)(2,1)} fusion(s32[192]{0:T(256)} %copy-done.6, f32[2,192,768]{2,1,0:T(8,128)} %copy-done.1), kind=kOutput, calls=%fused_computation.65 | convolution fusion | flops 76627968 | bytes 1573632 | tf_op jit(solution)/shard_map/rows_out/dot_general | solution.py:168
  165.9 0.9 constant_dynamic-slice_fusion.1
  166.8 4.0 %collective-permute-start.1 = (bf16[64,768]{1,0:T(8,128)(2,1)S(1)}, bf16[64,768]{1,0:T(8,128)(2,1)S(1)}, u32[]{:S(2)}, u32[]{:S(2)}) collective-permute-start(bf16[64,768]{1,0:T(8,128)(2,1)S(1)} %constant_dynamic-slice_fusion.1), channel_id=1, source_target_pairs={{0,384},{384,0},{1,385},{385,1},{2,386},{386,2},{3,387},{387,3},{4... | collective-permute-start | bytes 294920 | tf_op jit(solution)/shard_map/weight_out/ppermute | solution.py:176
  170.8 2.0 %convolution_convert_fusion.3 = bf16[256,192]{0,1:T(8,128)(2,1)} fusion(bf16[192,192]{0,1:T(8,128)(2,1)S(1)} %fusion.26, f32[192,192]{0,1:T(8,128)} %get-tuple-element.24, f32[192]{0:T(256)S(1)} %get-tuple-element.34, f32[192]{0:T(256)S(1)} %bitcast.97, f32[192]{0:T(256)S(1)} %get-tuple-element.33, f32[192]{0:T(256)} %dynamic_slice.23, ...), kind=kOutput, calls=%fused_computation.68 | convolution fusion | flops 19304448 | bytes 324096 | tf_op jit(solution)/shard_map/rows_out/dot_general | solution.py:165
  172.7 5.5 %collective-permute-done.1 = bf16[64,768]{1,0:T(8,128)(2,1)S(1)} collective-permute-done((bf16[64,768]{1,0:T(8,128)(2,1)S(1)}, bf16[64,768]{1,0:T(8,128)(2,1)S(1)}, u32[]{:S(2)}, u32[]{:S(2)}) %collective-permute-start.1) | collective-permute-done | bytes 98336 | tf_op jit(solution)/shard_map/weight_out/ppermute | solution.py:176
  178.3 1.6 convert_add_fusion
  (59 shorter events, 1.7 us)
Async XLA Ops:
  7.2 93.5 %copy-start = (bf16[256,768]{1,0:T(8,128)(2,1)S(1)}, bf16[256,768]{1,0:T(8,128)(2,1)}, u32[]{:S(2)}) copy-start(bf16[256,768]{1,0:T(8,128)(2,1)} %param.13) | copy-start | bytes 1179652
  7.2 12.7 %collective-permute-start = (bf16[64,768]{1,0:T(8,128)(2,1)}, bf16[64,768]{1,0:T(8,128)(2,1)S(1)}, u32[]{:S(2)}, u32[]{:S(2)}) collective-permute-start(bf16[64,768]{1,0:T(8,128)(2,1)} %param.12), channel_id=1, source_target_pairs={{0,384},{384,0},{1,385},{385,1},{2,386},{386,2},{3,387},{387,3},{4... | collective-permute-start | bytes 294920 | tf_op jit(solution)/shard_map/weight_pair/ppermute | solution.py:62
  13.4 86.2 %copy-start.6 = (s32[192]{0:T(256)}, s32[192]{0:T(256)S(1)}, u32[]{:S(2)}) copy-start(s32[192]{0:T(256)S(1)} %compare_select_fusion) | copy-start | bytes 2308
  19.9 11.1 %copy-start.5 = (f32[3072]{0:T(1024)S(1)}, f32[3072]{0:T(1024)}, u32[]{:S(2)}) copy-start(f32[3072]{0:T(1024)} %param.11) | copy-start | bytes 36868
  19.9 11.3 %copy-start.2 = (bf16[64,768]{1,0:T(8,128)(2,1)S(1)}, bf16[64,768]{1,0:T(8,128)(2,1)}, u32[]{:S(2)}) copy-start(bf16[64,768]{1,0:T(8,128)(2,1)} %param.12) | copy-start | bytes 294916
  21.3 63.3 %all-to-all-start.3 = ((bf16[16,128,384]{2,1,0:T(8,128)(2,1)}), bf16[16,128,384]{2,1,0:T(8,128)(2,1)S(1)}, u32[]{:S(2)}, u32[]{:S(2)}) async-start(bf16[16,128,384]{2,1,0:T(8,128)(2,1)} %broadcast_in_dim.14), calls=%async_computation.3 | async-start | bytes 3145728 | tf_op jit(solution)/shard_map/rows_gather/all_to_all | solution.py:74
  30.9 135.0 %reduce-scatter.2.cloned.1.call-start = ((), (), s32[]{:S(2)}) async-start(), calls=%async_computation.6 | async-start | bytes 2555904 | tf_op jit(solution)/shard_map/weight_grad/reduce_scatter | solution.py:117
  31.2 56.8 %copy-start.3 = (f32[1536]{0:T(1024)}, f32[1536]{0:T(1024)S(1)}, u32[]{:S(2)}) copy-start(f32[1536]{0:T(1024)S(1)} %mul.171) | copy-start | bytes 18436
  94.9 8.4 %copy-start.4 = (f32[1536]{0:T(1024)S(1)}, f32[1536]{0:T(1024)}, u32[]{:S(2)}) copy-start(f32[1536]{0:T(1024)} %copy-done.3) | copy-start | bytes 18436
  99.6 1.1 copy-start.1
  166.8 11.5 %collective-permute-start.1 = (bf16[64,768]{1,0:T(8,128)(2,1)S(1)}, bf16[64,768]{1,0:T(8,128)(2,1)S(1)}, u32[]{:S(2)}, u32[]{:S(2)}) collective-permute-start(bf16[64,768]{1,0:T(8,128)(2,1)S(1)} %constant_dynamic-slice_fusion.1), channel_id=1, source_target_pairs={{0,384},{384,0},{1,385},{385,1},{2,386},{386,2},{3,387},{387,3},{4... | collective-permute-start | bytes 294920 | tf_op jit(solution)/shard_map/weight_out/ppermute | solution.py:176
Sparse Core Ops, SparseCore 0:
  106.3 55.8 reduce-scatter.1

commit v5 on v2

--- a/solution.py
+++ b/solution.py
@@ -37,19 +37,26 @@
     core = lax.axis_index("core")
     bf16, f32 = jnp.bfloat16, jnp.float32
 
-    with jax.named_scope("weight_gather"):
-        pair_weight = lax.all_gather(w_in, "yh", axis=0, tiled=True)
-        weight = lax.all_gather(pair_weight, "z", axis=0, tiled=True)
-
     slot_ids = jnp.arange(KMOST, dtype=jnp.int32)
     row_ids = jnp.arange(own_rows, dtype=jnp.int32)
     slot_row = jnp.where(slot_ids < keep_count[0], keep_order[0, :KMOST], -1)
     select = (slot_row[:, None] == row_ids[None, :]).astype(bf16)
 
-    with jax.named_scope("rows_gather"):
+    with jax.named_scope("weight_pair"):
+        met_weight = lax.ppermute(w_in, "yh", [(0, 1), (1, 0)])
+
+    with jax.named_scope("own_rows"):
         own_x = lax.dot_general(
             patches, select, (((0,), (1,)), ((), ())), preferred_element_type=f32
         ).astype(bf16)
+
+    with jax.named_scope("weight_gather"):
+        own_x, met_weight = lax.optimization_barrier((own_x, met_weight))
+        first = lax.axis_index("yh") == 0
+        pair_weight = jnp.concatenate([jnp.where(first, w_in, met_weight), jnp.where(first, met_weight, w_in)])
+        weight = lax.all_gather(pair_weight, "z", axis=0, tiled=True)
+
+    with jax.named_scope("rows_gather"):
         block_x = lax.all_gather(own_x, "x", axis=0, tiled=True)
         blocks = block_x.shape[0] // (CORE * depth)
         by_core = block_x.reshape(blocks, CORE, depth, KMOST).transpose(1, 0, 2, 3)
@@ -86,6 +93,7 @@
         )
         act_value, act_slope = gelu_pair(part_act[0] + part_act[1])
         pre_grad = (rows_cot * act_slope).astype(bf16)
+        hidden_rows, pre_grad = lax.optimization_barrier((act_value.astype(bf16), pre_grad))
         pair_grad = lax.all_gather(pre_grad, "core", axis=0, tiled=True)
 
     with jax.named_scope("weight_grad"):
@@ -143,7 +151,7 @@
             select, grad_rows.astype(bf16), (((0,), (1,)), ((), ())), preferred_element_type=f32
         ).astype(bf16)
         hidden = lax.dot_general(
-            select, act_value.astype(bf16), (((0,), (0,)), ((), ())), preferred_element_type=f32
+            select, hidden_rows, (((0,), (0,)), ((), ())), preferred_element_type=f32
         ).astype(bf16)
 
     with jax.named_scope("weight_out"):

time: 187 us -> 186 us (level)
  waiting for transfers between devices: 10.2 us -> 19.5 us
  blocking collectives: 118 us -> 109 us
  local copies, waits for them, and re-layouts: 10.2 us -> 7.28 us
    all_gather x1 -> x0, blocking collectives: 11.1 us -> none  [per_device(): pair_weight = lax.all_gather(w_in, 'yh', axis=0, tiled=True)]
    all_gather x1, waiting for transfers between devices: 1.29 us -> 10.2 us  [per_device(): weight = lax.all_gather(pair_weight, 'z', axis=0, tiled=True)]
    ppermute x0 -> x1, waiting for transfers between devices: none -> 5.43 us  [per_device(): met_weight = lax.ppermute(w_in, 'yh', [(0, 1), (1, 0)])]
    ppermute x0 -> x1, starting transfers between devices: none -> 4.85 us  [per_device(): met_weight = lax.ppermute(w_in, 'yh', [(0, 1), (1, 0)])]
    all_to_all x0 -> x1, blocking collectives: none -> 3.95 us  [per_device(): lax.all_to_all(by_core.reshape(CORE, blocks * depth, KMOST), 'core', spli...]
    all_to_all x1 -> x0, starting transfers between devices: 3.45 us -> none  [per_device(): lax.all_to_all(by_core.reshape(CORE, blocks * depth, KMOST), 'core', spli...]
    reduce_scatter x1, waiting for transfers between devices: 2.95 us -> 0.24 us  [per_device(): pair_w = lax.psum_scatter(part_w, 'z', scatter_dimension=0, tiled=True)]
    all_gather x2, blocking collectives: 35.8 us -> 33.8 us  [per_device(): lax.all_gather(pair_x[i * cut:(i + 1) * cut], 'yl', axis=0, tiled=True)]
  transfers between devices with their start and end apart: 4 -> 4, of which waited for: 4 -> 4; matrix products, arithmetic and copies ran while one was open for 13% -> 11% of each run, Pallas kernels for 0% -> 0%
where the time goes in v5:
time: 186 us; the launch traced here: 184 us
  blocking collectives  109 us (59%)
  waiting for transfers between devices  19.5 us (10%)
  between operations  14.8 us (8%)
  matrix products  14.5 us (8%)
  starting transfers between devices  9.84 us (5%)
  other arithmetic  8.76 us (5%)
  local copies, waits for them, and re-layouts  7.28 us (4%)
    all_gather x2, blocking collectives, per_device(): lax.all_gather(pair_x[i * cut:(i + 1) * cut], 'yl', axis=0, tiled=True)  33.8 us
    all_to_all x1, blocking collectives, rows_grad(): lax.all_to_all(jnp.concatenate([by_yl, extra], axis=1), 'yl', split_axis=...  33.4 us
    all_gather x1, blocking collectives, per_device(): block_x = lax.all_gather(own_x, 'x', axis=0, tiled=True)  12.9 us
    all_to_all x1, blocking collectives, rows_grad(): lax.all_to_all(jnp.concatenate([by_x, extra], axis=1), 'x', split_axis=0,...  12.4 us
    all_gather x1, waiting for transfers between devices, per_device(): weight = lax.all_gather(pair_weight, 'z', axis=0, tiled=True)  10.2 us
    ppermute x1, waiting for transfers between devices, per_device(): met_weight = lax.ppermute(w_in, 'yh', [(0, 1), (1, 0)])  5.43 us
    ppermute x1, starting transfers between devices, per_device(): met_w = lax.ppermute(sent_w, 'yh', [(0, 1), (1, 0)])  4.92 us
    ppermute x1, starting transfers between devices, per_device(): met_weight = lax.ppermute(w_in, 'yh', [(0, 1), (1, 0)])  4.85 us
  transfers between devices with their start and end apart: 4, of which 4 were waited for; matrix products, arithmetic and copies ran while one was open for 11% of the time, Pallas kernels for 0%

profile of v5, /device:TPU:56, one launch (start us, length us, event | category | flops | bytes accessed | tf_op | source)
XLA Modules:
  0.0 184.2 jit_solution(2254225232692408646)
XLA Ops:
  7.2 4.8 %collective-permute-start = (bf16[64,768]{1,0:T(8,128)(2,1)}, bf16[64,768]{1,0:T(8,128)(2,1)S(1)}, u32[]{:S(2)}, u32[]{:S(2)}) collective-permute-start(bf16[64,768]{1,0:T(8,128)(2,1)} %param.12), channel_id=1, source_target_pairs={{0,384},{384,0},{1,385},{385,1},{2,386},{386,2},{3,387},{387,3},{4... | collective-permute-start | bytes 294920 | tf_op jit(solution)/shard_map/weight_pair/ppermute | solution.py:46
  12.7 0.7 compare_select_fusion
  13.4 1.1 fusion.28
  14.5 5.4 %collective-permute-done = bf16[64,768]{1,0:T(8,128)(2,1)S(1)} collective-permute-done((bf16[64,768]{1,0:T(8,128)(2,1)}, bf16[64,768]{1,0:T(8,128)(2,1)S(1)}, u32[]{:S(2)}, u32[]{:S(2)}) %collective-permute-start) | collective-permute-done | bytes 98336 | tf_op jit(solution)/shard_map/weight_pair/ppermute | solution.py:46
  20.0 0.9 broadcast_select_fusion.1
  20.9 0.7 pad_maximum_fusion.6
  21.6 0.8 reshape.119
  22.7 12.9 %all_gather.21 = bf16[768,192]{1,0:T(8,128)(2,1)S(1)} all-gather(bf16[192,192]{1,0:T(8,128)(2,1)S(1)} %copy.89), channel_id=1, replica_groups=mesh['yh'=2,'z'=12,'core'=2,'yl'=4,'x'=4] {'x'}, dimensions={0}, use_global_device_ids=true | all-gather | bytes 368640 | tf_op jit(solution)/shard_map/rows_gather/all_gather | solution.py:60
  35.6 0.2 copy.91
  35.8 4.0 %all_to_all.25 = bf16[2,384,192]{1,2,0:T(8,128)(2,1)S(1)} all-to-all(bf16[2,384,192]{1,2,0:T(8,128)(2,1)S(1)} %copy.91), channel_id=1, replica_groups=mesh['yh'=2,'z'=12,'core'=2,'yl'=4,'x'=4] {'core'}, dimensions={0} | all-to-all | bytes 589824 | tf_op jit(solution)/shard_map/rows_gather/all_to_all | solution.py:63
  39.8 0.1 copy.101
  39.9 0.1 copy.102
  40.2 17.2 %all_gather.22 = bf16[768,384]{1,0:T(8,128)(2,1)S(1)} all-gather(bf16[192,384]{1,0:T(8,128)(2,1)S(1)} %get-tuple-element.64), channel_id=1, replica_groups=mesh['yh'=2,'z'=12,'core'=2,'yl'=4,'x'=4] {'yl'}, dimensions={0}, use_global_device_ids=true | all-gather | bytes 737280 | tf_op jit(solution)/shard_map/rows_gather/all_gather | solution.py:69
  57.4 16.6 %all_gather.23 = bf16[768,384]{1,0:T(8,128)(2,1)S(1)} all-gather(bf16[192,384]{1,0:T(8,128)(2,1)S(1)} %get-tuple-element.65), channel_id=1, replica_groups=mesh['yh'=2,'z'=12,'core'=2,'yl'=4,'x'=4] {'yl'}, dimensions={0}, use_global_device_ids=true | all-gather | bytes 737280 | tf_op jit(solution)/shard_map/rows_gather/all_gather | solution.py:69
  74.0 0.2 convert_reduce_fusion.4
  74.2 0.4 fusion.23
  74.6 0.2 convert_bitcast_fusion
  74.8 0.2 copy.94
  75.0 1.8 all-gather.1
  76.8 1.4 fusion.45
  78.2 2.4 %copy.96 = bf16[384,1536]{1,0:T(8,128)(2,1)} copy(bf16[384,1536]{0,1:T(8,128)(2,1)} %get-tuple-element.45) | data formatting | bytes 2359296 | tf_op jit(solution)/shard_map/forward/dot_general | solution.py:90
  80.6 10.2 %all-gather.4.cloned.1.call-done = bf16[1536,768]{1,0:T(8,128)(2,1)} async-done(((bf16[128,768]{1,0:T(8,128)(2,1)}), bf16[1536,768]{1,0:T(8,128)(2,1)}) %all-gather.4.cloned.1.call-update) | async-done | bytes 2359312 | tf_op jit(solution)/shard_map/weight_gather/all_gather | solution.py:57
  90.8 3.1 %fusion.24 = f32[2,192,768]{2,1,0:T(8,128)S(1)} fusion(bf16[2,192,1536]{2,1,0:T(8,128)(2,1)} %bitcast.77, bf16[1536,768]{1,0:T(8,128)(2,1)} %all-gather.4.cloned.1.call-done), kind=kOutput, calls=%fused_computation.62 | convolution fusion | flops 905969664 | bytes 4718592 | tf_op jit(solution)/shard_map/forward/dot_general | solution.py:90
  93.9 4.7 %all_to_all.26 = f32[2,192,768]{2,1,0:T(8,128)S(1)} all-to-all(f32[2,192,768]{2,1,0:T(8,128)S(1)} %fusion.24), channel_id=1, replica_groups=mesh['yh'=2,'z'=12,'core'=2,'yl'=4,'x'=4] {'core'}, dimensions={0} | all-to-all | bytes 2359296 | tf_op jit(solution)/shard_map/forward/all_to_all | solution.py:91
  98.6 0.8 multiply_convert_fusion.1
  99.5 0.3 fusion.27
  99.8 2.2 %all_gather.27 = bf16[384,768]{1,0:T(8,128)(2,1)S(1)} all-gather(bf16[192,768]{1,0:T(8,128)(2,1)S(1)} %fusion.27), channel_id=1, replica_groups=mesh['yh'=2,'z'=12,'core'=2,'yl'=4,'x'=4] {'core'}, dimensions={0}, use_global_device_ids=true | all-gather | bytes 884736 | tf_op jit(solution)/shard_map/forward/all_gather | solution.py:97
  102.0 2.8 %convolution_convert_fusion.1 = bf16[1536,768]{1,0:T(8,128)(2,1)} fusion(bf16[384,768]{1,0:T(8,128)(2,1)S(1)} %all_gather.27, f32[1536,384]{1,0:T(8,128)S(1)} %get-tuple-element.46, f32[1536]{0:T(1024)S(1)} %mul.155), kind=kOutput, calls=%fused_computation.59 | convolution fusion | flops 908328960 | bytes 5314560 | tf_op jit(solution)/shard_map/weight_grad/dot_general | solution.py:100
  104.9 0.8 dynamic_slice.23
  105.7 56.1 %conditional.1 = (f32[2,192]{0,1:T(8,128)S(1)}, f32[192,192]{0,1:T(8,128)}) conditional(s32[]{:T(128)} %convert_element_type.92, () %tuple.21, (bf16[1536,768]{1,0:T(8,128)(2,1)}, bf16[384,768]{1,0:T(8,128)(2,1)S(1)}, f32[12,2,64]{2,1,0:T(2,128)S(1)}, f32[1536,384]{1,0:T(8,128)S(1)}) %tuple.54), branch_computations={%region_2.3_spmd, %region_3.11_spmd} | conditional | flops 914272512 | bytes 22098448 | solution.py:134
  105.8 3.1 %fusion = (f32[384]{0:T(512)S(1)}, f32[384]{0:T(512)S(1)}, bf16[1536,384]{1,0:T(8,128)(2,1)S(1)}) fusion(f32[1536]{0:T(1024)S(1)} %mul.107, f32[1536,384]{1,0:T(8,128)S(1)} %get-tuple-element.11, bf16[1536,768]{1,0:T(8,128)(2,1)} %get-tuple-element.8, bf16[384,768]{1,0:T(8,128)(2,1)S(1)} %get-tuple-element.9), kind=kOutput, calls=%fused_computation.3 | convolution fusion | flops 909507840 | bytes 6497280 | tf_op jit(solution)/shard_map/rows_grad/cond/branch_1_fun/dot_general | solution.py:105
  108.9 0.1 copy.81
  109.3 33.4 %all_to_all.22 = bf16[4,400,384]{2,1,0:T(8,128)(2,1)S(1)} all-to-all(bf16[4,400,384]{2,1,0:T(8,128)(2,1)S(1)} %pad_maximum_fusion), channel_id=1, replica_groups=mesh['yh'=2,'z'=12,'core'=2,'yl'=4,'x'=4] {'yl'}, dimensions={0} | all-to-all | bytes 2457600 | tf_op jit(solution)/shard_map/rows_grad/cond/branch_1_fun/all_to_all | solution.py:112
  142.7 0.2 slice_reduce_fusion
  143.1 0.2 copy.82
  143.3 4.0 %all_to_all.23 = bf16[2,400,192]{1,2,0:T(8,128)(2,1)S(1)} all-to-all(bf16[2,400,192]{1,2,0:T(8,128)(2,1)S(1)} %copy.82), channel_id=1, replica_groups=mesh['yh'=2,'z'=12,'core'=2,'yl'=4,'x'=4] {'core'}, dimensions={0} | all-to-all | bytes 614400 | tf_op jit(solution)/shard_map/rows_grad/cond/branch_1_fun/all_to_all | solution.py:119
  147.4 0.2 copy.97
  148.2 0.2 copy.88
  148.4 12.4 %all_to_all.24 = bf16[4,208,192]{1,2,0:T(8,128)(2,1)S(1)} all-to-all(bf16[4,208,192]{1,2,0:T(8,128)(2,1)S(1)} %copy.88), channel_id=1, replica_groups=mesh['yh'=2,'z'=12,'core'=2,'yl'=4,'x'=4] {'x'}, dimensions={0} | all-to-all | bytes 638976 | tf_op jit(solution)/shard_map/rows_grad/cond/branch_1_fun/all_to_all | solution.py:124
  161.0 0.7 convert_reduce_fusion
  161.8 0.2 slice_reduce_fusion.2
  162.0 2.1 %convolution_convert_fusion.2 = bf16[256,768]{1,0:T(8,128)(2,1)} fusion(bf16[192,768]{1,0:T(8,128)(2,1)} %get-tuple-element.25, s32[192]{0:T(256)S(1)} %compare_select_fusion), kind=kOutput, calls=%fused_computation.68 | convolution fusion | flops 75743232 | bytes 688896 | tf_op jit(solution)/shard_map/rows_out/dot_general | solution.py:153
  164.1 0.2 reduce-scatter.2.cloned.1.call-done
  164.4 0.9 constant_dynamic-slice_fusion.1
  165.3 4.9 %collective-permute-start.1 = (bf16[64,768]{1,0:T(8,128)(2,1)S(1)}, bf16[64,768]{1,0:T(8,128)(2,1)S(1)}, u32[]{:S(2)}, u32[]{:S(2)}) collective-permute-start(bf16[64,768]{1,0:T(8,128)(2,1)S(1)} %constant_dynamic-slice_fusion.1), channel_id=1, source_target_pairs={{0,384},{384,0},{1,385},{385,1},{2,386},{386,2},{3,387},{387,3},{4... | collective-permute-start | bytes 294920 | tf_op jit(solution)/shard_map/weight_out/ppermute | solution.py:161
  170.2 2.0 %convolution_convert_fusion.3 = bf16[256,192]{0,1:T(8,128)(2,1)} fusion(bf16[192,192]{0,1:T(8,128)(2,1)S(1)} %fusion.28, f32[192,192]{0,1:T(8,128)} %get-tuple-element.28, f32[192]{0:T(256)S(1)} %get-tuple-element.38, f32[192]{0:T(256)S(1)} %bitcast.84, f32[192]{0:T(256)S(1)} %get-tuple-element.37, f32[192]{0:T(256)S(1)} %dynamic_slice.23, ...), kind=kOutput, calls=%fused_computation.71 | convolution fusion | flops 19304448 | bytes 324096 | tf_op jit(solution)/shard_map/rows_out/dot_general | solution.py:150
  172.1 3.6 %collective-permute-done.1 = bf16[64,768]{1,0:T(8,128)(2,1)S(1)} collective-permute-done((bf16[64,768]{1,0:T(8,128)(2,1)S(1)}, bf16[64,768]{1,0:T(8,128)(2,1)S(1)}, u32[]{:S(2)}, u32[]{:S(2)}) %collective-permute-start.1) | collective-permute-done | bytes 98336 | tf_op jit(solution)/shard_map/weight_out/ppermute | solution.py:161
  175.7 1.6 convert_add_fusion
  (47 shorter events, 1.9 us)
Async XLA Ops:
  7.2 92.3 %copy-start = (bf16[256,768]{1,0:T(8,128)(2,1)S(1)}, bf16[256,768]{1,0:T(8,128)(2,1)}, u32[]{:S(2)}) copy-start(bf16[256,768]{1,0:T(8,128)(2,1)} %param.13) | copy-start | bytes 1179652
  7.2 83.6 %all-gather.4.cloned.1.call-start = ((), (), s32[]{:S(2)}) async-start(), calls=%async_computation.6 | async-start | bytes 2555904 | tf_op jit(solution)/shard_map/weight_gather/all_gather | solution.py:57
  7.2 12.7 %collective-permute-start = (bf16[64,768]{1,0:T(8,128)(2,1)}, bf16[64,768]{1,0:T(8,128)(2,1)S(1)}, u32[]{:S(2)}, u32[]{:S(2)}) collective-permute-start(bf16[64,768]{1,0:T(8,128)(2,1)} %param.12), channel_id=1, source_target_pairs={{0,384},{384,0},{1,385},{385,1},{2,386},{386,2},{3,387},{387,3},{4... | collective-permute-start | bytes 294920 | tf_op jit(solution)/shard_map/weight_pair/ppermute | solution.py:46
  21.6 142.8 %reduce-scatter.2.cloned.1.call-start = ((), (), s32[]{:S(2)}) async-start(), calls=%async_computation.7 | async-start | bytes 2555904 | tf_op jit(solution)/shard_map/weight_grad/reduce_scatter | solution.py:102
  165.3 10.5 %collective-permute-start.1 = (bf16[64,768]{1,0:T(8,128)(2,1)S(1)}, bf16[64,768]{1,0:T(8,128)(2,1)S(1)}, u32[]{:S(2)}, u32[]{:S(2)}) collective-permute-start(bf16[64,768]{1,0:T(8,128)(2,1)S(1)} %constant_dynamic-slice_fusion.1), channel_id=1, source_target_pairs={{0,384},{384,0},{1,385},{385,1},{2,386},{386,2},{3,387},{387,3},{4... | collective-permute-start | bytes 294920 | tf_op jit(solution)/shard_map/weight_out/ppermute | solution.py:161
Sparse Core Ops, SparseCore 0:
  21.7 69.0 all-gather.3
  105.0 59.3 reduce-scatter.1

commit v6 on v5

--- a/solution.py
+++ b/solution.py
@@ -1,6 +1,8 @@
 import jax
 import jax.numpy as jnp
 from jax import lax
+from jax.experimental import pallas as pl
+from jax.experimental.pallas import tpu as pltpu
 from jax.sharding import Mesh, PartitionSpec as P
 
 KMOST = 192
@@ -29,6 +31,54 @@
     return total[0:2] + total[2:4] + total[4:6]
 
 
+def columns_product(left, right):
+    depth, rows = left.shape
+    columns = right.shape[1]
+    step = depth // 4
+
+    def kernel(left_ref, right_ref, out_ref):
+        product = lax.dot_general(
+            left_ref[...], right_ref[...], (((0,), (0,)), ((), ())), preferred_element_type=jnp.float32
+        )
+        first = pl.program_id(0) == 0
+
+        @pl.when(first)
+        def _():
+            out_ref[...] = product
+
+        @pl.when(jnp.logical_not(first))
+        def _():
+            out_ref[...] += product
+
+    return pl.pallas_call(
+        kernel,
+        out_shape=jax.ShapeDtypeStruct((rows, columns), jnp.float32),
+        grid=(4,),
+        in_specs=[pl.BlockSpec((step, rows), lambda i: (i, 0)), pl.BlockSpec((step, columns), lambda i: (i, 0))],
+        out_specs=pl.BlockSpec((rows, columns), lambda i: (0, 0)),
+        compiler_params=pltpu.CompilerParams(vmem_limit_bytes=24 << 20),
+        name="columns_product",
+    )(left, right)
+
+
+def rows_product(left, right):
+    rows, depth = left.shape
+    columns = right.shape[1]
+    step = rows // 4
+
+    def kernel(left_ref, right_ref, out_ref):
+        out_ref[...] = jnp.dot(left_ref[...], right_ref[...], preferred_element_type=jnp.float32).astype(out_ref.dtype)
+
+    return pl.pallas_call(
+        kernel,
+        out_shape=jax.ShapeDtypeStruct((rows, columns), jnp.bfloat16),
+        grid=(4,),
+        in_specs=[pl.BlockSpec((step, depth), lambda i: (i, 0)), pl.BlockSpec((depth, columns), lambda i: (0, 0))],
+        out_specs=pl.BlockSpec((step, columns), lambda i: (i, 0)),
+        name="rows_product",
+    )(left, right)
+
+
 def per_device(patches, keep_order, keep_count, ln_gain, w_in, cotangent):
     own_rows, col_width = patches.shape
     depth, ff_width = w_in.shape
@@ -42,19 +92,14 @@
     slot_row = jnp.where(slot_ids < keep_count[0], keep_order[0, :KMOST], -1)
     select = (slot_row[:, None] == row_ids[None, :]).astype(bf16)
 
-    with jax.named_scope("weight_pair"):
-        met_weight = lax.ppermute(w_in, "yh", [(0, 1), (1, 0)])
+    with jax.named_scope("weight_gather"):
+        pair_weight = lax.all_gather(w_in, "yh", axis=0, tiled=True)
+        weight = lax.all_gather(pair_weight, "z", axis=0, tiled=True)
 
     with jax.named_scope("own_rows"):
         own_x = lax.dot_general(
             patches, select, (((0,), (1,)), ((), ())), preferred_element_type=f32
         ).astype(bf16)
-
-    with jax.named_scope("weight_gather"):
-        own_x, met_weight = lax.optimization_barrier((own_x, met_weight))
-        first = lax.axis_index("yh") == 0
-        pair_weight = jnp.concatenate([jnp.where(first, w_in, met_weight), jnp.where(first, met_weight, w_in)])
-        weight = lax.all_gather(pair_weight, "z", axis=0, tiled=True)
 
     with jax.named_scope("rows_gather"):
         block_x = lax.all_gather(own_x, "x", axis=0, tiled=True)
@@ -68,7 +113,7 @@
         cut = pair_x.shape[0] // 2
         parts = [lax.all_gather(pair_x[i * cut : (i + 1) * cut], "yl", axis=0, tiled=True) for i in range(2)]
         row_x = jnp.stack([p.reshape(YH, 2, blocks // 2, depth, rows) for p in parts])
-        row_x = row_x.transpose(2, 0, 3, 1, 4, 5).reshape(half, rows)
+        row_x = lax.optimization_barrier(row_x.transpose(2, 0, 3, 1, 4, 5).reshape(half, rows))
 
     with jax.named_scope("row_moments"):
         x32 = row_x.astype(f32)
@@ -87,7 +132,7 @@
 
     with jax.named_scope("forward"):
         rows_cot = jnp.dot(select, cotangent, preferred_element_type=f32)
-        part_act = lax.dot_general(normed, weight, (((0,), (0,)), ((), ())), preferred_element_type=f32)
+        part_act = columns_product(normed, weight)
         part_act = lax.all_to_all(
             part_act.reshape(CORE, KMOST, ff_width), "core", split_axis=0, concat_axis=0, tiled=True
         )
@@ -97,15 +142,19 @@
         pair_grad = lax.all_gather(pre_grad, "core", axis=0, tiled=True)
 
     with jax.named_scope("weight_grad"):
-        part_w = jnp.dot(normed, pair_grad, preferred_element_type=f32).astype(bf16)
+        part_w = rows_product(normed, pair_grad)
         part_w, pair_grad = lax.optimization_barrier((part_w, pair_grad))
         pair_w = lax.psum_scatter(part_w, "z", scatter_dimension=0, tiled=True)
 
-    def rows_grad(pair_grad):
+    def rows_grad(pair_grad, hidden_rows):
+        hidden = lax.dot_general(
+            select, hidden_rows, (((0,), (0,)), ((), ())), preferred_element_type=f32
+        ).astype(bf16)
         part_x = lax.dot_general(weight, pair_grad, (((1,), (1,)), ((), ())), preferred_element_type=f32)
         part_x = part_x.astype(bf16)
         scaled = part_x.astype(f32) * gain[:, None]
-        sums = jnp.stack([jnp.sum(scaled, axis=0), jnp.sum(scaled * normal_x, axis=0)])
+        own_normal = (row_x.astype(f32) - row_mean[None, :]) * inv_std[None, :]
+        sums = jnp.stack([jnp.sum(scaled, axis=0), jnp.sum(scaled * own_normal, axis=0)])
         by_yl = part_x.reshape(2, blocks, YH, depth, rows).transpose(2, 0, 1, 3, 4)
         by_yl = by_yl.reshape(YL, blocks * depth, rows)
         extra = jnp.broadcast_to(pieces_of(sums)[None], (YL, PIECES, rows))
@@ -128,14 +177,22 @@
         share_grad = jnp.sum(got[:, :-PIECES].astype(f32), axis=0)
 
 
-        return sums, share_grad
+        return sums, share_grad, hidden
+
+    def no_rows_grad(pair_grad, hidden_rows):
+        return (
+            jnp.zeros((2, KMOST), f32),
+            jnp.zeros((col_width, KMOST), f32),
+            jnp.zeros((own_rows, ff_width), bf16),
+        )
 
     with jax.named_scope("rows_grad"):
-        sums, share_grad = lax.cond(
+        sums, share_grad, hidden = lax.cond(
             keep_count[0] > 0,
             rows_grad,
-            lambda g: (jnp.zeros((2, KMOST), f32), jnp.zeros((col_width, KMOST), f32)),
+            no_rows_grad,
             pair_grad,
+            hidden_rows,
         )
 
     with jax.named_scope("rows_out"):
@@ -150,9 +207,6 @@
         grad_patches = lax.dot_general(
             select, grad_rows.astype(bf16), (((0,), (1,)), ((), ())), preferred_element_type=f32
         ).astype(bf16)
-        hidden = lax.dot_general(
-            select, hidden_rows, (((0,), (0,)), ((), ())), preferred_element_type=f32
-        ).astype(bf16)
 
     with jax.named_scope("weight_out"):
         yh = lax.axis_index("yh")

time: 186 us -> 185 us (level)
  Pallas kernels: 0 us -> 8.5 us
  matrix products: 14.5 us -> 6.04 us
  waiting for transfers between devices: 19.5 us -> 25.6 us
  other arithmetic: 8.76 us -> 4.82 us
  blocking collectives: 109 us -> 106 us
  starting transfers between devices: 9.84 us -> 12.7 us
  local copies, waits for them, and re-layouts: 7.28 us -> 4.91 us
    all_to_all x2 -> x0, blocking collectives: 16.4 us -> none  [the longest x1 12.4 us: rows_grad(): lax.all_to_all(jnp.concatenate([by_x, extra], axis=1), 'x', split_axis=0,...]
    all_gather x0 -> x1, blocking collectives: none -> 11.1 us  [per_device(): pair_weight = lax.all_gather(w_in, 'yh', axis=0, tiled=True)]
    all_to_all x0 -> x2, waiting for transfers between devices: none -> 9.59 us  [the longest x1 8.08 us: rows_grad(): lax.all_to_all(jnp.concatenate([by_x, extra], axis=1), 'x', split_axis=0,...]
    pallas_call x0 -> x2, Pallas kernels: none -> 8.5 us  [the longest x1 4.52 us: rows_product(): pl.pallas_call(kernel, out_shape=jax.ShapeDtypeStruct((rows, columns), jn...]
    dot_general x3 -> x1, matrix products: 8.04 us -> 0.29 us  [rows_grad(): lax.dot_general(select, hidden_rows, (((0,), (0,)), ((), ())), preferred_...]
    all_to_all x0 -> x2, starting transfers between devices: none -> 7.7 us  [the longest x1 4.25 us: rows_grad(): lax.all_to_all(jnp.concatenate([by_x, extra], axis=1), 'x', split_axis=0,...]
    ppermute x1 -> x0, waiting for transfers between devices: 5.43 us -> none  [per_device(): met_weight = lax.ppermute(w_in, 'yh', [(0, 1), (1, 0)])]
    ppermute x1 -> x0, starting transfers between devices: 4.85 us -> none  [per_device(): met_weight = lax.ppermute(w_in, 'yh', [(0, 1), (1, 0)])]
  transfers between devices with their start and end apart: 4 -> 5, of which waited for: 4 -> 5; matrix products, arithmetic and copies ran while one was open for 11% -> 7% of each run, Pallas kernels for 0% -> 0%
where the time goes in v6:
time: 185 us; the launch traced here: 184 us
  blocking collectives  106 us (57%)
  waiting for transfers between devices  25.6 us (14%)
  between operations  14.9 us (8%)
  starting transfers between devices  12.7 us (7%)
  Pallas kernels  8.5 us (5%)
  matrix products  6.04 us (3%)
  local copies, waits for them, and re-layouts  4.91 us (3%)
  other arithmetic  4.82 us (3%)
    all_gather x2, blocking collectives, per_device(): lax.all_gather(pair_x[i * cut:(i + 1) * cut], 'yl', axis=0, tiled=True)  35.8 us
    all_to_all x1, blocking collectives, rows_grad(): lax.all_to_all(jnp.concatenate([by_yl, extra], axis=1), 'yl', split_axis=...  33.4 us
    all_gather x1, blocking collectives, per_device(): block_x = lax.all_gather(own_x, 'x', axis=0, tiled=True)  13 us
    all_gather x1, blocking collectives, per_device(): pair_weight = lax.all_gather(w_in, 'yh', axis=0, tiled=True)  11.1 us
    all_to_all x1, waiting for transfers between devices, rows_grad(): lax.all_to_all(jnp.concatenate([by_x, extra], axis=1), 'x', split_axis=0,...  8.08 us
    all_gather x1, waiting for transfers between devices, per_device(): weight = lax.all_gather(pair_weight, 'z', axis=0, tiled=True)  7.88 us
    ppermute x1, waiting for transfers between devices, per_device(): met_w = lax.ppermute(sent_w, 'yh', [(0, 1), (1, 0)])  5.48 us
    ppermute x1, starting transfers between devices, per_device(): met_w = lax.ppermute(sent_w, 'yh', [(0, 1), (1, 0)])  4.95 us
  transfers between devices with their start and end apart: 5, of which 5 were waited for; matrix products, arithmetic and copies ran while one was open for 7% of the time, Pallas kernels for 0%

profile of v6, /device:TPU:56, one launch (start us, length us, event | category | flops | bytes accessed | tf_op | source)
XLA Modules:
  0.0 183.7 jit_solution(3481977011829291560)
XLA Ops:
  7.2 11.1 %all_gather.24 = bf16[128,768]{1,0:T(8,128)(2,1)} all-gather(bf16[64,768]{1,0:T(8,128)(2,1)} %param.12), channel_id=1, replica_groups=mesh['yh'=2,'z'=12,'core'=2,'yl'=4,'x'=4] {'yh'}, dimensions={0}, use_global_device_ids=true | all-gather | bytes 294912 | tf_op jit(solution)/shard_map/weight_gather/all_gather | solution.py:96
  19.0 0.7 compare_select_fusion
  19.6 1.1 fusion.28
  20.9 13.0 %all_gather.26 = bf16[768,192]{1,0:T(8,128)(2,1)S(1)} all-gather(bf16[192,192]{1,0:T(8,128)(2,1)S(1)} %copy.83), channel_id=1, replica_groups=mesh['yh'=2,'z'=12,'core'=2,'yl'=4,'x'=4] {'x'}, dimensions={0}, use_global_device_ids=true | all-gather | bytes 368640 | tf_op jit(solution)/shard_map/rows_gather/all_gather | solution.py:105
  33.9 0.9 copy.85
  34.8 3.4 %all-to-all-start.3 = ((bf16[2,384,192]{1,2,0:T(8,128)(2,1)}), bf16[2,384,192]{1,2,0:T(8,128)(2,1)S(1)}, u32[]{:S(2)}, u32[]{:S(2)}) async-start(bf16[2,384,192]{1,2,0:T(8,128)(2,1)} %copy.85), calls=%async_computation.3 | async-start | bytes 589824 | tf_op jit(solution)/shard_map/rows_gather/all_to_all | solution.py:108
  38.3 1.5 all-to-all-done.3
  39.9 0.1 copy.94
  40.0 0.1 copy.95
  40.1 0.1 fusion.35
  40.3 19.1 %all_gather.27 = bf16[768,384]{1,0:T(8,128)(2,1)S(1)} all-gather(bf16[192,384]{1,0:T(8,128)(2,1)S(1)} %get-tuple-element.68), channel_id=1, replica_groups=mesh['yh'=2,'z'=12,'core'=2,'yl'=4,'x'=4] {'yl'}, dimensions={0}, use_global_device_ids=true | all-gather | bytes 737280 | tf_op jit(solution)/shard_map/rows_gather/all_gather | solution.py:114
  59.3 16.7 %all_gather.28 = bf16[768,384]{1,0:T(8,128)(2,1)S(1)} all-gather(bf16[192,384]{1,0:T(8,128)(2,1)S(1)} %get-tuple-element.69), channel_id=1, replica_groups=mesh['yh'=2,'z'=12,'core'=2,'yl'=4,'x'=4] {'yl'}, dimensions={0}, use_global_device_ids=true | all-gather | bytes 737280 | tf_op jit(solution)/shard_map/rows_gather/all_gather | solution.py:114
  76.1 0.1 maximum_bitcast_fusion
  76.2 0.1 copy.88
  76.4 0.2 convert_reduce_fusion.4
  76.6 0.4 fusion.23
  77.2 1.8 all-gather.1
  79.1 0.4 fusion.26.left_ref
  79.5 7.9 %all-gather.4.cloned.1.call-done.right_ref = bf16[1536,768]{1,0:T(8,128)(2,1)} async-done(((bf16[128,768]{1,0:T(8,128)(2,1)}), bf16[1536,768]{1,0:T(8,128)(2,1)}) %all-gather.4.cloned.1.call-update) | async-done | bytes 2359312 | tf_op jit(solution)/shard_map/weight_gather/all_gather | solution.py:97
  87.3 4.0 %columns_product.1 = f32[384,768]{1,0:T(8,128)S(1)} custom-call(bf16[1536,384]{1,0:T(8,128)(2,1)S(1)} %fusion.26.left_ref, bf16[1536,768]{1,0:T(8,128)(2,1)} %all-gather.4.cloned.1.call-done.right_ref), custom_call_target="tpu_custom_call" | custom-call | tf_op jit(solution)/shard_map/forward/columns_product/pallas_call | solution.py:53
  91.3 4.7 %all_to_all.24 = f32[2,192,768]{2,1,0:T(8,128)S(1)} all-to-all(f32[2,192,768]{2,1,0:T(8,128)S(1)} %bitcast.55), channel_id=1, replica_groups=mesh['yh'=2,'z'=12,'core'=2,'yl'=4,'x'=4] {'core'}, dimensions={0} | all-to-all | bytes 2359296 | tf_op jit(solution)/shard_map/forward/all_to_all | solution.py:136
  96.0 0.1 multiply_convert_fusion
  96.2 0.3 fusion.27
  96.5 2.2 %all_gather.31.right_ref = bf16[384,768]{1,0:T(8,128)(2,1)S(1)} all-gather(bf16[192,768]{1,0:T(8,128)(2,1)S(1)} %fusion.27), channel_id=1, replica_groups=mesh['yh'=2,'z'=12,'core'=2,'yl'=4,'x'=4] {'core'}, dimensions={0}, use_global_device_ids=true | all-gather | bytes 884736 | tf_op jit(solution)/shard_map/forward/all_gather | solution.py:142
  98.7 4.5 %rows_product.1 = bf16[1536,768]{1,0:T(8,128)(2,1)} custom-call(bf16[1536,384]{1,0:T(8,128)(2,1)} %copy-done.1, bf16[384,768]{1,0:T(8,128)(2,1)S(1)} %all_gather.31.right_ref), custom_call_target="tpu_custom_call" | custom-call | tf_op jit(solution)/shard_map/weight_grad/rows_product/pallas_call | solution.py:72
  103.5 56.5 %conditional.1 = (f32[2,192]{0,1:T(8,128)S(1)}, f32[192,192]{0,1:T(8,128)S(1)}, bf16[256,768]{1,0:T(8,128)(2,1)S(1)}) conditional(s32[]{:T(128)} %convert_element_type.73, () %tuple.18, (bf16[1536,768]{1,0:T(8,128)(2,1)}, bf16[384,768]{1,0:T(8,128)(2,1)S(1)}, f32[12,2,64]{2,1,0:T(2,128)S(1)}, bf16[1536,384]{1,0:T(8,128)(2,1)S(1)}, f32[384]{0:T(512)S(1)}, ...), branch_computations={%region_2.3_spmd, %region_3.11_spmd} | conditional | flops 991736064 | bytes 22175288 | solution.py:190
  103.6 3.3 %fusion = (f32[384]{0:T(512)S(1)}, f32[384]{0:T(512)S(1)}, bf16[1536,384]{1,0:T(8,128)(2,1)S(1)}) fusion(f32[1536]{0:T(1024)S(1)} %mul.113, f32[384]{0:T(512)S(1)} %get-tuple-element.21, f32[384]{0:T(512)S(1)} %get-tuple-element.20, bf16[1536,384]{1,0:T(8,128)(2,1)S(1)} %get-tuple-element.19, bf16[1536,768]{1,0:T(8,128)(2,1)} %get-tuple-element.16, ...), kind=kOutput, calls=%fused_computation.3 | convolution fusion | flops 911277312 | bytes 5320704 | tf_op jit(solution)/shard_map/rows_grad/cond/branch_1_fun/dot_general | solution.py:153
  107.0 0.1 copy.75
  107.2 0.1 pad_maximum_fusion
  107.3 33.4 %all_to_all.22 = bf16[4,400,384]{2,1,0:T(8,128)(2,1)S(1)} all-to-all(bf16[4,400,384]{2,1,0:T(8,128)(2,1)S(1)} %pad_maximum_fusion), channel_id=1, replica_groups=mesh['yh'=2,'z'=12,'core'=2,'yl'=4,'x'=4] {'yl'}, dimensions={0} | all-to-all | bytes 2457600 | tf_op jit(solution)/shard_map/rows_grad/cond/branch_1_fun/all_to_all | solution.py:161
  140.8 0.2 slice_reduce_fusion
  140.9 0.1 fusion.2
  141.1 0.2 copy.76
  141.3 4.0 %all_to_all.23 = bf16[2,400,192]{1,2,0:T(8,128)(2,1)S(1)} all-to-all(bf16[2,400,192]{1,2,0:T(8,128)(2,1)S(1)} %copy.76), channel_id=1, replica_groups=mesh['yh'=2,'z'=12,'core'=2,'yl'=4,'x'=4] {'core'}, dimensions={0} | all-to-all | bytes 614400 | tf_op jit(solution)/shard_map/rows_grad/cond/branch_1_fun/all_to_all | solution.py:168
  145.4 0.2 copy.90
  146.2 1.0 copy.82
  147.1 4.2 %all-to-all-start.2 = ((bf16[4,208,192]{1,2,0:T(8,128)(2,1)}), bf16[4,208,192]{1,2,0:T(8,128)(2,1)S(1)}, u32[]{:S(2)}, u32[]{:S(2)}) async-start(bf16[4,208,192]{1,2,0:T(8,128)(2,1)} %copy.82), calls=%async_computation.2 | async-start | bytes 786432 | tf_op jit(solution)/shard_map/rows_grad/cond/branch_1_fun/all_to_all | solution.py:173
  151.4 0.3 convolution_convert_fusion.1
  151.7 8.1 %all-to-all-done.2 = bf16[4,208,192]{1,2,0:T(8,128)(2,1)S(1)} async-done(((bf16[4,208,192]{1,2,0:T(8,128)(2,1)}), bf16[4,208,192]{1,2,0:T(8,128)(2,1)S(1)}, u32[]{:S(2)}, u32[]{:S(2)}) %all-to-all-start.2) | async-done | bytes 319520 | tf_op jit(solution)/shard_map/rows_grad/cond/branch_1_fun/all_to_all | solution.py:173
  159.8 0.1 convert_reduce_fusion.1
  159.9 0.1 slice_add_fusion
  160.1 0.2 slice_reduce_fusion.2
  160.3 2.6 %reduce-scatter.2.cloned.1.call-done = bf16[128,768]{1,0:T(8,128)(2,1)} async-done(((bf16[1536,768]{1,0:T(8,128)(2,1)}), bf16[128,768]{1,0:T(8,128)(2,1)}) %reduce-scatter.2.cloned.1.call-update) | async-done | bytes 196624 | tf_op jit(solution)/shard_map/weight_grad/reduce_scatter | solution.py:147
  162.9 0.9 constant_dynamic-slice_fusion.1
  163.8 4.9 %collective-permute-start = (bf16[64,768]{1,0:T(8,128)(2,1)S(1)}, bf16[64,768]{1,0:T(8,128)(2,1)S(1)}, u32[]{:S(2)}, u32[]{:S(2)}) collective-permute-start(bf16[64,768]{1,0:T(8,128)(2,1)S(1)} %constant_dynamic-slice_fusion.1), channel_id=1, source_target_pairs={{0,384},{384,0},{1,385},{385,1},{2,386},{386,2},{3,387},{387,3},{4... | collective-permute-start | bytes 294920 | tf_op jit(solution)/shard_map/weight_out/ppermute | solution.py:215
  168.7 1.0 convolution_convert_fusion.2
  169.8 5.5 %collective-permute-done = bf16[64,768]{1,0:T(8,128)(2,1)S(1)} collective-permute-done((bf16[64,768]{1,0:T(8,128)(2,1)S(1)}, bf16[64,768]{1,0:T(8,128)(2,1)S(1)}, u32[]{:S(2)}, u32[]{:S(2)}) %collective-permute-start) | collective-permute-done | bytes 98336 | tf_op jit(solution)/shard_map/weight_out/ppermute | solution.py:215
  175.3 1.6 convert_add_fusion
  (52 shorter events, 1.7 us)
Async XLA Ops:
  7.2 89.0 %copy-start = (bf16[256,768]{1,0:T(8,128)(2,1)S(1)}, bf16[256,768]{1,0:T(8,128)(2,1)}, u32[]{:S(2)}) copy-start(bf16[256,768]{1,0:T(8,128)(2,1)} %param.13) | copy-start | bytes 1179652
  7.2 80.2 %all-gather.4.cloned.1.call-start = ((), (), s32[]{:S(2)}) async-start(), calls=%async_computation.6 | async-start | bytes 2555904 | tf_op jit(solution)/shard_map/weight_gather/all_gather | solution.py:97
  34.8 5.0 %all-to-all-start.3 = ((bf16[2,384,192]{1,2,0:T(8,128)(2,1)}), bf16[2,384,192]{1,2,0:T(8,128)(2,1)S(1)}, u32[]{:S(2)}, u32[]{:S(2)}) async-start(bf16[2,384,192]{1,2,0:T(8,128)(2,1)} %copy.85), calls=%async_computation.3 | async-start | bytes 589824 | tf_op jit(solution)/shard_map/rows_gather/all_to_all | solution.py:108
  38.3 124.6 %reduce-scatter.2.cloned.1.call-start = ((), (), s32[]{:S(2)}) async-start(), calls=%async_computation.7 | async-start | bytes 2555904 | tf_op jit(solution)/shard_map/weight_grad/reduce_scatter | solution.py:147
  76.2 0.8 copy-start.3
  79.4 11.9 %copy-start.1 = (bf16[1536,384]{1,0:T(8,128)(2,1)}, bf16[1536,384]{1,0:T(8,128)(2,1)S(1)}, u32[]{:S(2)}) copy-start(bf16[1536,384]{1,0:T(8,128)(2,1)S(1)} %fusion.26.left_ref) | copy-start | bytes 3538948
  147.1 12.6 %all-to-all-start.2 = ((bf16[4,208,192]{1,2,0:T(8,128)(2,1)}), bf16[4,208,192]{1,2,0:T(8,128)(2,1)S(1)}, u32[]{:S(2)}, u32[]{:S(2)}) async-start(bf16[4,208,192]{1,2,0:T(8,128)(2,1)} %copy.82), calls=%async_computation.2 | async-start | bytes 786432 | tf_op jit(solution)/shard_map/rows_grad/cond/branch_1_fun/all_to_all | solution.py:173
  160.1 16.8 %copy-start.2 = (bf16[256,768]{1,0:T(8,128)(2,1)}, bf16[256,768]{1,0:T(8,128)(2,1)S(1)}, u32[]{:S(2)}) copy-start(bf16[256,768]{1,0:T(8,128)(2,1)S(1)} %get-tuple-element.31) | copy-start | bytes 1179652
  163.8 11.5 %collective-permute-start = (bf16[64,768]{1,0:T(8,128)(2,1)S(1)}, bf16[64,768]{1,0:T(8,128)(2,1)S(1)}, u32[]{:S(2)}, u32[]{:S(2)}) collective-permute-start(bf16[64,768]{1,0:T(8,128)(2,1)S(1)} %constant_dynamic-slice_fusion.1), channel_id=1, source_target_pairs={{0,384},{384,0},{1,385},{385,1},{2,386},{386,2},{3,387},{387,3},{4... | collective-permute-start | bytes 294920 | tf_op jit(solution)/shard_map/weight_out/ppermute | solution.py:215
Sparse Core Ops, SparseCore 0:
  18.4 68.8 all-gather.3
  103.4 59.4 reduce-scatter.1

commit v7 on v5

--- a/solution.py
+++ b/solution.py
@@ -42,19 +42,14 @@
     slot_row = jnp.where(slot_ids < keep_count[0], keep_order[0, :KMOST], -1)
     select = (slot_row[:, None] == row_ids[None, :]).astype(bf16)
 
-    with jax.named_scope("weight_pair"):
-        met_weight = lax.ppermute(w_in, "yh", [(0, 1), (1, 0)])
+    with jax.named_scope("weight_gather"):
+        pair_weight = lax.all_gather(w_in, "yh", axis=0, tiled=True)
+        weight = lax.all_gather(pair_weight, "z", axis=0, tiled=True)
 
     with jax.named_scope("own_rows"):
         own_x = lax.dot_general(
             patches, select, (((0,), (1,)), ((), ())), preferred_element_type=f32
         ).astype(bf16)
-
-    with jax.named_scope("weight_gather"):
-        own_x, met_weight = lax.optimization_barrier((own_x, met_weight))
-        first = lax.axis_index("yh") == 0
-        pair_weight = jnp.concatenate([jnp.where(first, w_in, met_weight), jnp.where(first, met_weight, w_in)])
-        weight = lax.all_gather(pair_weight, "z", axis=0, tiled=True)
 
     with jax.named_scope("rows_gather"):
         block_x = lax.all_gather(own_x, "x", axis=0, tiled=True)
@@ -68,7 +63,7 @@
         cut = pair_x.shape[0] // 2
         parts = [lax.all_gather(pair_x[i * cut : (i + 1) * cut], "yl", axis=0, tiled=True) for i in range(2)]
         row_x = jnp.stack([p.reshape(YH, 2, blocks // 2, depth, rows) for p in parts])
-        row_x = row_x.transpose(2, 0, 3, 1, 4, 5).reshape(half, rows)
+        row_x = lax.optimization_barrier(row_x.transpose(2, 0, 3, 1, 4, 5).reshape(half, rows))
 
     with jax.named_scope("row_moments"):
         x32 = row_x.astype(f32)
@@ -83,7 +78,7 @@
         gain = lax.dynamic_index_in_dim(gain, core, 2, keepdims=False)
         gain = gain.transpose(1, 0, 2).reshape(half)
         normal_x = (x32 - row_mean[None, :]) * inv_std[None, :]
-        normed = (normal_x * gain[:, None]).astype(bf16)
+        normed = lax.optimization_barrier((normal_x * gain[:, None]).astype(bf16))
 
     with jax.named_scope("forward"):
         rows_cot = jnp.dot(select, cotangent, preferred_element_type=f32)
@@ -101,11 +96,15 @@
         part_w, pair_grad = lax.optimization_barrier((part_w, pair_grad))
         pair_w = lax.psum_scatter(part_w, "z", scatter_dimension=0, tiled=True)
 
-    def rows_grad(pair_grad):
+    def rows_grad(pair_grad, hidden_rows):
+        hidden = lax.dot_general(
+            select, hidden_rows, (((0,), (0,)), ((), ())), preferred_element_type=f32
+        ).astype(bf16)
         part_x = lax.dot_general(weight, pair_grad, (((1,), (1,)), ((), ())), preferred_element_type=f32)
         part_x = part_x.astype(bf16)
         scaled = part_x.astype(f32) * gain[:, None]
-        sums = jnp.stack([jnp.sum(scaled, axis=0), jnp.sum(scaled * normal_x, axis=0)])
+        own_normal = (row_x.astype(f32) - row_mean[None, :]) * inv_std[None, :]
+        sums = jnp.stack([jnp.sum(scaled, axis=0), jnp.sum(scaled * own_normal, axis=0)])
         by_yl = part_x.reshape(2, blocks, YH, depth, rows).transpose(2, 0, 1, 3, 4)
         by_yl = by_yl.reshape(YL, blocks * depth, rows)
         extra = jnp.broadcast_to(pieces_of(sums)[None], (YL, PIECES, rows))
@@ -128,14 +127,22 @@
         share_grad = jnp.sum(got[:, :-PIECES].astype(f32), axis=0)
 
 
-        return sums, share_grad
+        return sums, share_grad, hidden
+
+    def no_rows_grad(pair_grad, hidden_rows):
+        return (
+            jnp.zeros((2, KMOST), f32),
+            jnp.zeros((col_width, KMOST), f32),
+            jnp.zeros((own_rows, ff_width), bf16),
+        )
 
     with jax.named_scope("rows_grad"):
-        sums, share_grad = lax.cond(
+        sums, share_grad, hidden = lax.cond(
             keep_count[0] > 0,
             rows_grad,
-            lambda g: (jnp.zeros((2, KMOST), f32), jnp.zeros((col_width, KMOST), f32)),
+            no_rows_grad,
             pair_grad,
+            hidden_rows,
         )
 
     with jax.named_scope("rows_out"):
@@ -150,16 +157,10 @@
         grad_patches = lax.dot_general(
             select, grad_rows.astype(bf16), (((0,), (1,)), ((), ())), preferred_element_type=f32
         ).astype(bf16)
-        hidden = lax.dot_general(
-            select, hidden_rows, (((0,), (0,)), ((), ())), preferred_element_type=f32
-        ).astype(bf16)
 
     with jax.named_scope("weight_out"):
-        yh = lax.axis_index("yh")
-        kept_w = lax.dynamic_slice_in_dim(pair_w, yh * depth, depth, 0)
-        sent_w = lax.dynamic_slice_in_dim(pair_w, (1 - yh) * depth, depth, 0)
-        met_w = lax.ppermute(sent_w, "yh", [(0, 1), (1, 0)])
-        w_grad = kept_w.astype(f32) + met_w.astype(f32)
+        met_w = lax.all_to_all(pair_w.reshape(YH, depth, ff_width), "yh", split_axis=0, concat_axis=0, tiled=True)
+        w_grad = met_w[0].astype(f32) + met_w[1].astype(f32)
     return (hidden, grad_patches, w_grad)
 
 

time: 186 us -> 185 us (level)
  the two profiles are of different devices: /device:TPU:56 before, /device:TPU:8 now
where the time goes in v7:
time: 185 us
  blocking collectives  107 us (58%)
  waiting for transfers between devices  27.1 us (15%)
  between operations  14.9 us (8%)
  starting transfers between devices  13.9 us (8%)
  matrix products  11.6 us (6%)
  local copies, waits for them, and re-layouts  5.62 us (3%)
  other arithmetic  3.93 us (2%)
    all_gather x2, blocking collectives, per_device(): lax.all_gather(pair_x[i * cut:(i + 1) * cut], 'yl', axis=0, tiled=True)  36 us
    all_to_all x1, blocking collectives, rows_grad(): lax.all_to_all(jnp.concatenate([by_yl, extra], axis=1), 'yl', split_axis=...  33.3 us
    all_gather x1, blocking collectives, per_device(): block_x = lax.all_gather(own_x, 'x', axis=0, tiled=True)  12.9 us
    all_gather x1, blocking collectives, per_device(): pair_weight = lax.all_gather(w_in, 'yh', axis=0, tiled=True)  12.4 us
    all_to_all x1, waiting for transfers between devices, per_device(): lax.all_to_all(pair_w.reshape(YH, depth, ff_width), 'yh', split_axis=0, c...  8.66 us
    all_to_all x1, waiting for transfers between devices, rows_grad(): lax.all_to_all(jnp.concatenate([by_x, extra], axis=1), 'x', split_axis=0,...  8.08 us
    all_gather x1, waiting for transfers between devices, per_device(): weight = lax.all_gather(pair_weight, 'z', axis=0, tiled=True)  6.94 us
    all_to_all x1, starting transfers between devices, per_device(): lax.all_to_all(pair_w.reshape(YH, depth, ff_width), 'yh', split_axis=0, c...  6.14 us
  transfers between devices with their start and end apart: 5, of which 5 were waited for; matrix products, arithmetic and copies ran while one was open for 7% of the time, Pallas kernels for 0%

profile of v7, /device:TPU:8, one launch (start us, length us, event | category | flops | bytes accessed | tf_op | source)
XLA Modules:
  0.0 184.6 jit_solution(17729457708918514992)
XLA Ops:
  7.2 12.4 %all_gather.24 = bf16[128,768]{1,0:T(8,128)(2,1)} all-gather(bf16[64,768]{1,0:T(8,128)(2,1)} %param.12), channel_id=1, replica_groups=mesh['yh'=2,'z'=12,'core'=2,'yl'=4,'x'=4] {'yh'}, dimensions={0}, use_global_device_ids=true | all-gather | bytes 294912 | tf_op jit(solution)/shard_map/weight_gather/all_gather | solution.py:46
  20.3 0.7 compare_select_fusion
  21.0 1.1 fusion.28
  22.2 12.9 %all_gather.26 = bf16[768,192]{1,0:T(8,128)(2,1)S(1)} all-gather(bf16[192,192]{1,0:T(8,128)(2,1)S(1)} %copy.82), channel_id=1, replica_groups=mesh['yh'=2,'z'=12,'core'=2,'yl'=4,'x'=4] {'x'}, dimensions={0}, use_global_device_ids=true | all-gather | bytes 368640 | tf_op jit(solution)/shard_map/rows_gather/all_gather | solution.py:55
  35.2 0.9 copy.84
  36.0 3.4 %all-to-all-start.3 = ((bf16[2,384,192]{1,2,0:T(8,128)(2,1)}), bf16[2,384,192]{1,2,0:T(8,128)(2,1)S(1)}, u32[]{:S(2)}, u32[]{:S(2)}) async-start(bf16[2,384,192]{1,2,0:T(8,128)(2,1)} %copy.84), calls=%async_computation.3 | async-start | bytes 589824 | tf_op jit(solution)/shard_map/rows_gather/all_to_all | solution.py:58
  39.6 1.5 all-to-all-done.3
  41.1 0.1 copy.93
  41.2 0.1 copy.94
  41.4 0.1 fusion.35
  41.5 19.5 %all_gather.27 = bf16[768,384]{1,0:T(8,128)(2,1)S(1)} all-gather(bf16[192,384]{1,0:T(8,128)(2,1)S(1)} %get-tuple-element.68), channel_id=1, replica_groups=mesh['yh'=2,'z'=12,'core'=2,'yl'=4,'x'=4] {'yl'}, dimensions={0}, use_global_device_ids=true | all-gather | bytes 737280 | tf_op jit(solution)/shard_map/rows_gather/all_gather | solution.py:64
  61.0 16.6 %all_gather.28 = bf16[768,384]{1,0:T(8,128)(2,1)S(1)} all-gather(bf16[192,384]{1,0:T(8,128)(2,1)S(1)} %get-tuple-element.69), channel_id=1, replica_groups=mesh['yh'=2,'z'=12,'core'=2,'yl'=4,'x'=4] {'yl'}, dimensions={0}, use_global_device_ids=true | all-gather | bytes 737280 | tf_op jit(solution)/shard_map/rows_gather/all_gather | solution.py:64
  77.5 0.1 maximum_bitcast_fusion
  77.7 0.1 copy.87
  77.8 0.2 convert_reduce_fusion.4
  78.1 0.4 fusion.23
  78.7 1.8 all-gather.1
  80.6 0.4 fusion.26
  80.9 6.9 %all-gather.4.cloned.1.call-done = bf16[1536,768]{1,0:T(8,128)(2,1)} async-done(((bf16[128,768]{1,0:T(8,128)(2,1)}), bf16[1536,768]{1,0:T(8,128)(2,1)}) %all-gather.4.cloned.1.call-update) | async-done | bytes 2359312 | tf_op jit(solution)/shard_map/weight_gather/all_gather | solution.py:47
  87.9 2.8 %fusion.49 = f32[384,768]{1,0:T(8,128)S(1)} fusion(bf16[1536,384]{1,0:T(8,128)(2,1)S(1)} %fusion.26, bf16[1536,768]{1,0:T(8,128)(2,1)} %all-gather.4.cloned.1.call-done), kind=kOutput, calls=%fused_computation.115 | convolution fusion | flops 905969664 | bytes 4718592 | tf_op jit(solution)/shard_map/forward/dot_general | solution.py:85
  90.7 4.7 %all_to_all.29 = f32[2,192,768]{2,1,0:T(8,128)S(1)} all-to-all(f32[2,192,768]{2,1,0:T(8,128)S(1)} %bitcast.74), channel_id=1, replica_groups=mesh['yh'=2,'z'=12,'core'=2,'yl'=4,'x'=4] {'core'}, dimensions={0} | all-to-all | bytes 2359296 | tf_op jit(solution)/shard_map/forward/all_to_all | solution.py:86
  95.3 0.1 multiply_convert_fusion
  95.5 0.3 fusion.27
  95.8 2.2 %all_gather.31 = bf16[384,768]{1,0:T(8,128)(2,1)S(1)} all-gather(bf16[192,768]{1,0:T(8,128)(2,1)S(1)} %fusion.27), channel_id=1, replica_groups=mesh['yh'=2,'z'=12,'core'=2,'yl'=4,'x'=4] {'core'}, dimensions={0}, use_global_device_ids=true | all-gather | bytes 884736 | tf_op jit(solution)/shard_map/forward/all_gather | solution.py:92
  98.1 0.8 copy-done.1
  98.9 2.8 %convolution_convert_fusion.2 = bf16[1536,768]{1,0:T(8,128)(2,1)} fusion(bf16[1536,384]{1,0:T(8,128)(2,1)S(1)} %fusion.26, bf16[384,768]{1,0:T(8,128)(2,1)S(1)} %all_gather.31), kind=kOutput, calls=%fused_computation.60 | convolution fusion | flops 907149312 | bytes 4128768 | tf_op jit(solution)/shard_map/weight_grad/dot_general | solution.py:95
  102.0 0.8 copy-done.2
  102.8 56.3 %conditional.1 = (f32[2,192]{0,1:T(8,128)S(1)}, f32[192,192]{0,1:T(8,128)S(1)}, bf16[256,768]{1,0:T(8,128)(2,1)S(1)}) conditional(s32[]{:T(128)} %convert_element_type.78, () %tuple.18, (bf16[1536,768]{1,0:T(8,128)(2,1)}, bf16[384,768]{1,0:T(8,128)(2,1)S(1)}, f32[12,2,64]{2,1,0:T(2,128)S(1)}, bf16[1536,384]{1,0:T(8,128)(2,1)S(1)}, f32[384]{0:T(512)S(1)}, ...), branch_computations={%region_2.3_spmd, %region_3.11_spmd} | conditional | flops 991736064 | bytes 22175288 | solution.py:140
  102.8 3.3 %fusion = (f32[384]{0:T(512)S(1)}, f32[384]{0:T(512)S(1)}, bf16[1536,384]{1,0:T(8,128)(2,1)S(1)}) fusion(f32[1536]{0:T(1024)S(1)} %mul.109, f32[384]{0:T(512)S(1)} %get-tuple-element.21, f32[384]{0:T(512)S(1)} %get-tuple-element.20, bf16[1536,384]{1,0:T(8,128)(2,1)S(1)} %get-tuple-element.19, bf16[1536,768]{1,0:T(8,128)(2,1)} %get-tuple-element.16, ...), kind=kOutput, calls=%fused_computation.3 | convolution fusion | flops 911277312 | bytes 5320704 | tf_op jit(solution)/shard_map/rows_grad/cond/branch_1_fun/dot_general | solution.py:103
  106.1 0.1 copy.74
  106.3 0.1 pad_maximum_fusion
  106.5 33.3 %all_to_all.27 = bf16[4,400,384]{2,1,0:T(8,128)(2,1)S(1)} all-to-all(bf16[4,400,384]{2,1,0:T(8,128)(2,1)S(1)} %pad_maximum_fusion), channel_id=1, replica_groups=mesh['yh'=2,'z'=12,'core'=2,'yl'=4,'x'=4] {'yl'}, dimensions={0} | all-to-all | bytes 2457600 | tf_op jit(solution)/shard_map/rows_grad/cond/branch_1_fun/all_to_all | solution.py:111
  139.8 0.2 slice_reduce_fusion
  140.0 0.1 fusion.2
  140.2 0.2 copy.75
  140.4 4.0 %all_to_all.28 = bf16[2,400,192]{1,2,0:T(8,128)(2,1)S(1)} all-to-all(bf16[2,400,192]{1,2,0:T(8,128)(2,1)S(1)} %copy.75), channel_id=1, replica_groups=mesh['yh'=2,'z'=12,'core'=2,'yl'=4,'x'=4] {'core'}, dimensions={0} | all-to-all | bytes 614400 | tf_op jit(solution)/shard_map/rows_grad/cond/branch_1_fun/all_to_all | solution.py:118
  144.5 0.2 copy.89
  145.2 1.0 copy.81
  146.2 4.2 %all-to-all-start.2 = ((bf16[4,208,192]{1,2,0:T(8,128)(2,1)}), bf16[4,208,192]{1,2,0:T(8,128)(2,1)S(1)}, u32[]{:S(2)}, u32[]{:S(2)}) async-start(bf16[4,208,192]{1,2,0:T(8,128)(2,1)} %copy.81), calls=%async_computation.2 | async-start | bytes 786432 | tf_op jit(solution)/shard_map/rows_grad/cond/branch_1_fun/all_to_all | solution.py:123
  150.4 0.3 convolution_convert_fusion.1
  150.7 8.1 %all-to-all-done.2 = bf16[4,208,192]{1,2,0:T(8,128)(2,1)S(1)} async-done(((bf16[4,208,192]{1,2,0:T(8,128)(2,1)}), bf16[4,208,192]{1,2,0:T(8,128)(2,1)S(1)}, u32[]{:S(2)}, u32[]{:S(2)}) %all-to-all-start.2) | async-done | bytes 319520 | tf_op jit(solution)/shard_map/rows_grad/cond/branch_1_fun/all_to_all | solution.py:123
  158.8 0.1 convert_reduce_fusion.1
  159.1 0.2 slice_reduce_fusion.2
  159.3 1.9 %reduce-scatter.2.cloned.1.call-done = bf16[128,768]{1,0:T(8,128)(2,1)} async-done(((bf16[1536,768]{1,0:T(8,128)(2,1)}), bf16[128,768]{1,0:T(8,128)(2,1)}) %reduce-scatter.2.cloned.1.call-update) | async-done | bytes 196624 | tf_op jit(solution)/shard_map/weight_grad/reduce_scatter | solution.py:97
  161.2 6.1 %all-to-all-start.5 = ((bf16[2,64,768]{2,1,0:T(8,128)(2,1)}), bf16[2,64,768]{2,1,0:T(8,128)(2,1)S(1)}, u32[]{:S(2)}, u32[]{:S(2)}) async-start(bf16[2,64,768]{2,1,0:T(8,128)(2,1)} %bitcast.77), calls=%async_computation.6 | async-start | bytes 393216 | tf_op jit(solution)/shard_map/weight_out/all_to_all | solution.py:162
  167.4 1.0 convolution_convert_fusion.3
  168.4 8.7 %all-to-all-done.5 = bf16[2,64,768]{2,1,0:T(8,128)(2,1)S(1)} async-done(((bf16[2,64,768]{2,1,0:T(8,128)(2,1)}), bf16[2,64,768]{2,1,0:T(8,128)(2,1)S(1)}, u32[]{:S(2)}, u32[]{:S(2)}) %all-to-all-start.5) | async-done | bytes 196640 | tf_op jit(solution)/shard_map/weight_out/all_to_all | solution.py:162
  177.0 0.7 add_bitcast_fusion
  (53 shorter events, 1.8 us)
Async XLA Ops:
  7.2 88.3 %copy-start = (bf16[256,768]{1,0:T(8,128)(2,1)S(1)}, bf16[256,768]{1,0:T(8,128)(2,1)}, u32[]{:S(2)}) copy-start(bf16[256,768]{1,0:T(8,128)(2,1)} %param.13) | copy-start | bytes 1179652
  7.2 80.7 %all-gather.4.cloned.1.call-start = ((), (), s32[]{:S(2)}) async-start(), calls=%async_computation.7 | async-start | bytes 2555904 | tf_op jit(solution)/shard_map/weight_gather/all_gather | solution.py:47
  36.0 5.0 %all-to-all-start.3 = ((bf16[2,384,192]{1,2,0:T(8,128)(2,1)}), bf16[2,384,192]{1,2,0:T(8,128)(2,1)S(1)}, u32[]{:S(2)}, u32[]{:S(2)}) async-start(bf16[2,384,192]{1,2,0:T(8,128)(2,1)} %copy.84), calls=%async_computation.3 | async-start | bytes 589824 | tf_op jit(solution)/shard_map/rows_gather/all_to_all | solution.py:58
  39.5 121.7 %reduce-scatter.2.cloned.1.call-start = ((), (), s32[]{:S(2)}) async-start(), calls=%async_computation.8 | async-start | bytes 2555904 | tf_op jit(solution)/shard_map/weight_grad/reduce_scatter | solution.py:97
  77.7 0.8 copy-start.4
  98.1 0.8 copy-start.1
  101.7 1.1 copy-start.2
  146.2 12.6 %all-to-all-start.2 = ((bf16[4,208,192]{1,2,0:T(8,128)(2,1)}), bf16[4,208,192]{1,2,0:T(8,128)(2,1)S(1)}, u32[]{:S(2)}, u32[]{:S(2)}) async-start(bf16[4,208,192]{1,2,0:T(8,128)(2,1)} %copy.81), calls=%async_computation.2 | async-start | bytes 786432 | tf_op jit(solution)/shard_map/rows_grad/cond/branch_1_fun/all_to_all | solution.py:123
  159.1 18.7 %copy-start.3 = (bf16[256,768]{1,0:T(8,128)(2,1)}, bf16[256,768]{1,0:T(8,128)(2,1)S(1)}, u32[]{:S(2)}) copy-start(bf16[256,768]{1,0:T(8,128)(2,1)S(1)} %get-tuple-element.31) | copy-start | bytes 1179652
  161.2 15.8 %all-to-all-start.5 = ((bf16[2,64,768]{2,1,0:T(8,128)(2,1)}), bf16[2,64,768]{2,1,0:T(8,128)(2,1)S(1)}, u32[]{:S(2)}, u32[]{:S(2)}) async-start(bf16[2,64,768]{2,1,0:T(8,128)(2,1)} %bitcast.77), calls=%async_computation.6 | async-start | bytes 393216 | tf_op jit(solution)/shard_map/weight_out/all_to_all | solution.py:162
Sparse Core Ops, SparseCore 0:
  19.8 68.0 all-gather.3
  101.8 59.3 reduce-scatter.1

commit v8 on v7

--- a/solution.py
+++ b/solution.py
@@ -93,7 +93,6 @@
 
     with jax.named_scope("weight_grad"):
         part_w = jnp.dot(normed, pair_grad, preferred_element_type=f32).astype(bf16)
-        part_w, pair_grad = lax.optimization_barrier((part_w, pair_grad))
         pair_w = lax.psum_scatter(part_w, "z", scatter_dimension=0, tiled=True)
 
     def rows_grad(pair_grad, hidden_rows):
@@ -159,8 +158,11 @@
         ).astype(bf16)
 
     with jax.named_scope("weight_out"):
-        met_w = lax.all_to_all(pair_w.reshape(YH, depth, ff_width), "yh", split_axis=0, concat_axis=0, tiled=True)
-        w_grad = met_w[0].astype(f32) + met_w[1].astype(f32)
+        yh = lax.axis_index("yh")
+        kept_w = lax.dynamic_slice_in_dim(pair_w, yh * depth, depth, 0)
+        sent_w = lax.dynamic_slice_in_dim(pair_w, (1 - yh) * depth, depth, 0)
+        met_w = lax.ppermute(sent_w, "yh", [(0, 1), (1, 0)])
+        w_grad = kept_w.astype(f32) + met_w.astype(f32)
     return (hidden, grad_patches, w_grad)
 
 

time: 185 us -> 183 us (0.989)
  the two profiles are of different devices: /device:TPU:8 before, /device:TPU:56 now
where the time goes in v8:
time: 183 us; the launch traced here: 182 us
  blocking collectives  106 us (58%)
  waiting for transfers between devices  24.9 us (14%)
  between operations  14.9 us (8%)
  starting transfers between devices  12.7 us (7%)
  matrix products  11.6 us (6%)
  local copies, waits for them, and re-layouts  6.52 us (4%)
  other arithmetic  4.83 us (3%)
    all_gather x2, blocking collectives, per_device(): lax.all_gather(pair_x[i * cut:(i + 1) * cut], 'yl', axis=0, tiled=True)  35.8 us
    all_to_all x1, blocking collectives, rows_grad(): lax.all_to_all(jnp.concatenate([by_yl, extra], axis=1), 'yl', split_axis=...  33.4 us
    all_gather x1, blocking collectives, per_device(): block_x = lax.all_gather(own_x, 'x', axis=0, tiled=True)  13 us
    all_gather x1, blocking collectives, per_device(): pair_weight = lax.all_gather(w_in, 'yh', axis=0, tiled=True)  11.1 us
    all_to_all x1, waiting for transfers between devices, rows_grad(): lax.all_to_all(jnp.concatenate([by_x, extra], axis=1), 'x', split_axis=0,...  8.08 us
    all_gather x1, waiting for transfers between devices, per_device(): weight = lax.all_gather(pair_weight, 'z', axis=0, tiled=True)  7.87 us
    ppermute x1, waiting for transfers between devices, per_device(): met_w = lax.ppermute(sent_w, 'yh', [(0, 1), (1, 0)])  5.53 us
    ppermute x1, starting transfers between devices, per_device(): met_w = lax.ppermute(sent_w, 'yh', [(0, 1), (1, 0)])  4.89 us
  transfers between devices with their start and end apart: 5, of which 5 were waited for; matrix products, arithmetic and copies ran while one was open for 7% of the time, Pallas kernels for 0%

profile of v8, /device:TPU:56, one launch (start us, length us, event | category | flops | bytes accessed | tf_op | source)
XLA Modules:
  0.0 181.6 jit_solution(6858444699221999351)
XLA Ops:
  7.2 11.1 %all_gather.24 = bf16[128,768]{1,0:T(8,128)(2,1)} all-gather(bf16[64,768]{1,0:T(8,128)(2,1)} %param.12), channel_id=1, replica_groups=mesh['yh'=2,'z'=12,'core'=2,'yl'=4,'x'=4] {'yh'}, dimensions={0}, use_global_device_ids=true | all-gather | bytes 294912 | tf_op jit(solution)/shard_map/weight_gather/all_gather | solution.py:46
  19.0 0.7 compare_select_fusion
  19.6 1.1 fusion.28
  20.9 13.0 %all_gather.26 = bf16[768,192]{1,0:T(8,128)(2,1)S(1)} all-gather(bf16[192,192]{1,0:T(8,128)(2,1)S(1)} %copy.82), channel_id=1, replica_groups=mesh['yh'=2,'z'=12,'core'=2,'yl'=4,'x'=4] {'x'}, dimensions={0}, use_global_device_ids=true | all-gather | bytes 368640 | tf_op jit(solution)/shard_map/rows_gather/all_gather | solution.py:55
  33.9 0.9 copy.84
  34.8 3.4 %all-to-all-start.3 = ((bf16[2,384,192]{1,2,0:T(8,128)(2,1)}), bf16[2,384,192]{1,2,0:T(8,128)(2,1)S(1)}, u32[]{:S(2)}, u32[]{:S(2)}) async-start(bf16[2,384,192]{1,2,0:T(8,128)(2,1)} %copy.84), calls=%async_computation.3 | async-start | bytes 589824 | tf_op jit(solution)/shard_map/rows_gather/all_to_all | solution.py:58
  38.3 1.5 all-to-all-done.3
  39.9 0.1 copy.93
  40.0 0.1 copy.94
  40.2 0.1 fusion.35
  40.3 19.1 %all_gather.27 = bf16[768,384]{1,0:T(8,128)(2,1)S(1)} all-gather(bf16[192,384]{1,0:T(8,128)(2,1)S(1)} %get-tuple-element.64), channel_id=1, replica_groups=mesh['yh'=2,'z'=12,'core'=2,'yl'=4,'x'=4] {'yl'}, dimensions={0}, use_global_device_ids=true | all-gather | bytes 737280 | tf_op jit(solution)/shard_map/rows_gather/all_gather | solution.py:64
  59.3 16.7 %all_gather.28 = bf16[768,384]{1,0:T(8,128)(2,1)S(1)} all-gather(bf16[192,384]{1,0:T(8,128)(2,1)S(1)} %get-tuple-element.65), channel_id=1, replica_groups=mesh['yh'=2,'z'=12,'core'=2,'yl'=4,'x'=4] {'yl'}, dimensions={0}, use_global_device_ids=true | all-gather | bytes 737280 | tf_op jit(solution)/shard_map/rows_gather/all_gather | solution.py:64
  76.1 0.1 maximum_bitcast_fusion
  76.2 0.1 copy.87
  76.4 0.2 convert_reduce_fusion.4
  76.6 0.4 fusion.23
  77.3 1.8 all-gather.1
  79.1 0.4 fusion.26
  79.5 7.9 %all-gather.4.cloned.1.call-done = bf16[1536,768]{1,0:T(8,128)(2,1)} async-done(((bf16[128,768]{1,0:T(8,128)(2,1)}), bf16[1536,768]{1,0:T(8,128)(2,1)}) %all-gather.4.cloned.1.call-update) | async-done | bytes 2359312 | tf_op jit(solution)/shard_map/weight_gather/all_gather | solution.py:47
  87.3 2.8 %fusion.49 = f32[384,768]{1,0:T(8,128)S(1)} fusion(bf16[1536,384]{1,0:T(8,128)(2,1)S(1)} %fusion.26, bf16[1536,768]{1,0:T(8,128)(2,1)} %all-gather.4.cloned.1.call-done), kind=kOutput, calls=%fused_computation.116 | convolution fusion | flops 905969664 | bytes 4718592 | tf_op jit(solution)/shard_map/forward/dot_general | solution.py:85
  90.1 4.7 %all_to_all.24 = f32[2,192,768]{2,1,0:T(8,128)S(1)} all-to-all(f32[2,192,768]{2,1,0:T(8,128)S(1)} %bitcast.71), channel_id=1, replica_groups=mesh['yh'=2,'z'=12,'core'=2,'yl'=4,'x'=4] {'core'}, dimensions={0} | all-to-all | bytes 2359296 | tf_op jit(solution)/shard_map/forward/all_to_all | solution.py:86
  94.8 0.1 multiply_convert_fusion
  95.0 0.3 fusion.27
  95.3 2.2 %all_gather.31 = bf16[384,768]{1,0:T(8,128)(2,1)S(1)} all-gather(bf16[192,768]{1,0:T(8,128)(2,1)S(1)} %fusion.27), channel_id=1, replica_groups=mesh['yh'=2,'z'=12,'core'=2,'yl'=4,'x'=4] {'core'}, dimensions={0}, use_global_device_ids=true | all-gather | bytes 884736 | tf_op jit(solution)/shard_map/forward/all_gather | solution.py:92
  97.5 0.8 copy-done.1
  98.4 2.8 %convolution_convert_fusion.2 = bf16[1536,768]{1,0:T(8,128)(2,1)} fusion(bf16[1536,384]{1,0:T(8,128)(2,1)S(1)} %fusion.26, bf16[384,768]{1,0:T(8,128)(2,1)S(1)} %all_gather.31), kind=kOutput, calls=%fused_computation.60 | convolution fusion | flops 907149312 | bytes 4128768 | tf_op jit(solution)/shard_map/weight_grad/dot_general | solution.py:95
  101.4 0.8 copy-done.2
  102.2 56.5 %conditional.1 = (f32[2,192]{0,1:T(8,128)S(1)}, f32[192,192]{0,1:T(8,128)S(1)}, bf16[256,768]{1,0:T(8,128)(2,1)S(1)}) conditional(s32[]{:T(128)} %convert_element_type.76, () %tuple.17, (bf16[1536,768]{1,0:T(8,128)(2,1)}, bf16[384,768]{1,0:T(8,128)(2,1)S(1)}, f32[12,2,64]{2,1,0:T(2,128)S(1)}, bf16[1536,384]{1,0:T(8,128)(2,1)S(1)}, f32[384]{0:T(512)S(1)}, ...), branch_computations={%region_2.3_spmd, %region_3.11_spmd} | conditional | flops 991736064 | bytes 22175288 | solution.py:139
  102.3 3.3 %fusion = (f32[384]{0:T(512)S(1)}, f32[384]{0:T(512)S(1)}, bf16[1536,384]{1,0:T(8,128)(2,1)S(1)}) fusion(f32[1536]{0:T(1024)S(1)} %mul.113, f32[384]{0:T(512)S(1)} %get-tuple-element.21, f32[384]{0:T(512)S(1)} %get-tuple-element.20, bf16[1536,384]{1,0:T(8,128)(2,1)S(1)} %get-tuple-element.19, bf16[1536,768]{1,0:T(8,128)(2,1)} %get-tuple-element.16, ...), kind=kOutput, calls=%fused_computation.3 | convolution fusion | flops 911277312 | bytes 5320704 | tf_op jit(solution)/shard_map/rows_grad/cond/branch_1_fun/dot_general | solution.py:102
  105.6 0.1 copy.74
  105.8 0.1 pad_maximum_fusion
  105.9 33.4 %all_to_all.22 = bf16[4,400,384]{2,1,0:T(8,128)(2,1)S(1)} all-to-all(bf16[4,400,384]{2,1,0:T(8,128)(2,1)S(1)} %pad_maximum_fusion), channel_id=1, replica_groups=mesh['yh'=2,'z'=12,'core'=2,'yl'=4,'x'=4] {'yl'}, dimensions={0} | all-to-all | bytes 2457600 | tf_op jit(solution)/shard_map/rows_grad/cond/branch_1_fun/all_to_all | solution.py:110
  139.4 0.2 slice_reduce_fusion
  139.6 0.1 fusion.2
  139.8 0.2 copy.75
  140.0 4.0 %all_to_all.23 = bf16[2,400,192]{1,2,0:T(8,128)(2,1)S(1)} all-to-all(bf16[2,400,192]{1,2,0:T(8,128)(2,1)S(1)} %copy.75), channel_id=1, replica_groups=mesh['yh'=2,'z'=12,'core'=2,'yl'=4,'x'=4] {'core'}, dimensions={0} | all-to-all | bytes 614400 | tf_op jit(solution)/shard_map/rows_grad/cond/branch_1_fun/all_to_all | solution.py:117
  144.1 0.2 copy.89
  144.8 1.0 copy.81
  145.8 4.2 %all-to-all-start.2 = ((bf16[4,208,192]{1,2,0:T(8,128)(2,1)}), bf16[4,208,192]{1,2,0:T(8,128)(2,1)S(1)}, u32[]{:S(2)}, u32[]{:S(2)}) async-start(bf16[4,208,192]{1,2,0:T(8,128)(2,1)} %copy.81), calls=%async_computation.2 | async-start | bytes 786432 | tf_op jit(solution)/shard_map/rows_grad/cond/branch_1_fun/all_to_all | solution.py:122
  150.0 0.3 convolution_convert_fusion.1
  150.3 8.1 %all-to-all-done.2 = bf16[4,208,192]{1,2,0:T(8,128)(2,1)S(1)} async-done(((bf16[4,208,192]{1,2,0:T(8,128)(2,1)}), bf16[4,208,192]{1,2,0:T(8,128)(2,1)S(1)}, u32[]{:S(2)}, u32[]{:S(2)}) %all-to-all-start.2) | async-done | bytes 319520 | tf_op jit(solution)/shard_map/rows_grad/cond/branch_1_fun/all_to_all | solution.py:122
  158.7 0.2 slice_reduce_fusion.2
  158.9 1.9 %reduce-scatter.2.cloned.1.call-done = bf16[128,768]{1,0:T(8,128)(2,1)} async-done(((bf16[1536,768]{1,0:T(8,128)(2,1)}), bf16[128,768]{1,0:T(8,128)(2,1)}) %reduce-scatter.2.cloned.1.call-update) | async-done | bytes 196624 | tf_op jit(solution)/shard_map/weight_grad/reduce_scatter | solution.py:96
  160.8 0.9 constant_dynamic-slice_fusion.1
  161.7 4.9 %collective-permute-start = (bf16[64,768]{1,0:T(8,128)(2,1)S(1)}, bf16[64,768]{1,0:T(8,128)(2,1)S(1)}, u32[]{:S(2)}, u32[]{:S(2)}) collective-permute-start(bf16[64,768]{1,0:T(8,128)(2,1)S(1)} %constant_dynamic-slice_fusion.1), channel_id=1, source_target_pairs={{0,384},{384,0},{1,385},{385,1},{2,386},{386,2},{3,387},{387,3},{4... | collective-permute-start | bytes 294920 | tf_op jit(solution)/shard_map/weight_out/ppermute | solution.py:164
  166.6 1.0 convolution_convert_fusion.3
  167.6 5.5 %collective-permute-done = bf16[64,768]{1,0:T(8,128)(2,1)S(1)} collective-permute-done((bf16[64,768]{1,0:T(8,128)(2,1)S(1)}, bf16[64,768]{1,0:T(8,128)(2,1)S(1)}, u32[]{:S(2)}, u32[]{:S(2)}) %collective-permute-start) | collective-permute-done | bytes 98336 | tf_op jit(solution)/shard_map/weight_out/ppermute | solution.py:164
  173.2 1.6 convert_add_fusion
  (54 shorter events, 1.9 us)
Async XLA Ops:
  7.2 87.8 %copy-start = (bf16[256,768]{1,0:T(8,128)(2,1)S(1)}, bf16[256,768]{1,0:T(8,128)(2,1)}, u32[]{:S(2)}) copy-start(bf16[256,768]{1,0:T(8,128)(2,1)} %param.13) | copy-start | bytes 1179652
  7.2 80.2 %all-gather.4.cloned.1.call-start = ((), (), s32[]{:S(2)}) async-start(), calls=%async_computation.6 | async-start | bytes 2555904 | tf_op jit(solution)/shard_map/weight_gather/all_gather | solution.py:47
  34.8 5.0 %all-to-all-start.3 = ((bf16[2,384,192]{1,2,0:T(8,128)(2,1)}), bf16[2,384,192]{1,2,0:T(8,128)(2,1)S(1)}, u32[]{:S(2)}, u32[]{:S(2)}) async-start(bf16[2,384,192]{1,2,0:T(8,128)(2,1)} %copy.84), calls=%async_computation.3 | async-start | bytes 589824 | tf_op jit(solution)/shard_map/rows_gather/all_to_all | solution.py:58
  38.3 122.6 %reduce-scatter.2.cloned.1.call-start = ((), (), s32[]{:S(2)}) async-start(), calls=%async_computation.7 | async-start | bytes 2555904 | tf_op jit(solution)/shard_map/weight_grad/reduce_scatter | solution.py:96
  76.2 0.8 copy-start.4
  97.5 0.8 copy-start.1
  101.1 1.1 copy-start.2
  145.8 12.6 %all-to-all-start.2 = ((bf16[4,208,192]{1,2,0:T(8,128)(2,1)}), bf16[4,208,192]{1,2,0:T(8,128)(2,1)S(1)}, u32[]{:S(2)}, u32[]{:S(2)}) async-start(bf16[4,208,192]{1,2,0:T(8,128)(2,1)} %copy.81), calls=%async_computation.2 | async-start | bytes 786432 | tf_op jit(solution)/shard_map/rows_grad/cond/branch_1_fun/all_to_all | solution.py:122
  158.7 16.1 %copy-start.3 = (bf16[256,768]{1,0:T(8,128)(2,1)}, bf16[256,768]{1,0:T(8,128)(2,1)S(1)}, u32[]{:S(2)}) copy-start(bf16[256,768]{1,0:T(8,128)(2,1)S(1)} %get-tuple-element.29) | copy-start | bytes 1179652
  161.7 11.5 %collective-permute-start = (bf16[64,768]{1,0:T(8,128)(2,1)S(1)}, bf16[64,768]{1,0:T(8,128)(2,1)S(1)}, u32[]{:S(2)}, u32[]{:S(2)}) collective-permute-start(bf16[64,768]{1,0:T(8,128)(2,1)S(1)} %constant_dynamic-slice_fusion.1), channel_id=1, source_target_pairs={{0,384},{384,0},{1,385},{385,1},{2,386},{386,2},{3,387},{387,3},{4... | collective-permute-start | bytes 294920 | tf_op jit(solution)/shard_map/weight_out/ppermute | solution.py:164
Sparse Core Ops, SparseCore 0:
  18.4 68.8 all-gather.3
  101.3 59.4 reduce-scatter.1

commit v9 on v8

--- a/solution.py
+++ b/solution.py
@@ -101,9 +101,8 @@
         ).astype(bf16)
         part_x = lax.dot_general(weight, pair_grad, (((1,), (1,)), ((), ())), preferred_element_type=f32)
         part_x = part_x.astype(bf16)
-        scaled = part_x.astype(f32) * gain[:, None]
-        own_normal = (row_x.astype(f32) - row_mean[None, :]) * inv_std[None, :]
-        sums = jnp.stack([jnp.sum(scaled, axis=0), jnp.sum(scaled * own_normal, axis=0)])
+        part_32 = part_x.astype(f32)
+        sums = jnp.stack([jnp.sum(part_32 * gain[:, None], axis=0), jnp.sum(part_32 * normed.astype(f32), axis=0)])
         by_yl = part_x.reshape(2, blocks, YH, depth, rows).transpose(2, 0, 1, 3, 4)
         by_yl = by_yl.reshape(YL, blocks * depth, rows)
         extra = jnp.broadcast_to(pieces_of(sums)[None], (YL, PIECES, rows))
@@ -161,6 +160,7 @@
         yh = lax.axis_index("yh")
         kept_w = lax.dynamic_slice_in_dim(pair_w, yh * depth, depth, 0)
         sent_w = lax.dynamic_slice_in_dim(pair_w, (1 - yh) * depth, depth, 0)
+        kept_w, sent_w = lax.optimization_barrier((kept_w, sent_w))
         met_w = lax.ppermute(sent_w, "yh", [(0, 1), (1, 0)])
         w_grad = kept_w.astype(f32) + met_w.astype(f32)
     return (hidden, grad_patches, w_grad)

time: 183 us -> 181 us (0.989)
  no operation moved by 1% of the time
where the time goes in v9:
time: 181 us; the launch traced here: 180 us
  blocking collectives  106 us (59%)
  waiting for transfers between devices  24.9 us (14%)
  between operations  14.9 us (8%)
  starting transfers between devices  12.9 us (7%)
  matrix products  11.5 us (6%)
  local copies, waits for them, and re-layouts  5.52 us (3%)
  other arithmetic  3.93 us (2%)
    all_gather x2, blocking collectives, per_device(): lax.all_gather(pair_x[i * cut:(i + 1) * cut], 'yl', axis=0, tiled=True)  35.8 us
    all_to_all x1, blocking collectives, rows_grad(): lax.all_to_all(jnp.concatenate([by_yl, extra], axis=1), 'yl', split_axis=...  33.4 us
    all_gather x1, blocking collectives, per_device(): block_x = lax.all_gather(own_x, 'x', axis=0, tiled=True)  13 us
    all_gather x1, blocking collectives, per_device(): pair_weight = lax.all_gather(w_in, 'yh', axis=0, tiled=True)  11.1 us
    all_to_all x1, waiting for transfers between devices, rows_grad(): lax.all_to_all(jnp.concatenate([by_x, extra], axis=1), 'x', split_axis=0,...  8.08 us
    all_gather x1, waiting for transfers between devices, per_device(): weight = lax.all_gather(pair_weight, 'z', axis=0, tiled=True)  7.33 us
    ppermute x1, waiting for transfers between devices, per_device(): met_w = lax.ppermute(sent_w, 'yh', [(0, 1), (1, 0)])  5.34 us
    ppermute x1, starting transfers between devices, per_device(): met_w = lax.ppermute(sent_w, 'yh', [(0, 1), (1, 0)])  5.1 us
  transfers between devices with their start and end apart: 5, of which 5 were waited for; matrix products, arithmetic and copies ran while one was open for 7% of the time, Pallas kernels for 0%

profile of v9, /device:TPU:56, one launch (start us, length us, event | category | flops | bytes accessed | tf_op | source)
XLA Modules:
  0.0 179.8 jit_solution(10521599676951369003)
XLA Ops:
  7.2 11.1 %all_gather.24 = bf16[128,768]{1,0:T(8,128)(2,1)} all-gather(bf16[64,768]{1,0:T(8,128)(2,1)} %param.12), channel_id=1, replica_groups=mesh['yh'=2,'z'=12,'core'=2,'yl'=4,'x'=4] {'yh'}, dimensions={0}, use_global_device_ids=true | all-gather | bytes 294912 | tf_op jit(solution)/shard_map/weight_gather/all_gather | solution.py:46
  19.0 0.7 compare_select_fusion
  19.6 1.1 fusion.29
  20.9 13.0 %all_gather.26 = bf16[768,192]{1,0:T(8,128)(2,1)S(1)} all-gather(bf16[192,192]{1,0:T(8,128)(2,1)S(1)} %copy.82), channel_id=1, replica_groups=mesh['yh'=2,'z'=12,'core'=2,'yl'=4,'x'=4] {'x'}, dimensions={0}, use_global_device_ids=true | all-gather | bytes 368640 | tf_op jit(solution)/shard_map/rows_gather/all_gather | solution.py:55
  33.9 0.9 copy.84
  34.8 3.4 %all-to-all-start.3 = ((bf16[2,384,192]{1,2,0:T(8,128)(2,1)}), bf16[2,384,192]{1,2,0:T(8,128)(2,1)S(1)}, u32[]{:S(2)}, u32[]{:S(2)}) async-start(bf16[2,384,192]{1,2,0:T(8,128)(2,1)} %copy.84), calls=%async_computation.3 | async-start | bytes 589824 | tf_op jit(solution)/shard_map/rows_gather/all_to_all | solution.py:58
  38.3 1.5 all-to-all-done.3
  39.9 0.1 copy.93
  40.0 0.1 copy.94
  40.1 0.1 fusion.36
  40.3 19.1 %all_gather.28 = bf16[768,384]{1,0:T(8,128)(2,1)S(1)} all-gather(bf16[192,384]{1,0:T(8,128)(2,1)S(1)} %get-tuple-element.63), channel_id=1, replica_groups=mesh['yh'=2,'z'=12,'core'=2,'yl'=4,'x'=4] {'yl'}, dimensions={0}, use_global_device_ids=true | all-gather | bytes 737280 | tf_op jit(solution)/shard_map/rows_gather/all_gather | solution.py:64
  59.3 16.7 %all_gather.27 = bf16[768,384]{1,0:T(8,128)(2,1)S(1)} all-gather(bf16[192,384]{1,0:T(8,128)(2,1)S(1)} %get-tuple-element.62), channel_id=1, replica_groups=mesh['yh'=2,'z'=12,'core'=2,'yl'=4,'x'=4] {'yl'}, dimensions={0}, use_global_device_ids=true | all-gather | bytes 737280 | tf_op jit(solution)/shard_map/rows_gather/all_gather | solution.py:64
  76.1 0.1 maximum_bitcast_fusion
  76.2 0.1 copy.87
  76.4 0.6 copy-done.2
  77.1 0.2 convert_reduce_fusion.4
  77.4 0.4 fusion.24
  77.8 1.8 all-gather.1
  79.6 0.4 fusion.27
  80.0 7.3 %all-gather.4.cloned.1.call-done = bf16[1536,768]{1,0:T(8,128)(2,1)} async-done(((bf16[128,768]{1,0:T(8,128)(2,1)}), bf16[1536,768]{1,0:T(8,128)(2,1)}) %all-gather.4.cloned.1.call-update) | async-done | bytes 2359312 | tf_op jit(solution)/shard_map/weight_gather/all_gather | solution.py:47
  87.3 2.8 %fusion.50 = f32[384,768]{1,0:T(8,128)S(1)} fusion(bf16[1536,384]{1,0:T(8,128)(2,1)S(1)} %fusion.27, bf16[1536,768]{1,0:T(8,128)(2,1)} %all-gather.4.cloned.1.call-done), kind=kOutput, calls=%fused_computation.118 | convolution fusion | flops 905969664 | bytes 4718592 | tf_op jit(solution)/shard_map/forward/dot_general | solution.py:85
  90.1 4.7 %all_to_all.24 = f32[2,192,768]{2,1,0:T(8,128)S(1)} all-to-all(f32[2,192,768]{2,1,0:T(8,128)S(1)} %bitcast.70), channel_id=1, replica_groups=mesh['yh'=2,'z'=12,'core'=2,'yl'=4,'x'=4] {'core'}, dimensions={0} | all-to-all | bytes 2359296 | tf_op jit(solution)/shard_map/forward/all_to_all | solution.py:86
  94.8 0.1 multiply_convert_fusion
  94.9 0.3 fusion.28
  95.3 2.2 %all_gather.31 = bf16[384,768]{1,0:T(8,128)(2,1)S(1)} all-gather(bf16[192,768]{1,0:T(8,128)(2,1)S(1)} %fusion.28), channel_id=1, replica_groups=mesh['yh'=2,'z'=12,'core'=2,'yl'=4,'x'=4] {'core'}, dimensions={0}, use_global_device_ids=true | all-gather | bytes 884736 | tf_op jit(solution)/shard_map/forward/all_gather | solution.py:92
  97.5 2.8 %convolution_convert_fusion.2 = bf16[1536,768]{1,0:T(8,128)(2,1)} fusion(bf16[1536,384]{1,0:T(8,128)(2,1)S(1)} %fusion.27, bf16[384,768]{1,0:T(8,128)(2,1)S(1)} %all_gather.31), kind=kOutput, calls=%fused_computation.61 | convolution fusion | flops 907149312 | bytes 4128768 | tf_op jit(solution)/shard_map/weight_grad/dot_general | solution.py:95
  100.6 56.4 %conditional.1 = (f32[2,192]{0,1:T(8,128)S(1)}, f32[192,192]{0,1:T(8,128)S(1)}, bf16[256,768]{1,0:T(8,128)(2,1)S(1)}) conditional(s32[]{:T(128)} %convert_element_type.76, () %tuple.18, (bf16[1536,768]{1,0:T(8,128)(2,1)}, bf16[384,768]{1,0:T(8,128)(2,1)S(1)}, f32[12,2,64]{2,1,0:T(2,128)S(1)}, bf16[1536,384]{1,0:T(8,128)(2,1)S(1)}, ...), branch_computations={%region_2.3_spmd, %region_3.11_spmd} | conditional | flops 990556416 | bytes 22172216 | solution.py:138
  100.7 3.2 %fusion = (f32[384]{0:T(512)S(1)}, f32[384]{0:T(512)S(1)}, bf16[1536,384]{1,0:T(8,128)(2,1)S(1)}) fusion(f32[1536]{0:T(1024)S(1)} %mul.107, bf16[1536,384]{1,0:T(8,128)(2,1)S(1)} %get-tuple-element.15, bf16[1536,768]{1,0:T(8,128)(2,1)} %get-tuple-element.12, bf16[384,768]{1,0:T(8,128)(2,1)S(1)} %get-tuple-element.13), kind=kOutput, calls=%fused_computation.3 | convolution fusion | flops 910097664 | bytes 5317632 | tf_op jit(solution)/shard_map/rows_grad/cond/branch_1_fun/dot_general | solution.py:102
  103.9 0.1 copy.74
  104.1 0.1 pad_maximum_fusion
  104.2 33.4 %all_to_all.22 = bf16[4,400,384]{2,1,0:T(8,128)(2,1)S(1)} all-to-all(bf16[4,400,384]{2,1,0:T(8,128)(2,1)S(1)} %pad_maximum_fusion), channel_id=1, replica_groups=mesh['yh'=2,'z'=12,'core'=2,'yl'=4,'x'=4] {'yl'}, dimensions={0} | all-to-all | bytes 2457600 | tf_op jit(solution)/shard_map/rows_grad/cond/branch_1_fun/all_to_all | solution.py:109
  137.7 0.2 slice_reduce_fusion
  137.8 0.1 fusion.3
  138.1 0.2 copy.75
  138.3 4.0 %all_to_all.23 = bf16[2,400,192]{1,2,0:T(8,128)(2,1)S(1)} all-to-all(bf16[2,400,192]{1,2,0:T(8,128)(2,1)S(1)} %copy.75), channel_id=1, replica_groups=mesh['yh'=2,'z'=12,'core'=2,'yl'=4,'x'=4] {'core'}, dimensions={0} | all-to-all | bytes 614400 | tf_op jit(solution)/shard_map/rows_grad/cond/branch_1_fun/all_to_all | solution.py:116
  142.8 0.2 copy.89
  143.1 1.0 copy.81
  144.0 4.2 %all-to-all-start.2 = ((bf16[4,208,192]{1,2,0:T(8,128)(2,1)}), bf16[4,208,192]{1,2,0:T(8,128)(2,1)S(1)}, u32[]{:S(2)}, u32[]{:S(2)}) async-start(bf16[4,208,192]{1,2,0:T(8,128)(2,1)} %copy.81), calls=%async_computation.2 | async-start | bytes 786432 | tf_op jit(solution)/shard_map/rows_grad/cond/branch_1_fun/all_to_all | solution.py:121
  148.3 0.3 convolution_convert_fusion.1
  148.6 8.1 %all-to-all-done.2 = bf16[4,208,192]{1,2,0:T(8,128)(2,1)S(1)} async-done(((bf16[4,208,192]{1,2,0:T(8,128)(2,1)}), bf16[4,208,192]{1,2,0:T(8,128)(2,1)S(1)}, u32[]{:S(2)}, u32[]{:S(2)}) %all-to-all-start.2) | async-done | bytes 319520 | tf_op jit(solution)/shard_map/rows_grad/cond/branch_1_fun/all_to_all | solution.py:121
  156.7 0.1 convert_reduce_fusion.1
  157.0 0.2 slice_reduce_fusion.2
  157.2 2.6 %reduce-scatter.2.cloned.1.call-done = bf16[128,768]{1,0:T(8,128)(2,1)} async-done(((bf16[1536,768]{1,0:T(8,128)(2,1)}), bf16[128,768]{1,0:T(8,128)(2,1)}) %reduce-scatter.2.cloned.1.call-update) | async-done | bytes 196624 | tf_op jit(solution)/shard_map/weight_grad/reduce_scatter | solution.py:96
  159.8 1.0 constant_dynamic-slice_fusion.1
  160.8 5.1 %collective-permute-start = (bf16[64,768]{1,0:T(8,128)(2,1)S(1)}, bf16[64,768]{1,0:T(8,128)(2,1)S(1)}, u32[]{:S(2)}, u32[]{:S(2)}) collective-permute-start(bf16[64,768]{1,0:T(8,128)(2,1)S(1)} %get-tuple-element.34), channel_id=1, source_target_pairs={{0,384},{384,0},{1,385},{385,1},{2,386},{386,2},{3,387},{387,3},{4... | collective-permute-start | bytes 294920 | tf_op jit(solution)/shard_map/weight_out/ppermute | solution.py:164
  165.9 1.0 convolution_convert_fusion.3
  166.9 5.3 %collective-permute-done = bf16[64,768]{1,0:T(8,128)(2,1)S(1)} collective-permute-done((bf16[64,768]{1,0:T(8,128)(2,1)S(1)}, bf16[64,768]{1,0:T(8,128)(2,1)S(1)}, u32[]{:S(2)}, u32[]{:S(2)}) %collective-permute-start) | collective-permute-done | bytes 98336 | tf_op jit(solution)/shard_map/weight_out/ppermute | solution.py:164
  172.2 0.7 convert_add_fusion
  (50 shorter events, 1.8 us)
Async XLA Ops:
  7.2 87.8 %copy-start = (bf16[256,768]{1,0:T(8,128)(2,1)S(1)}, bf16[256,768]{1,0:T(8,128)(2,1)}, u32[]{:S(2)}) copy-start(bf16[256,768]{1,0:T(8,128)(2,1)} %param.13) | copy-start | bytes 1179652
  7.2 80.2 %all-gather.4.cloned.1.call-start = ((), (), s32[]{:S(2)}) async-start(), calls=%async_computation.6 | async-start | bytes 2555904 | tf_op jit(solution)/shard_map/weight_gather/all_gather | solution.py:47
  34.8 5.0 %all-to-all-start.3 = ((bf16[2,384,192]{1,2,0:T(8,128)(2,1)}), bf16[2,384,192]{1,2,0:T(8,128)(2,1)S(1)}, u32[]{:S(2)}, u32[]{:S(2)}) async-start(bf16[2,384,192]{1,2,0:T(8,128)(2,1)} %copy.84), calls=%async_computation.3 | async-start | bytes 589824 | tf_op jit(solution)/shard_map/rows_gather/all_to_all | solution.py:58
  38.3 121.6 %reduce-scatter.2.cloned.1.call-start = ((), (), s32[]{:S(2)}) async-start(), calls=%async_computation.7 | async-start | bytes 2555904 | tf_op jit(solution)/shard_map/weight_grad/reduce_scatter | solution.py:96
  76.2 0.7 copy-start.2
  144.0 12.6 %all-to-all-start.2 = ((bf16[4,208,192]{1,2,0:T(8,128)(2,1)}), bf16[4,208,192]{1,2,0:T(8,128)(2,1)S(1)}, u32[]{:S(2)}, u32[]{:S(2)}) async-start(bf16[4,208,192]{1,2,0:T(8,128)(2,1)} %copy.81), calls=%async_computation.2 | async-start | bytes 786432 | tf_op jit(solution)/shard_map/rows_grad/cond/branch_1_fun/all_to_all | solution.py:121
  157.0 16.0 %copy-start.1 = (bf16[256,768]{1,0:T(8,128)(2,1)}, bf16[256,768]{1,0:T(8,128)(2,1)S(1)}, u32[]{:S(2)}) copy-start(bf16[256,768]{1,0:T(8,128)(2,1)S(1)} %get-tuple-element.25) | copy-start | bytes 1179652
  160.8 11.5 %collective-permute-start = (bf16[64,768]{1,0:T(8,128)(2,1)S(1)}, bf16[64,768]{1,0:T(8,128)(2,1)S(1)}, u32[]{:S(2)}, u32[]{:S(2)}) collective-permute-start(bf16[64,768]{1,0:T(8,128)(2,1)S(1)} %get-tuple-element.34), channel_id=1, source_target_pairs={{0,384},{384,0},{1,385},{385,1},{2,386},{386,2},{3,387},{387,3},{4... | collective-permute-start | bytes 294920 | tf_op jit(solution)/shard_map/weight_out/ppermute | solution.py:164
Sparse Core Ops, SparseCore 0:
  18.4 68.8 all-gather.3
  100.4 59.3 reduce-scatter.1

commit v10 on v9

--- a/solution.py
+++ b/solution.py
@@ -83,10 +83,12 @@
     with jax.named_scope("forward"):
         rows_cot = jnp.dot(select, cotangent, preferred_element_type=f32)
         part_act = lax.dot_general(normed, weight, (((0,), (0,)), ((), ())), preferred_element_type=f32)
-        part_act = lax.all_to_all(
-            part_act.reshape(CORE, KMOST, ff_width), "core", split_axis=0, concat_axis=0, tiled=True
-        )
-        act_value, act_slope = gelu_pair(part_act[0] + part_act[1])
+        low = core == 0
+        sent_act = jnp.where(low, part_act[KMOST:], part_act[:KMOST]).astype(bf16)
+        met_act = lax.all_gather(sent_act, "core", axis=0)
+        own_act = jnp.where(low, part_act[:KMOST], part_act[KMOST:])
+        met_act = jnp.where(low, met_act[1], met_act[0]).astype(f32)
+        act_value, act_slope = gelu_pair(own_act + met_act)
         pre_grad = (rows_cot * act_slope).astype(bf16)
         hidden_rows, pre_grad = lax.optimization_barrier((act_value.astype(bf16), pre_grad))
         pair_grad = lax.all_gather(pre_grad, "core", axis=0, tiled=True)

time: 181 us -> 179 us (0.989)
  blocking collectives: 106 us -> 104 us
    all_to_all x1 -> x0, blocking collectives: 4.68 us -> none  [per_device(): lax.all_to_all(part_act.reshape(CORE, KMOST, ff_width), 'core', split_axi...]
    all_gather x0 -> x1, blocking collectives: none -> 2.23 us  [per_device(): met_act = lax.all_gather(sent_act, 'core', axis=0)]
where the time goes in v10:
time: 179 us; the launch traced here: 178 us
  blocking collectives  104 us (58%)
  waiting for transfers between devices  25.1 us (14%)
  between operations  14.9 us (8%)
  starting transfers between devices  12.7 us (7%)
  matrix products  11.5 us (6%)
  local copies, waits for them, and re-layouts  5.52 us (3%)
  other arithmetic  4.06 us (2%)
    all_gather x2, blocking collectives, per_device(): lax.all_gather(pair_x[i * cut:(i + 1) * cut], 'yl', axis=0, tiled=True)  35.8 us
    all_to_all x1, blocking collectives, rows_grad(): lax.all_to_all(jnp.concatenate([by_yl, extra], axis=1), 'yl', split_axis=...  33.4 us
    all_gather x1, blocking collectives, per_device(): block_x = lax.all_gather(own_x, 'x', axis=0, tiled=True)  13 us
    all_gather x1, blocking collectives, per_device(): pair_weight = lax.all_gather(w_in, 'yh', axis=0, tiled=True)  11.1 us
    all_to_all x1, waiting for transfers between devices, rows_grad(): lax.all_to_all(jnp.concatenate([by_x, extra], axis=1), 'x', split_axis=0,...  8.08 us
    all_gather x1, waiting for transfers between devices, per_device(): weight = lax.all_gather(pair_weight, 'z', axis=0, tiled=True)  7.33 us
    ppermute x1, waiting for transfers between devices, per_device(): met_w = lax.ppermute(sent_w, 'yh', [(0, 1), (1, 0)])  5.51 us
    ppermute x1, starting transfers between devices, per_device(): met_w = lax.ppermute(sent_w, 'yh', [(0, 1), (1, 0)])  4.93 us
  transfers between devices with their start and end apart: 5, of which 5 were waited for; matrix products, arithmetic and copies ran while one was open for 7% of the time, Pallas kernels for 0%

profile of v10, /device:TPU:56, one launch (start us, length us, event | category | flops | bytes accessed | tf_op | source)
XLA Modules:
  0.0 177.6 jit_solution(11882589495367526798)
XLA Ops:
  7.2 11.1 %all_gather.30 = bf16[128,768]{1,0:T(8,128)(2,1)} all-gather(bf16[64,768]{1,0:T(8,128)(2,1)} %param.12), channel_id=1, replica_groups=mesh['yh'=2,'z'=12,'core'=2,'yl'=4,'x'=4] {'yh'}, dimensions={0}, use_global_device_ids=true | all-gather | bytes 294912 | tf_op jit(solution)/shard_map/weight_gather/all_gather | solution.py:46
  19.0 0.7 compare_select_fusion
  19.6 1.1 fusion.29
  20.9 13.0 %all_gather.32 = bf16[768,192]{1,0:T(8,128)(2,1)S(1)} all-gather(bf16[192,192]{1,0:T(8,128)(2,1)S(1)} %copy.82), channel_id=1, replica_groups=mesh['yh'=2,'z'=12,'core'=2,'yl'=4,'x'=4] {'x'}, dimensions={0}, use_global_device_ids=true | all-gather | bytes 368640 | tf_op jit(solution)/shard_map/rows_gather/all_gather | solution.py:55
  33.9 0.9 copy.84
  34.8 3.4 %all-to-all-start.3 = ((bf16[2,384,192]{1,2,0:T(8,128)(2,1)}), bf16[2,384,192]{1,2,0:T(8,128)(2,1)S(1)}, u32[]{:S(2)}, u32[]{:S(2)}) async-start(bf16[2,384,192]{1,2,0:T(8,128)(2,1)} %copy.84), calls=%async_computation.3 | async-start | bytes 589824 | tf_op jit(solution)/shard_map/rows_gather/all_to_all | solution.py:58
  38.3 1.5 all-to-all-done.3
  39.9 0.1 copy.93
  40.0 0.1 copy.94
  40.1 0.1 fusion.35
  40.3 19.1 %all_gather.34 = bf16[768,384]{1,0:T(8,128)(2,1)S(1)} all-gather(bf16[192,384]{1,0:T(8,128)(2,1)S(1)} %get-tuple-element.63), channel_id=1, replica_groups=mesh['yh'=2,'z'=12,'core'=2,'yl'=4,'x'=4] {'yl'}, dimensions={0}, use_global_device_ids=true | all-gather | bytes 737280 | tf_op jit(solution)/shard_map/rows_gather/all_gather | solution.py:64
  59.3 16.7 %all_gather.33 = bf16[768,384]{1,0:T(8,128)(2,1)S(1)} all-gather(bf16[192,384]{1,0:T(8,128)(2,1)S(1)} %get-tuple-element.62), channel_id=1, replica_groups=mesh['yh'=2,'z'=12,'core'=2,'yl'=4,'x'=4] {'yl'}, dimensions={0}, use_global_device_ids=true | all-gather | bytes 737280 | tf_op jit(solution)/shard_map/rows_gather/all_gather | solution.py:64
  76.1 0.1 maximum_bitcast_fusion
  76.2 0.1 copy.87
  76.4 0.6 copy-done.2
  77.1 0.2 convert_reduce_fusion.4
  77.4 0.4 fusion.24
  77.8 1.8 %all-gather.2 = f32[2,2,384]{2,1,0:T(2,128)S(1)} all-gather(f32[1,2,384]{2,1,0:T(2,128)S(1)} %maximum_bitcast_fusion.1), channel_id=2, replica_groups=mesh['yh'=2,'z'=12,'core'=2,'yl'=4,'x'=4] {'core'}, dimensions={0}, use_global_device_ids=true | all-gather | bytes 9216 | tf_op jit(solution)/shard_map/row_moments/all_gather | solution.py:72
  79.6 0.4 fusion.27
  80.0 7.3 %all-gather.5.cloned.1.call-done = bf16[1536,768]{1,0:T(8,128)(2,1)} async-done(((bf16[128,768]{1,0:T(8,128)(2,1)}), bf16[1536,768]{1,0:T(8,128)(2,1)}) %all-gather.5.cloned.1.call-update) | async-done | bytes 2359312 | tf_op jit(solution)/shard_map/weight_gather/all_gather | solution.py:47
  87.3 2.8 %fusion.49 = f32[384,768]{1,0:T(8,128)S(1)} fusion(bf16[1536,384]{1,0:T(8,128)(2,1)S(1)} %fusion.27, bf16[1536,768]{1,0:T(8,128)(2,1)} %all-gather.5.cloned.1.call-done), kind=kOutput, calls=%fused_computation.119 | convolution fusion | flops 905969664 | bytes 4718592 | tf_op jit(solution)/shard_map/forward/dot_general | solution.py:85
  90.2 2.2 %all-gather.1 = bf16[384,768]{1,0:T(8,128)(2,1)S(1)} all-gather(bf16[192,768]{1,0:T(8,128)(2,1)S(1)} %select_convert_fusion), channel_id=3, replica_groups=mesh['yh'=2,'z'=12,'core'=2,'yl'=4,'x'=4] {'core'}, dimensions={0}, use_global_device_ids=true | all-gather | bytes 884736 | tf_op jit(solution)/shard_map/forward/all_gather | solution.py:88
  92.4 0.2 multiply_convert_fusion
  92.6 0.4 fusion.28
  93.0 2.2 %all_gather.39 = bf16[384,768]{1,0:T(8,128)(2,1)S(1)} all-gather(bf16[192,768]{1,0:T(8,128)(2,1)S(1)} %fusion.28), channel_id=1, replica_groups=mesh['yh'=2,'z'=12,'core'=2,'yl'=4,'x'=4] {'core'}, dimensions={0}, use_global_device_ids=true | all-gather | bytes 884736 | tf_op jit(solution)/shard_map/forward/all_gather | solution.py:94
  95.2 2.8 %convolution_convert_fusion.2 = bf16[1536,768]{1,0:T(8,128)(2,1)} fusion(bf16[1536,384]{1,0:T(8,128)(2,1)S(1)} %fusion.27, bf16[384,768]{1,0:T(8,128)(2,1)S(1)} %all_gather.39), kind=kOutput, calls=%fused_computation.61 | convolution fusion | flops 907149312 | bytes 4128768 | tf_op jit(solution)/shard_map/weight_grad/dot_general | solution.py:97
  98.3 56.4 %conditional.1 = (f32[2,192]{0,1:T(8,128)S(1)}, f32[192,192]{0,1:T(8,128)S(1)}, bf16[256,768]{1,0:T(8,128)(2,1)S(1)}) conditional(s32[]{:T(128)} %convert_element_type.85, () %tuple.18, (bf16[1536,768]{1,0:T(8,128)(2,1)}, bf16[384,768]{1,0:T(8,128)(2,1)S(1)}, f32[12,2,64]{2,1,0:T(2,128)S(1)}, bf16[1536,384]{1,0:T(8,128)(2,1)S(1)}, ...), branch_computations={%region_2.3_spmd, %region_3.11_spmd} | conditional | flops 990556416 | bytes 22172216 | solution.py:140
  98.4 3.2 %fusion = (f32[384]{0:T(512)S(1)}, f32[384]{0:T(512)S(1)}, bf16[1536,384]{1,0:T(8,128)(2,1)S(1)}) fusion(f32[1536]{0:T(1024)S(1)} %mul.107, bf16[1536,384]{1,0:T(8,128)(2,1)S(1)} %get-tuple-element.15, bf16[1536,768]{1,0:T(8,128)(2,1)} %get-tuple-element.12, bf16[384,768]{1,0:T(8,128)(2,1)S(1)} %get-tuple-element.13), kind=kOutput, calls=%fused_computation.3 | convolution fusion | flops 910097664 | bytes 5317632 | tf_op jit(solution)/shard_map/rows_grad/cond/branch_1_fun/dot_general | solution.py:104
  101.6 0.1 copy.74
  101.8 0.1 pad_maximum_fusion
  101.9 33.4 %all_to_all.17 = bf16[4,400,384]{2,1,0:T(8,128)(2,1)S(1)} all-to-all(bf16[4,400,384]{2,1,0:T(8,128)(2,1)S(1)} %pad_maximum_fusion), channel_id=1, replica_groups=mesh['yh'=2,'z'=12,'core'=2,'yl'=4,'x'=4] {'yl'}, dimensions={0} | all-to-all | bytes 2457600 | tf_op jit(solution)/shard_map/rows_grad/cond/branch_1_fun/all_to_all | solution.py:111
  135.4 0.2 slice_reduce_fusion
  135.6 0.1 fusion.3
  135.8 0.2 copy.75
  136.0 4.0 %all_to_all.18 = bf16[2,400,192]{1,2,0:T(8,128)(2,1)S(1)} all-to-all(bf16[2,400,192]{1,2,0:T(8,128)(2,1)S(1)} %copy.75), channel_id=1, replica_groups=mesh['yh'=2,'z'=12,'core'=2,'yl'=4,'x'=4] {'core'}, dimensions={0} | all-to-all | bytes 614400 | tf_op jit(solution)/shard_map/rows_grad/cond/branch_1_fun/all_to_all | solution.py:118
  140.5 0.2 copy.89
  140.8 1.0 copy.81
  141.8 4.3 %all-to-all-start.2 = ((bf16[4,208,192]{1,2,0:T(8,128)(2,1)}), bf16[4,208,192]{1,2,0:T(8,128)(2,1)S(1)}, u32[]{:S(2)}, u32[]{:S(2)}) async-start(bf16[4,208,192]{1,2,0:T(8,128)(2,1)} %copy.81), calls=%async_computation.2 | async-start | bytes 786432 | tf_op jit(solution)/shard_map/rows_grad/cond/branch_1_fun/all_to_all | solution.py:123
  146.0 0.3 convolution_convert_fusion.1
  146.3 8.1 %all-to-all-done.2 = bf16[4,208,192]{1,2,0:T(8,128)(2,1)S(1)} async-done(((bf16[4,208,192]{1,2,0:T(8,128)(2,1)}), bf16[4,208,192]{1,2,0:T(8,128)(2,1)S(1)}, u32[]{:S(2)}, u32[]{:S(2)}) %all-to-all-start.2) | async-done | bytes 319520 | tf_op jit(solution)/shard_map/rows_grad/cond/branch_1_fun/all_to_all | solution.py:123
  154.4 0.1 convert_reduce_fusion.1
  154.8 0.2 slice_reduce_fusion.2
  155.0 2.6 %reduce-scatter.2.cloned.1.call-done = bf16[128,768]{1,0:T(8,128)(2,1)} async-done(((bf16[1536,768]{1,0:T(8,128)(2,1)}), bf16[128,768]{1,0:T(8,128)(2,1)}) %reduce-scatter.2.cloned.1.call-update) | async-done | bytes 196624 | tf_op jit(solution)/shard_map/weight_grad/reduce_scatter | solution.py:98
  157.6 1.0 constant_dynamic-slice_fusion.1
  158.5 4.9 %collective-permute-start = (bf16[64,768]{1,0:T(8,128)(2,1)S(1)}, bf16[64,768]{1,0:T(8,128)(2,1)S(1)}, u32[]{:S(2)}, u32[]{:S(2)}) collective-permute-start(bf16[64,768]{1,0:T(8,128)(2,1)S(1)} %get-tuple-element.34), channel_id=1, source_target_pairs={{0,384},{384,0},{1,385},{385,1},{2,386},{386,2},{3,387},{387,3},{4... | collective-permute-start | bytes 294920 | tf_op jit(solution)/shard_map/weight_out/ppermute | solution.py:166
  163.5 1.0 convolution_convert_fusion.3
  164.5 5.5 %collective-permute-done = bf16[64,768]{1,0:T(8,128)(2,1)S(1)} collective-permute-done((bf16[64,768]{1,0:T(8,128)(2,1)S(1)}, bf16[64,768]{1,0:T(8,128)(2,1)S(1)}, u32[]{:S(2)}, u32[]{:S(2)}) %collective-permute-start) | collective-permute-done | bytes 98336 | tf_op jit(solution)/shard_map/weight_out/ppermute | solution.py:166
  170.0 0.7 convert_add_fusion.1
  (51 shorter events, 1.8 us)
Async XLA Ops:
  7.2 85.5 %copy-start = (bf16[256,768]{1,0:T(8,128)(2,1)S(1)}, bf16[256,768]{1,0:T(8,128)(2,1)}, u32[]{:S(2)}) copy-start(bf16[256,768]{1,0:T(8,128)(2,1)} %param.13) | copy-start | bytes 1179652
  7.2 80.2 %all-gather.5.cloned.1.call-start = ((), (), s32[]{:S(2)}) async-start(), calls=%async_computation.5 | async-start | bytes 2555904 | tf_op jit(solution)/shard_map/weight_gather/all_gather | solution.py:47
  34.8 5.0 %all-to-all-start.3 = ((bf16[2,384,192]{1,2,0:T(8,128)(2,1)}), bf16[2,384,192]{1,2,0:T(8,128)(2,1)S(1)}, u32[]{:S(2)}, u32[]{:S(2)}) async-start(bf16[2,384,192]{1,2,0:T(8,128)(2,1)} %copy.84), calls=%async_computation.3 | async-start | bytes 589824 | tf_op jit(solution)/shard_map/rows_gather/all_to_all | solution.py:58
  38.3 119.3 %reduce-scatter.2.cloned.1.call-start = ((), (), s32[]{:S(2)}) async-start(), calls=%async_computation.6 | async-start | bytes 2555904 | tf_op jit(solution)/shard_map/weight_grad/reduce_scatter | solution.py:98
  76.2 0.7 copy-start.2
  141.8 12.6 %all-to-all-start.2 = ((bf16[4,208,192]{1,2,0:T(8,128)(2,1)}), bf16[4,208,192]{1,2,0:T(8,128)(2,1)S(1)}, u32[]{:S(2)}, u32[]{:S(2)}) async-start(bf16[4,208,192]{1,2,0:T(8,128)(2,1)} %copy.81), calls=%async_computation.2 | async-start | bytes 786432 | tf_op jit(solution)/shard_map/rows_grad/cond/branch_1_fun/all_to_all | solution.py:123
  154.7 16.0 %copy-start.1 = (bf16[256,768]{1,0:T(8,128)(2,1)}, bf16[256,768]{1,0:T(8,128)(2,1)S(1)}, u32[]{:S(2)}) copy-start(bf16[256,768]{1,0:T(8,128)(2,1)S(1)} %get-tuple-element.25) | copy-start | bytes 1179652
  158.5 11.5 %collective-permute-start = (bf16[64,768]{1,0:T(8,128)(2,1)S(1)}, bf16[64,768]{1,0:T(8,128)(2,1)S(1)}, u32[]{:S(2)}, u32[]{:S(2)}) collective-permute-start(bf16[64,768]{1,0:T(8,128)(2,1)S(1)} %get-tuple-element.34), channel_id=1, source_target_pairs={{0,384},{384,0},{1,385},{385,1},{2,386},{386,2},{3,387},{387,3},{4... | collective-permute-start | bytes 294920 | tf_op jit(solution)/shard_map/weight_out/ppermute | solution.py:166
Sparse Core Ops, SparseCore 0:
  18.4 68.8 all-gather.4
  98.2 59.3 reduce-scatter.1
